TPU v7x, 128 devices: a whole 4x4x4 slice. The times are simulated.
128 devices in a mesh: section: 2 (over core), rep: 4 (over y), fsdp: 16 (over z, x).
Axes of the slice: x: 4, y: 4, z: 4, core: 2. Of those that a mesh axis runs over, the one named last changes fastest.
Arguments:
- inputs: bfloat16 [2, 64, 128, 1024], P(None, ('rep', 'fsdp')), may hold values from -6 to 6
- out_grad: bfloat16 [2, 64, 128, 1024], P(None, ('rep', 'fsdp')), may hold values from -6 to 6
- mixer_norm_gain: bfloat16 [2, 1024], P('section', 'fsdp'), may hold values from 0.5 to 1.5
- w_query: bfloat16 [2, 1024, 1024], P('section', 'fsdp'), may hold values from -0.1875 to 0.1875
- w_key: bfloat16 [2, 1024, 1024], P('section', 'fsdp'), may hold values from -0.1875 to 0.1875
- w_value: bfloat16 [2, 1024, 2048], P('section', 'fsdp'), may hold values from -0.1875 to 0.1875
- w_gate: bfloat16 [2, 1024, 2048], P('section', 'fsdp'), may hold values from -0.1875 to 0.1875
- w_alpha: bfloat16 [2, 1024, 8], P('section', 'fsdp'), may hold values from -0.1875 to 0.1875
- w_beta: bfloat16 [2, 1024, 8], P('section', 'fsdp'), may hold values from -0.1875 to 0.1875
- log_rate: float32 [2, 8], P('section'), may hold values from -1.5 to 2.5
- dt_bias: float32 [2, 8], P('section'), may hold values from -6 to -2
- conv_query: bfloat16 [2, 4, 1024], P('section', None, 'fsdp'), may hold values from -3 to 3
- conv_key: bfloat16 [2, 4, 1024], P('section', None, 'fsdp'), may hold values from -3 to 3
- conv_value: bfloat16 [2, 4, 2048], P('section', None, 'fsdp'), may hold values from -3 to 3
- out_gain: bfloat16 [2, 256], P('section', 'fsdp'), may hold values from 0.5 to 1.5
- w_out: bfloat16 [2, 2048, 1024], P('section', 'fsdp'), may hold values from -0.25 to 0.25
- gain_ffn: bfloat16 [2, 1024], P('section', 'fsdp'), may hold values from 0.5 to 1.5
- w_ffgate: bfloat16 [2, 1024, 2816], P('section', 'fsdp'), may hold values from -0.1875 to 0.1875
- w_ffup: bfloat16 [2, 1024, 2816], P('section', 'fsdp'), may hold values from -0.1875 to 0.1875
- w_ffdown: bfloat16 [2, 2816, 1024], P('section', 'fsdp'), may hold values from -0.109375 to 0.109375
Outputs:
- edges: float32 [2, 2, 64, 128, 1024], P('section', None, ('rep', 'fsdp'))
- grad_gain_mix: float32 [2, 1024], P('section', 'fsdp')
- grad_w_query: float32 [2, 1024, 1024], P('section', 'fsdp')
- grad_w_key: float32 [2, 1024, 1024], P('section', 'fsdp')
- grad_w_value: float32 [2, 1024, 2048], P('section', 'fsdp')
- grad_w_gate: float32 [2, 1024, 2048], P('section', 'fsdp')
- grad_w_alpha: float32 [2, 1024, 8], P('section', 'fsdp')
- grad_w_beta: float32 [2, 1024, 8], P('section', 'fsdp')
- grad_log_rate: float32 [2, 8], P('section')
- grad_dt_bias: float32 [2, 8], P('section')
- grad_conv_query: float32 [2, 4, 1024], P('section', None, 'fsdp')
- grad_conv_key: float32 [2, 4, 1024], P('section', None, 'fsdp')
- grad_conv_value: float32 [2, 4, 2048], P('section', None, 'fsdp')
- grad_out_gain: float32 [2, 256], P('section', 'fsdp')
- grad_w_out: float32 [2, 2048, 1024], P('section', 'fsdp')
- grad_gain_ffn: float32 [2, 1024], P('section', 'fsdp')
- grad_w_ffgate: float32 [2, 1024, 2816], P('section', 'fsdp')
- grad_w_ffup: float32 [2, 1024, 2816], P('section', 'fsdp')
- grad_w_ffdown: float32 [2, 2816, 1024], P('section', 'fsdp')
All inputs are finite; a program needn't handle non-finite values.
Results may differ from a plain program's by a relative error of at most 0.033.
Values may be sent and summed in bfloat16 or wider, within the bound.
No kernel may reach another device: no remote copies, remote signals or barrier semaphores. Data moves between devices by JAX's collectives and lax.ppermute only.
A program may use at most 320 MiB of HBM per device.

v0:
```python
import math

import jax
import jax.numpy as jnp
from jax import lax
from jax.sharding import PartitionSpec as P


def sent_together(arrays, axis, dim, along):
    columns = [a.reshape(*a.shape[:along], -1) for a in arrays]
    both = jnp.concatenate(columns, axis=along)
    filled, at, gathered = (lax.all_gather(both, axis, axis=dim, tiled=True), 0, [])
    for a, column in zip(arrays, columns):
        share = filled[..., at : at + column.shape[along]]
        gathered.append(share.reshape(*share.shape[:along], *a.shape[along:]))
        at += column.shape[along]
    return tuple(gathered)


def in_one_piece(arrays, axis, dim, along):
    ends, at = ([], 0)
    for a in arrays[:-1]:
        at += a.shape[along]
        ends.append(at)
    both = jnp.concatenate(arrays, axis=along)
    return tuple(jnp.split(lax.all_gather(both, axis, axis=dim, tiled=True), ends, axis=along))


def sent_together_2(arrays, axis, dim, along):
    widths = [math.prod(a.shape[along:]) for a in arrays]
    both = jnp.concatenate(
        [a.reshape(*a.shape[:along], w) for a, w in zip(arrays, widths)], axis=along
    )
    filled = lax.psum_scatter(both, axis, scatter_dimension=dim, tiled=True)
    blocks = jnp.split(filled, [sum(widths[:k]) for k in range(1, len(widths))], axis=along)
    return tuple(
        (b.reshape(*filled.shape[:along], *a.shape[along:]) for a, b in zip(arrays, blocks))
    )


def sent_together_3(arrays, axis, dim, along):
    widths = [a.shape[along] for a in arrays]
    both = jnp.concatenate(arrays, axis=along)
    filled = lax.psum_scatter(both, axis, scatter_dimension=dim, tiled=True)
    return tuple(jnp.split(filled, [sum(widths[:k]) for k in range(1, len(widths))], axis=along))


def shifted(value, axis, by):
    devices = lax.axis_size(axis)
    pairs = [(i, i + by) for i in range(devices) if 0 <= i + by < devices]
    return lax.ppermute(value, axis, pairs)


def copy_for_each(value, axis):
    copies = jnp.broadcast_to(value, (lax.axis_size(axis), *value.shape))
    return lax.all_to_all(copies, axis, split_axis=0, concat_axis=0, tiled=True)


def taken_together(value, axis):
    everything = copy_for_each(value, axis)
    return jnp.sum(everything, axis=0)


def packed_total(arrays, axis):
    flat, at, gathered = (jnp.concatenate([a.reshape(-1) for a in arrays]), 0, [])
    total = taken_together(flat, axis)
    for a in arrays:
        gathered.append(total[at : at + a.size].reshape(a.shape))
        at += a.size
    return tuple(gathered)


def root_norm(tensor, epsilon):
    return tensor * lax.rsqrt(jnp.mean(tensor * tensor, axis=-1, keepdims=True) + epsilon)


def unit_rows(tensor):
    return tensor * lax.rsqrt(jnp.sum(tensor * tensor, axis=-1, keepdims=True) + 1e-06)


def causal_conv(values, kernel):
    taps = kernel.shape[0]
    length = values.shape[0]
    padded = jnp.pad(values, ((taps - 1, 0), (0, 0)))
    summed = jnp.zeros_like(values)
    for offset in range(taps):
        summed = summed + kernel[offset] * padded[offset : offset + length]
    return jax.nn.silu(summed)


def delta_blocks(queries, keys_in, values_in, strength, decay):
    length, head_count, key_size = queries.shape
    value_size = values_in.shape[-1]
    block_len = math.gcd(128, length)
    pieces = length // block_len

    def by_block(tensor):
        shaped = tensor.reshape((pieces, block_len) + tensor.shape[1:])
        return jnp.moveaxis(shaped, 2, 1)

    strict = jnp.tril(jnp.ones((block_len, block_len), jnp.float32), -1)
    inclusive = strict + jnp.eye(block_len, dtype=jnp.float32)
    unit_matrix = jnp.eye(block_len, dtype=jnp.float32)

    def advance(memory_state, item):
        query_block, key_block, value_block, strength_block, decay_block = item
        running = jnp.cumsum(decay_block, axis=-1)
        spread = running[:, :, None] - running[:, None, :]
        ratios = jnp.exp(jnp.where(inclusive > 0, spread, 0.0)) * inclusive
        scale_in = jnp.exp(running)
        intersection = jnp.einsum("htd,hsd->hts", key_block, key_block)
        system = unit_matrix + strength_block[:, :, None] * intersection * ratios * strict
        predicted_values = jnp.einsum("htd,hdv->htv", key_block, memory_state)
        target = strength_block[:, :, None] * (
            value_block - scale_in[:, :, None] * predicted_values
        )
        updates = lax.linalg.triangular_solve(
            system, target, left_side=True, lower=True, unit_diagonal=True
        )
        weighting = jnp.einsum("htd,hsd->hts", query_block, key_block) * ratios
        mixer_output = scale_in[:, :, None] * jnp.einsum("htd,hdv->htv", query_block, memory_state)
        mixer_output = mixer_output + jnp.einsum("hts,hsv->htv", weighting, updates)
        remain = jnp.exp(running[:, -1:] - running)
        memory_state = jnp.exp(running[:, -1])[:, None, None] * memory_state + jnp.einsum(
            "hsd,hsv->hdv", key_block * remain[:, :, None], updates
        )
        return (memory_state, mixer_output)

    initial = jnp.zeros((head_count, key_size, value_size), jnp.float32)
    _, outputs = lax.scan(
        advance,
        initial,
        (
            by_block(queries),
            by_block(keys_in),
            by_block(values_in),
            by_block(strength),
            by_block(decay),
        ),
    )
    return jnp.moveaxis(outputs, 1, 2).reshape(length, head_count, value_size)


def mixer_core(
    query_pre,
    key_pre,
    value_pre,
    gate_pre,
    alpha_pre,
    beta_pre,
    query_kernel,
    key_kernel,
    value_kernel,
    log_rate,
    dt_bias,
    out_gain,
):
    head_count = log_rate.shape[0]
    length = query_pre.shape[0]
    queries = causal_conv(query_pre, query_kernel).reshape(length, head_count, -1)
    keys_in = causal_conv(key_pre, key_kernel).reshape(length, head_count, -1)
    values_in = causal_conv(value_pre, value_kernel).reshape(length, head_count, -1)
    key_size = queries.shape[-1]
    queries = unit_rows(queries) * key_size ** (-0.5)
    keys_in = unit_rows(keys_in)
    strength = jax.nn.sigmoid(beta_pre)
    decay = -jnp.exp(log_rate) * jax.nn.softplus(alpha_pre + dt_bias)
    recur = delta_blocks(queries, keys_in, values_in, strength, decay)
    gates = jax.nn.silu(gate_pre.reshape(length, head_count, -1))
    normed = root_norm(recur, 0.002) * out_gain * gates
    return normed.reshape(length, -1)


def forward_layer(source, weights, rates):
    (
        mixer_norm_gain,
        w_query,
        w_key,
        w_value,
        w_gate,
        w_alpha,
        w_beta,
        conv_query,
        conv_key,
        conv_value,
        out_gain,
        w_out,
        gain_ffn,
        w_ffgate,
        w_ffup,
        w_ffdown,
    ) = weights
    normed = (root_norm(source, 1e-06) * mixer_norm_gain.astype(jnp.float32)).astype(jnp.bfloat16)
    query_pre = jnp.dot(normed, w_query, preferred_element_type=jnp.float32)
    key_pre = jnp.dot(normed, w_key, preferred_element_type=jnp.float32)
    value_pre = jnp.dot(normed, w_value, preferred_element_type=jnp.float32)
    gate_pre = jnp.dot(normed, w_gate, preferred_element_type=jnp.float32)
    alpha_pre = jnp.dot(normed, w_alpha, preferred_element_type=jnp.float32)
    beta_pre = jnp.dot(normed, w_beta, preferred_element_type=jnp.float32)
    mixed = mixer_core(
        query_pre,
        key_pre,
        value_pre,
        gate_pre,
        alpha_pre,
        beta_pre,
        conv_query.astype(jnp.float32),
        conv_key.astype(jnp.float32),
        conv_value.astype(jnp.float32),
        rates[0],
        rates[1],
        out_gain.astype(jnp.float32),
    ).astype(jnp.bfloat16)
    after_mix = source + jnp.dot(mixed, w_out, preferred_element_type=jnp.float32)
    normed_ffn = (root_norm(after_mix, 1e-06) * gain_ffn.astype(jnp.float32)).astype(jnp.bfloat16)
    gate_act = jnp.dot(normed_ffn, w_ffgate, preferred_element_type=jnp.float32)
    up_act = jnp.dot(normed_ffn, w_ffup, preferred_element_type=jnp.float32)
    hidden = (jax.nn.silu(gate_act) * up_act).astype(jnp.bfloat16)
    layer_out = after_mix + jnp.dot(hidden, w_ffdown, preferred_element_type=jnp.float32)
    saved = (
        source,
        normed,
        query_pre,
        key_pre,
        value_pre,
        gate_pre,
        alpha_pre,
        beta_pre,
        mixed,
        after_mix,
        normed_ffn,
        gate_act,
        up_act,
        hidden,
    )
    return (layer_out, saved)


def backward_layer(grad_top, saved, weights, rates):
    (
        source,
        normed,
        query_pre,
        key_pre,
        value_pre,
        gate_pre,
        alpha_pre,
        beta_pre,
        mixed,
        after_mix,
        normed_ffn,
        gate_act,
        up_act,
        hidden,
    ) = saved
    (
        mixer_norm_gain,
        w_query,
        w_key,
        w_value,
        w_gate,
        w_alpha,
        w_beta,
        conv_query,
        conv_key,
        conv_value,
        out_gain,
        w_out,
        gain_ffn,
        w_ffgate,
        w_ffup,
        w_ffdown,
    ) = weights
    down_grad = grad_top.astype(jnp.bfloat16)
    hidden_grad = jnp.einsum("ld,fd->lf", down_grad, w_ffdown, preferred_element_type=jnp.float32)
    _, swiglu_pull = jax.vjp(lambda gate_in, up_in: jax.nn.silu(gate_in) * up_in, gate_act, up_act)
    gate_grad, up_grad = swiglu_pull(hidden_grad)
    gate_grad = gate_grad.astype(jnp.bfloat16)
    up_grad = up_grad.astype(jnp.bfloat16)
    ffn_in_grad = jnp.einsum("lf,df->ld", gate_grad, w_ffgate, preferred_element_type=jnp.float32)
    ffn_in_grad = ffn_in_grad + jnp.einsum(
        "lf,df->ld", up_grad, w_ffup, preferred_element_type=jnp.float32
    )
    _, second_pull = jax.vjp(
        lambda tensor, weight: root_norm(tensor, 1e-06) * weight,
        after_mix,
        gain_ffn.astype(jnp.float32),
    )
    residual_grad, grad_gain_ffn = second_pull(ffn_in_grad)
    mix_grad = grad_top + residual_grad
    mix_low = mix_grad.astype(jnp.bfloat16)
    mixed_grad = jnp.einsum("ld,vd->lv", mix_low, w_out, preferred_element_type=jnp.float32)
    _, core_pull = jax.vjp(
        mixer_core,
        query_pre,
        key_pre,
        value_pre,
        gate_pre,
        alpha_pre,
        beta_pre,
        conv_query.astype(jnp.float32),
        conv_key.astype(jnp.float32),
        conv_value.astype(jnp.float32),
        rates[0],
        rates[1],
        out_gain.astype(jnp.float32),
    )
    core_grads = core_pull(mixed_grad)
    matrices = (w_query, w_key, w_value, w_gate, w_alpha, w_beta)
    preceding_lower = tuple((core_grads[number].astype(jnp.bfloat16) for number in range(6)))
    normed_grad = jnp.einsum(
        "ln,dn->ld", preceding_lower[0], matrices[0], preferred_element_type=jnp.float32
    )
    for number in range(1, 6):
        normed_grad = normed_grad + jnp.einsum(
            "ln,dn->ld",
            preceding_lower[number],
            matrices[number],
            preferred_element_type=jnp.float32,
        )
    _, first_pull = jax.vjp(
        lambda tensor, weight: root_norm(tensor, 1e-06) * weight,
        source,
        mixer_norm_gain.astype(jnp.float32),
    )
    source_grad, grad_gain_mix = first_pull(normed_grad)
    input_grad = mix_grad + source_grad
    smalls = (
        grad_gain_mix,
        grad_gain_ffn,
        core_grads[6],
        core_grads[7],
        core_grads[8],
        core_grads[11],
        core_grads[9],
        core_grads[10],
    )
    factors = (down_grad, gate_grad, up_grad, mix_low) + preceding_lower
    return (input_grad, smalls, factors)


def large_grads(normed, mixed, normed_ffn, hidden, factors):
    down_grad, gate_grad, up_grad, mix_low = (factors[0], factors[1], factors[2], factors[3])
    grad_ffdown = jnp.einsum("lf,ld->fd", hidden, down_grad, preferred_element_type=jnp.float32)
    grad_ffgate = jnp.einsum("ld,lf->df", normed_ffn, gate_grad, preferred_element_type=jnp.float32)
    grad_ffup = jnp.einsum("ld,lf->df", normed_ffn, up_grad, preferred_element_type=jnp.float32)
    grad_out_proj = jnp.einsum("lv,ld->vd", mixed, mix_low, preferred_element_type=jnp.float32)
    grad_proj = tuple(
        (
            jnp.einsum("ld,ln->dn", normed, grad_low, preferred_element_type=jnp.float32)
            for grad_low in factors[4:]
        )
    )
    return (grad_proj, grad_out_proj, grad_ffgate, grad_ffup, grad_ffdown)


def assemble(smalls, bigs):
    grad_proj, grad_out_proj, grad_ffgate, grad_ffup, grad_ffdown = bigs
    return (
        smalls[0],
        grad_proj[0],
        grad_proj[1],
        grad_proj[2],
        grad_proj[3],
        grad_proj[4],
        grad_proj[5],
        smalls[2],
        smalls[3],
        smalls[4],
        smalls[5],
        grad_out_proj,
        smalls[1],
        grad_ffgate,
        grad_ffup,
        grad_ffdown,
    )


def accumulate(left, right):
    return tuple((first + second for first, second in zip(left, right)))


def flatten_rows(tensor):
    return tensor.reshape((tensor.shape[0] * tensor.shape[1],) + tensor.shape[2:])


def per_device(
    inputs,
    out_grad,
    mixer_norm_gain,
    w_query,
    w_key,
    w_value,
    w_gate,
    w_alpha,
    w_beta,
    log_rate,
    dt_bias,
    conv_query,
    conv_key,
    conv_value,
    out_gain,
    w_out,
    gain_ffn,
    w_ffgate,
    w_ffup,
    w_ffdown,
):
    micro_count = inputs.shape[0]
    length = inputs.shape[2]
    model_width = inputs.shape[3]
    section_index = lax.axis_index("section")
    rates = (log_rate[0], dt_bias[0])

    def fetch():
        whole = (
            *sent_together(
                (mixer_norm_gain, w_query, w_key, w_value, w_gate, w_alpha, w_beta), "fsdp", 1, 2
            ),
            *in_one_piece((conv_query, conv_key), "fsdp", 2, 0),
            lax.all_gather(conv_value, "fsdp", axis=2, tiled=True),
            lax.all_gather(out_gain, "fsdp", axis=1, tiled=True),
            lax.all_gather(w_out, "fsdp", axis=1, tiled=True),
            *sent_together((gain_ffn, w_ffgate, w_ffup), "fsdp", 1, 2),
            lax.all_gather(w_ffdown, "fsdp", axis=1, tiled=True),
        )
        return tuple((gathered[0] for gathered in whole))

    forward_weights = fetch()
    key_cols = forward_weights[1].shape[1]
    value_cols = forward_weights[3].shape[1]
    head_count = log_rate.shape[1]
    ffn_cols = forward_weights[13].shape[1]

    def empty(columns, dtype):
        return jnp.zeros((micro_count, length, columns), dtype)

    kept_acts = (
        empty(model_width, jnp.float32),
        empty(model_width, jnp.bfloat16),
        empty(key_cols, jnp.float32),
        empty(key_cols, jnp.float32),
        empty(value_cols, jnp.float32),
        empty(value_cols, jnp.float32),
        empty(head_count, jnp.float32),
        empty(head_count, jnp.float32),
        empty(value_cols, jnp.bfloat16),
        empty(model_width, jnp.float32),
        empty(model_width, jnp.bfloat16),
        empty(ffn_cols, jnp.float32),
        empty(ffn_cols, jnp.float32),
        empty(ffn_cols, jnp.bfloat16),
    )
    first_inputs = inputs[:, 0]
    boundary = jnp.zeros((micro_count, length, model_width), jnp.float32)
    received = jnp.zeros((length, model_width), jnp.bfloat16)
    for moment in range(micro_count + 1):
        micro_index = moment - section_index
        active = (micro_index >= 0) & (micro_index < micro_count)
        micro_slot = jnp.clip(micro_index, 0, micro_count - 1)
        own_input = first_inputs[min(moment, micro_count - 1)]
        source = jnp.where(section_index == 0, own_input, received).astype(jnp.float32)

        def run_forward(operands):
            source_in, buffers = operands
            layer_out, saved = forward_layer(source_in, forward_weights, rates)
            buffers = tuple(
                (
                    lax.dynamic_update_index_in_dim(buffer, value, micro_slot, 0)
                    for buffer, value in zip(buffers, saved)
                )
            )
            return (layer_out, buffers)

        def skip_forward(operands):
            return (jnp.zeros_like(operands[0]), operands[1])

        layer_out, kept_acts = lax.cond(active, run_forward, skip_forward, (source, kept_acts))
        previous = lax.dynamic_index_in_dim(boundary, micro_slot, 0, keepdims=False)
        boundary = lax.dynamic_update_index_in_dim(
            boundary, jnp.where(active & (section_index == 1), layer_out, previous), micro_slot, 0
        )
        if moment < micro_count:
            received = shifted(layer_out.astype(jnp.bfloat16), "section", 1)
    backward_weights = fetch()
    small_zero = (
        jnp.zeros(backward_weights[0].shape, jnp.float32),
        jnp.zeros(backward_weights[12].shape, jnp.float32),
        jnp.zeros(backward_weights[7].shape, jnp.float32),
        jnp.zeros(backward_weights[8].shape, jnp.float32),
        jnp.zeros(backward_weights[9].shape, jnp.float32),
        jnp.zeros(backward_weights[10].shape, jnp.float32),
        jnp.zeros((head_count,), jnp.float32),
        jnp.zeros((head_count,), jnp.float32),
    )
    small_totals = small_zero
    factor_store = (
        empty(model_width, jnp.bfloat16),
        empty(ffn_cols, jnp.bfloat16),
        empty(ffn_cols, jnp.bfloat16),
        empty(model_width, jnp.bfloat16),
        empty(key_cols, jnp.bfloat16),
        empty(key_cols, jnp.bfloat16),
        empty(value_cols, jnp.bfloat16),
        empty(value_cols, jnp.bfloat16),
        empty(head_count, jnp.bfloat16),
        empty(head_count, jnp.bfloat16),
    )
    shard_totals = None
    received_grad = jnp.zeros((length, model_width), jnp.bfloat16)
    own_grads = out_grad[:, 0]
    for moment in range(micro_count + 1):
        micro_index = micro_count - moment - section_index
        active = (micro_index >= 0) & (micro_index < micro_count)
        micro_slot = jnp.clip(micro_index, 0, micro_count - 1)
        own_grad = lax.dynamic_index_in_dim(own_grads, micro_slot, 0, keepdims=False)
        incoming = jnp.where(section_index == 1, own_grad, received_grad).astype(jnp.float32)
        picked = tuple(
            (
                lax.dynamic_index_in_dim(buffer, micro_slot, 0, keepdims=False)
                for buffer in kept_acts
            )
        )

        def run_backward(operands):
            grad_top, stores = operands
            input_grad, smalls, factors = backward_layer(grad_top, picked, backward_weights, rates)
            stores = tuple(
                (
                    lax.dynamic_update_index_in_dim(store, value, micro_slot, 0)
                    for store, value in zip(stores, factors)
                )
            )
            return (input_grad, smalls, stores, factors)

        def skip_backward(operands):
            grad_top, stores = operands
            return (
                jnp.zeros_like(grad_top),
                small_zero,
                stores,
                tuple((jnp.zeros(store.shape[1:], store.dtype) for store in stores)),
            )

        input_grad, smalls, factor_store, factors = lax.cond(
            active, run_backward, skip_backward, (incoming, factor_store)
        )
        small_totals = accumulate(small_totals, smalls)
        previous = lax.dynamic_index_in_dim(boundary, micro_slot, 0, keepdims=False)
        boundary = lax.dynamic_update_index_in_dim(
            boundary, jnp.where(active & (section_index == 0), input_grad, previous), micro_slot, 0
        )
        if moment < micro_count:
            received_grad = shifted(input_grad.astype(jnp.bfloat16), "section", -1)
    bigs = large_grads(
        flatten_rows(kept_acts[1]),
        flatten_rows(kept_acts[8]),
        flatten_rows(kept_acts[10]),
        flatten_rows(kept_acts[13]),
        tuple((flatten_rows(store) for store in factor_store)),
    )
    full = assemble(small_totals, bigs)
    shard_totals = (
        *tuple(
            (
                part.astype(jnp.float32)
                for part in sent_together_2(
                    (
                        full[0].astype(jnp.bfloat16),
                        full[1].astype(jnp.bfloat16),
                        full[2].astype(jnp.bfloat16),
                        full[3].astype(jnp.bfloat16),
                        full[4].astype(jnp.bfloat16),
                        full[5].astype(jnp.bfloat16),
                        full[6].astype(jnp.bfloat16),
                    ),
                    "fsdp",
                    0,
                    1,
                )
            )
        ),
        *tuple(
            (
                part.astype(jnp.float32)
                for part in sent_together_3(
                    (full[7].astype(jnp.bfloat16), full[8].astype(jnp.bfloat16)), "fsdp", 1, 0
                )
            )
        ),
        lax.psum_scatter(
            full[9].astype(jnp.bfloat16), "fsdp", scatter_dimension=1, tiled=True
        ).astype(jnp.float32),
        lax.psum_scatter(
            full[10].astype(jnp.bfloat16), "fsdp", scatter_dimension=0, tiled=True
        ).astype(jnp.float32),
        lax.psum_scatter(
            full[11].astype(jnp.bfloat16), "fsdp", scatter_dimension=0, tiled=True
        ).astype(jnp.float32),
        *tuple(
            (
                part.astype(jnp.float32)
                for part in sent_together_2(
                    (
                        full[12].astype(jnp.bfloat16),
                        full[13].astype(jnp.bfloat16),
                        full[14].astype(jnp.bfloat16),
                    ),
                    "fsdp",
                    0,
                    1,
                )
            )
        ),
        lax.psum_scatter(
            full[15].astype(jnp.bfloat16), "fsdp", scatter_dimension=0, tiled=True
        ).astype(jnp.float32),
    )
    summed = (
        lax.psum(shard_totals[0].astype(jnp.bfloat16), "rep").astype(jnp.float32),
        lax.psum(shard_totals[1].astype(jnp.bfloat16), "rep").astype(jnp.float32),
        lax.psum(shard_totals[2].astype(jnp.bfloat16), "rep").astype(jnp.float32),
        lax.psum(shard_totals[3].astype(jnp.bfloat16), "rep").astype(jnp.float32),
        lax.psum(shard_totals[4].astype(jnp.bfloat16), "rep").astype(jnp.float32),
        lax.psum(shard_totals[5].astype(jnp.bfloat16), "rep").astype(jnp.float32),
        lax.psum(shard_totals[6].astype(jnp.bfloat16), "rep").astype(jnp.float32),
        lax.psum(shard_totals[7].astype(jnp.bfloat16), "rep").astype(jnp.float32),
        lax.psum(shard_totals[8].astype(jnp.bfloat16), "rep").astype(jnp.float32),
        lax.psum(shard_totals[9].astype(jnp.bfloat16), "rep").astype(jnp.float32),
        lax.psum(shard_totals[10].astype(jnp.bfloat16), "rep").astype(jnp.float32),
        lax.psum(shard_totals[11].astype(jnp.bfloat16), "rep").astype(jnp.float32),
        lax.psum(shard_totals[12].astype(jnp.bfloat16), "rep").astype(jnp.float32),
        lax.psum(shard_totals[13].astype(jnp.bfloat16), "rep").astype(jnp.float32),
        lax.psum(shard_totals[14].astype(jnp.bfloat16), "rep").astype(jnp.float32),
        lax.psum(shard_totals[15].astype(jnp.bfloat16), "rep").astype(jnp.float32),
    )
    rate_sums = packed_total((small_totals[6], small_totals[7]), ("rep", "fsdp"))
    grads_out = tuple((grad[None] for grad in summed))
    return (
        boundary[None, :, None],
        grads_out[0],
        grads_out[1],
        grads_out[2],
        grads_out[3],
        grads_out[4],
        grads_out[5],
        grads_out[6],
        rate_sums[0][None],
        rate_sums[1][None],
        grads_out[7],
        grads_out[8],
        grads_out[9],
        grads_out[10],
        grads_out[11],
        grads_out[12],
        grads_out[13],
        grads_out[14],
        grads_out[15],
    )


def solution(mesh):
    placed = (
        P(None, ("rep", "fsdp"), None, None),
        P(None, ("rep", "fsdp"), None, None),
        P("section", "fsdp"),
        P("section", "fsdp", None),
        P("section", "fsdp", None),
        P("section", "fsdp", None),
        P("section", "fsdp", None),
        P("section", "fsdp", None),
        P("section", "fsdp", None),
        P("section", None),
        P("section", None),
        P("section", None, "fsdp"),
        P("section", None, "fsdp"),
        P("section", None, "fsdp"),
        P("section", "fsdp"),
        P("section", "fsdp", None),
        P("section", "fsdp"),
        P("section", "fsdp", None),
        P("section", "fsdp", None),
        P("section", "fsdp", None),
    )
    return jax.shard_map(
        per_device,
        mesh=mesh,
        in_specs=placed,
        out_specs=(
            P("section", None, ("rep", "fsdp"), None, None),
            P("section", "fsdp"),
            P("section", "fsdp", None),
            P("section", "fsdp", None),
            P("section", "fsdp", None),
            P("section", "fsdp", None),
            P("section", "fsdp", None),
            P("section", "fsdp", None),
            P("section", None),
            P("section", None),
            P("section", None, "fsdp"),
            P("section", None, "fsdp"),
            P("section", None, "fsdp"),
            P("section", "fsdp"),
            P("section", "fsdp", None),
            P("section", "fsdp"),
            P("section", "fsdp", None),
            P("section", "fsdp", None),
            P("section", "fsdp", None),
        ),
        check_vma=False,
    )
```

profile of v0, /device:TPU:0, one launch (start us, length us, event | category | flops | bytes accessed | tf_op | source)
XLA Modules:
  0.0 2029.6 jit_solution(4429127627408708137)
XLA Ops:
  14.1 26.5 %all_gather.29 = bf16[2,4,1024]{1,0,2:T(2,128)(2,1)S(1)} all-gather(bf16[2,4,64]{1,0,2:T(2,128)(2,1)S(1)} %copy.1432), channel_id=1, replica_groups=mesh['section'=2,'rep'=4,'fsdp'=16] {'fsdp'}, dimensions={2}, use_global_device_ids=true | all-gather | bytes 17408 | tf_op jit(solution)/shard_map/all_gather | solution.py:26
  43.5 38.8 %all-reduce.96 = bf16[256]{0:T(256)(128)(2,1)S(1)} all-reduce(bf16[256]{0:T(256)(128)(2,1)S(1)} %dynamic-update-slice), channel_id=1, replica_groups=mesh['section'=2,'rep'=4,'fsdp'=16] {'fsdp'}, use_global_device_ids=true, to_apply=%add.96 | all-reduce | flops 256 | bytes 1024 | tf_op jit(solution)/shard_map/squeeze | solution.py:427
  82.3 20.4 %all_gather.30 = bf16[1,4,2048]{2,1,0:T(4,128)(2,1)S(1)} all-gather(bf16[1,4,128]{2,1,0:T(4,128)(2,1)S(1)} %copy-done.380), channel_id=1, replica_groups=mesh['section'=2,'rep'=4,'fsdp'=16] {'fsdp'}, dimensions={2}, use_global_device_ids=true | all-gather | bytes 17408 | tf_op jit(solution)/shard_map/all_gather | solution.py:421
  103.8 15.3 slice_bitcast_fusion
  119.0 76.4 %all-gather.5.cloned.1.call-done = bf16[1,1024,6161]{2,1,0:T(8,128)(2,1)} async-done(((bf16[1,64,6161]{2,1,0:T(8,128)(2,1)}), bf16[1,1024,6161]{2,1,0:T(8,128)(2,1)}) %all-gather.5.cloned.1.call-update) | async-done | bytes 12617744 | tf_op jit(solution)/shard_map/all_gather | solution.py:12
  197.8 6.0 slice_bitcast_fusion.4
  203.9 8.5 slice_bitcast_fusion.2
  212.3 36.5 %all-gather.7.cloned.1.call-done = bf16[1,2048,1024]{2,1,0:T(8,128)(2,1)} async-done(((bf16[1,128,1024]{2,1,0:T(8,128)(2,1)}), bf16[1,2048,1024]{2,1,0:T(8,128)(2,1)}) %all-gather.7.cloned.1.call-update) | async-done | bytes 4194320 | tf_op jit(solution)/shard_map/all_gather | solution.py:423
  248.8 60.6 %all-gather.11.cloned.1.call-done = bf16[1,2816,1024]{2,1,0:T(8,128)(2,1)} async-done(((bf16[1,176,1024]{2,1,0:T(8,128)(2,1)}), bf16[1,2816,1024]{2,1,0:T(8,128)(2,1)}) %all-gather.11.cloned.1.call-update) | async-done | bytes 5767184 | tf_op jit(solution)/shard_map/all_gather | solution.py:425
  310.2 165.2 %conditional.6 = (f32[128,1024]{1,0:T(8,128)S(1)}, f32[2,128,1024]{2,1,0:T(8,128)}, bf16[2,128,1024]{2,1,0:T(8,128)(2,1)S(1)}, f32[2,128,1024]{2,1,0:T(8,128)}, ...) conditional(s32[]{:T(128)} %convert_element_type.622, ...), branch_computations={%region_0.1_spmd, %region_1.9_spmd} | conditional | flops 5058131968 | bytes 212554176 | solution.py:478
  336.1 3.9 bitcast_dynamic-update-slice_fusion.3
  348.2 2.9 bitcast_dynamic-update-slice_fusion.7
  354.5 2.9 fusion.2
  359.1 80.0 %custom-call.18 = f32[8,1,128,128]{2,3,1,0:T(8,128)} custom-call(f32[8,1,128,128]{3,2,1,0:T(8,128)} %fusion.8), custom_call_target="InvertDiagBlocksLowerTriangular" | custom-call | tf_op jit(solution)/shard_map/cond/branch_1_fun/while/body/eval_jaxpr/triangular_solve/custom-call.1 | solution.py:117
  439.2 3.2 fusion.16
  442.4 3.2 multiply_reduce_fusion
  453.4 3.3 bitcast_dynamic-update-slice_fusion.6
  480.0 144.0 %conditional.7 = (f32[128,1024]{1,0:T(8,128)S(1)}, f32[2,128,1024]{2,1,0:T(8,128)}, bf16[2,128,1024]{2,1,0:T(8,128)(2,1)S(1)}, f32[2,128,1024]{2,1,0:T(8,128)}, ...) conditional(s32[]{:T(128)} %convert_element_type.625, ...), branch_computations={%region_8.10_spmd, %region_9.17_spmd} | conditional | flops 5054330880 | bytes 182674368 | solution.py:478
  490.7 4.1 bitcast_dynamic-update-slice_fusion.16
  496.4 2.6 copy.1319
  502.7 3.0 bitcast_dynamic-update-slice_fusion.20
  510.5 2.8 fusion.73
  515.8 80.0 %custom-call.19 = f32[8,1,128,128]{2,3,1,0:T(8,128)} custom-call(f32[8,1,128,128]{3,2,1,0:T(8,128)} %fusion.79), custom_call_target="InvertDiagBlocksLowerTriangular" | custom-call | tf_op jit(solution)/shard_map/cond/branch_1_fun/while/body/eval_jaxpr/triangular_solve/custom-call.1 | solution.py:117
  595.8 3.2 fusion.81
  599.1 3.4 multiply_reduce_fusion.2
  608.9 4.6 bitcast_dynamic-update-slice_fusion.19
  624.8 3.1 collective-permute-start.1
  631.1 17.5 conditional.9
  651.1 354.5 %collective-permute-done.2 = bf16[128,1024]{1,0:T(8,128)(2,1)S(1)} collective-permute-done((bf16[128,1024]{1,0:T(8,128)(2,1)S(1)}, bf16[128,1024]{1,0:T(8,128)(2,1)S(1)}, u32[]{:S(2)}, u32[]{:S(2)}) %collective-permute-start.2) | collective-permute-done | bytes 262176 | tf_op jit(solution)/shard_map/ppermute | solution.py:51
  1006.6 204.3 %conditional.10 = (f32[128,1024]{1,0:T(8,128)}, f32[1024]{0:T(1024)}, f32[1024]{0:T(1024)}, f32[4,1024]{1,0:T(4,128)}, f32[4,1024]{1,0:T(4,128)}, /*index=5*/f32...) conditional(s32[]{:T(128)} %convert_element_type.625, ...), branch_computations={%region_63.68_spmd, %region_64.106_spmd} | conditional | flops 6639607808 | bytes 406425088 | solution.py:545
  1009.6 7.0 bitcast_dynamic-update-slice_fusion.41
  1018.6 3.7 fusion.248
  1043.2 80.0 %custom-call.24 = f32[8,1,128,128]{2,3,1,0:T(8,128)} custom-call(f32[8,1,128,128]{3,2,1,0:T(8,128)} %add_bitcast_fusion), custom_call_target="InvertDiagBlocksLowerTriangular" | custom-call | tf_op jit(solution)/shard_map/cond/branch_1_fun/jvp()/while/body/eval_jaxpr/triangular_solve/custom-call.1 | solution.py:117
  1131.7 3.4 copy.1447
  1140.0 2.6 copy.1360
  1149.4 5.0 bitcast_dynamic-update-slice_fusion.43
  1160.4 2.6 multiply_reduce_fusion.14
  1216.4 191.9 %conditional.11 = (f32[128,1024]{1,0:T(8,128)}, f32[1024]{0:T(1024)}, f32[1024]{0:T(1024)}, f32[4,1024]{1,0:T(4,128)S(1)}, f32[4,1024]{1,0:T(4,128)S(1)}, /*inde...) conditional(s32[]{:T(128)} %convert_element_type.622, ...), branch_computations={%region_102.107_spmd, %region_103.145_spmd} | conditional | flops 6639607808 | bytes 389436416 | solution.py:545
  1219.4 7.0 bitcast_dynamic-update-slice_fusion.49
  1228.4 3.7 fusion.434
  1251.7 80.0 %custom-call.27 = f32[8,1,128,128]{2,3,1,0:T(8,128)} custom-call(f32[8,1,128,128]{3,2,1,0:T(8,128)} %add_bitcast_fusion.2), custom_call_target="InvertDiagBlocksLowerTriangular" | custom-call | tf_op jit(solution)/shard_map/cond/branch_1_fun/jvp()/while/body/eval_jaxpr/triangular_solve/custom-call.1 | solution.py:117
  1339.1 3.1 copy.1454
  1347.0 2.6 copy.1388
  1355.7 5.0 bitcast_dynamic-update-slice_fusion.51
  1409.9 5.8 bitcast_convert_fusion.2
  1415.6 5.6 bitcast_convert_fusion.1
  1421.2 22.7 %concatenate.30 = bf16[1024,5633]{1,0:T(8,128)(2,1)} concatenate(bf16[1024,1]{1,0:T(8,128)(2,1)S(1)} %reshape.2693, bf16[1024,2816]{1,0:T(8,128)(2,1)} %bitcast_convert_fusion.2, bf16[1024,2816]{1,0:T(8,128)(2,1)} %bitcast_convert_fusion.1), dimensions={1} | concatenate | bytes 23072768 | tf_op jit(solution)/shard_map/concatenate | solution.py:31
  1447.2 4.0 copy.1462
  1453.3 4.0 copy.1463
  1459.3 4.5 bitcast_convert_fusion.5
  1463.8 4.6 bitcast_convert_fusion.4
  1468.4 22.9 %concatenate.27 = bf16[1024,6161]{1,0:T(8,128)(2,1)} concatenate(bf16[1024,1]{1,0:T(8,128)(2,1)S(1)} %reshape.2692, bf16[1024,1024]{1,0:T(8,128)(2,1)} %copy.1462, bf16[1024,1024]{1,0:T(8,128)(2,1)} %copy.1463, bf16[1024,2048]{1,0:T(8,128)(2,1)} %bitcast_convert_fusion.5, bf16[1024,2048]{1,0:T(8,128)(2,1)} %bitcast_convert_fusion.4, bf16[1024,8]{1,0:T(8,128)(2,1)S(1)} %copy.1464, ...), dimensions={1} | concatenate | bytes 25235456 | tf_op jit(solution)/shard_map/concatenate | solution.py:31
  1491.3 4.8 bitcast_convert_fusion.3
  1496.4 5.6 bitcast_convert_fusion
  1507.8 28.4 %reduce-scatter.15.cloned.1.call-done = bf16[64,5633]{1,0:T(8,128)(2,1)} async-done(((bf16[1024,5633]{1,0:T(8,128)(2,1)}), bf16[64,5633]{1,0:T(8,128)(2,1)}) %reduce-scatter.15.cloned.1.call-update) | async-done | bytes 721040 | tf_op jit(solution)/shard_map/reduce_scatter | solution.py:34
  1538.5 95.9 %reduce-scatter.11.cloned.1.call-done = bf16[64,6161]{1,0:T(8,128)(2,1)} async-done(((bf16[1024,6161]{1,0:T(8,128)(2,1)}), bf16[64,6161]{1,0:T(8,128)(2,1)}) %reduce-scatter.11.cloned.1.call-update) | async-done | bytes 788624 | tf_op jit(solution)/shard_map/reduce_scatter | solution.py:34
  1638.3 76.1 %reduce-scatter.13.cloned.1.call-done = bf16[128,1024]{1,0:T(8,128)(2,1)} async-done(((bf16[2048,1024]{1,0:T(8,128)(2,1)}), bf16[128,1024]{1,0:T(8,128)(2,1)}) %reduce-scatter.13.cloned.1.call-update) | async-done | bytes 262160 | tf_op jit(solution)/shard_map/reduce_scatter | solution.py:597
  1714.3 83.2 %reduce-scatter.17.cloned.1.call-done = bf16[176,1024]{1,0:T(8,128)(2,1)} async-done(((bf16[2816,1024]{1,0:T(8,128)(2,1)}), bf16[176,1024]{1,0:T(8,128)(2,1)}) %reduce-scatter.17.cloned.1.call-update) | async-done | bytes 360464 | tf_op jit(solution)/shard_map/reduce_scatter | solution.py:615
  1800.2 8.3 all-to-all-start
  1809.2 40.4 %all-reduce.97 = bf16[256]{0:T(256)(128)(2,1)S(1)} all-reduce(bf16[256]{0:T(256)(128)(2,1)S(1)} %add_convert_fusion.5), channel_id=5, replica_groups=mesh['section'=2,'rep'=4,'fsdp'=16] {'fsdp'}, use_global_device_ids=true, to_apply=%region_155.160.clone | all-reduce | flops 256 | bytes 1024
  1851.6 21.4 %reduce-scatter.19.cloned.1.call-done = bf16[64,8]{1,0:T(8,128)(2,1)} async-done(((bf16[1024,8]{1,0:T(8,128)(2,1)}), bf16[64,8]{1,0:T(8,128)(2,1)}) %reduce-scatter.19.cloned.1.call-update) | async-done | bytes 1040
  1874.0 74.2 %reduce-scatter.21.cloned.1.call-done = bf16[128,4]{1,0:T(8,128)(2,1)} async-done(((bf16[2048,4]{1,0:T(8,128)(2,1)}), bf16[128,4]{1,0:T(8,128)(2,1)}) %reduce-scatter.21.cloned.1.call-update) | async-done | bytes 1040
  1951.7 17.7 all-reduce.98
  1974.0 38.3 %all-reduce.102.cloned.1.call-done = (bf16[1,64,1024]{2,1,0:T(8,128)(2,1)}, bf16[1,64,1024]{2,1,0:T(8,128)(2,1)}, bf16[1,64,2048]{2,1,0:T(8,128)(2,1)}, bf16[1,6...) async-done(((bf16[1,64,1024]{2,1,0:T(8,128)(2,1)}, ...) | async-done | bytes 2129936 | tf_op jit(solution)/shard_map/psum | solution.py:621
  (1092 shorter events, 368.3 us)
Async XLA Ops:
  7.3 95.4 %all-gather.9.cloned.1.call-start = ((), (), s32[]{:S(2)}) async-start(), calls=%async_computation.9 | async-start | bytes 12533760 | tf_op jit(solution)/shard_map/all_gather | solution.py:12
  10.6 184.8 %all-gather.5.cloned.1.call-start = ((), (), s32[]{:S(2)}) async-start(), calls=%async_computation.7 | async-start | bytes 13647872 | tf_op jit(solution)/shard_map/all_gather | solution.py:12
  12.5 236.3 %all-gather.7.cloned.1.call-start = ((), (), s32[]{:S(2)}) async-start(), calls=%async_computation.8 | async-start | bytes 4456448 | tf_op jit(solution)/shard_map/all_gather | solution.py:423
  13.2 28.7 %copy-start.376 = (u32[128]{0:T(128)S(1)}, u32[128]{0:T(128)}, u32[]{:S(2)}) copy-start(u32[128]{0:T(128)} %constant.1309) | copy-start | bytes 1540
  13.2 30.0 %copy-start.393 = (bf16[1,16]{1,0:T(2,128)(2,1)S(1)}, bf16[1,16]{1,0:T(2,128)(2,1)}, u32[]{:S(2)}) copy-start(bf16[1,16]{1,0:T(2,128)(2,1)} %param.53) | copy-start | bytes 100
  13.2 69.0 %copy-start.380 = (bf16[1,4,128]{2,1,0:T(4,128)(2,1)S(1)}, bf16[1,4,128]{2,1,0:T(4,128)(2,1)}, u32[]{:S(2)}) copy-start(bf16[1,4,128]{2,1,0:T(4,128)(2,1)} %param.52) | copy-start | bytes 3076
  13.3 296.2 %all-gather.11.cloned.1.call-start = ((), (), s32[]{:S(2)}) async-start(), calls=%async_computation.10 | async-start | bytes 6127616 | tf_op jit(solution)/shard_map/all_gather | solution.py:425
  13.8 1522.4 %reduce-scatter.15.cloned.1.call-start = ((), (), s32[]{:S(2)}) async-start(), calls=%async_computation.13 | async-start | bytes 12533760 | tf_op jit(solution)/shard_map/reduce_scatter | solution.py:34
  82.3 227.9 %copy-start.403 = (bf16[256]{0:T(256)(128)(2,1)}, bf16[256]{0:T(256)(128)(2,1)S(1)}, u32[]{:S(2)}) copy-start(bf16[256]{0:T(256)(128)(2,1)S(1)} %all-reduce.96) | copy-start | bytes 1540
  103.8 526.4 %copy-start.197 = (bf16[1024]{0:T(1024)(128)(2,1)}, bf16[1024]{0:T(1024)(128)(2,1)S(1)}, u32[]{:S(2)}) copy-start(bf16[1024]{0:T(1024)(128)(2,1)S(1)} %slice_reduce_fusion.3) | copy-start | bytes 6148
  196.5 433.7 %copy-start.198 = (bf16[1024]{0:T(1024)(128)(2,1)}, bf16[1024]{0:T(1024)(128)(2,1)S(1)}, u32[]{:S(2)}) copy-start(bf16[1024]{0:T(1024)(128)(2,1)S(1)} %slice_reduce_fusion.4) | copy-start | bytes 6148
  197.8 112.3 %copy-start.38 = (bf16[1024,8]{1,0:T(8,128)(2,1)}, bf16[1024,8]{1,0:T(8,128)(2,1)S(1)}, u32[]{:S(2)}) copy-start(bf16[1024,8]{1,0:T(8,128)(2,1)S(1)} %get-tuple-element.5409) | copy-start | bytes 49156
  203.9 106.3 %copy-start.225 = (f32[1,8]{1,0:T(1,128)S(1)}, f32[1,8]{1,0:T(1,128)}, u32[]{:S(2)}) copy-start(f32[1,8]{1,0:T(1,128)} %param.49) | copy-start | bytes 100
  203.9 106.3 %copy-start.394 = (f32[1,8]{1,0:T(1,128)S(1)}, f32[1,8]{1,0:T(1,128)}, u32[]{:S(2)}) copy-start(f32[1,8]{1,0:T(1,128)} %param.48) | copy-start | bytes 100
  453.4 6.2 slice-start
  457.7 5.2 slice-start.12
  476.2 2.8 collective-permute-start
  607.8 5.7 copy-start.11
  608.2 6.5 slice-start.2
  608.9 5.8 slice-start.3
  624.8 3.9 collective-permute-start.1
  648.7 357.9 %copy-start.191 = (f32[4,2048]{1,0:T(4,128)}, f32[4,2048]{1,0:T(4,128)S(1)}, u32[]{:S(2)}) copy-start(f32[4,2048]{1,0:T(4,128)S(1)} %get-tuple-element.2780) | copy-start | bytes 98308
  649.8 355.8 %collective-permute-start.2 = (bf16[128,1024]{1,0:T(8,128)(2,1)S(1)}, bf16[128,1024]{1,0:T(8,128)(2,1)S(1)}, u32[]{:S(2)}, u32[]{:S(2)}) collective-permute-start(bf16[128,1024]{1,0:T(8,128)(2,1)S(1)} %convert_element_type.633), channel_id=1, source_target_pairs={{64,0},{65,1},{66,2},{67,3},{68,4},{69,5},{70,6},{71,7},{72,8},{73... | collective-permute-start | bytes 786440 | tf_op jit(solution)/shard_map/ppermute | solution.py:51
  1006.6 9.9 slice-start.8
  1006.6 11.9 slice-start.20
  1008.2 16.4 copy-start.384
  1009.6 7.0 slice-start.9
  1009.6 9.0 slice-start.21
  1036.7 87.8 %copy-start.111 = (f32[128,1024]{0,1:T(8,128)}, f32[128,1024]{0,1:T(8,128)S(1)}, u32[]{:S(2)}) copy-start(f32[128,1024]{0,1:T(8,128)S(1)} %get-tuple-element.5056) | copy-start | bytes 1572868 | tf_op jit(solution)/shard_map/cond
  1036.9 89.7 %copy-start.21 = (f32[128,1024]{0,1:T(8,128)}, f32[128,1024]{0,1:T(8,128)S(1)}, u32[]{:S(2)}) copy-start(f32[128,1024]{0,1:T(8,128)S(1)} %fusion.255) | copy-start | bytes 1572868 | tf_op jit(solution)/shard_map/cond
  1149.3 5.0 copy-start.34
  1149.3 5.0 copy-start.137
  1149.4 5.0 copy-start.244
  1149.4 5.0 copy-start.353
  1197.1 6.2 copy-start.300
  1197.1 6.2 copy-start.325
  1197.1 6.2 copy-start.365
  1199.4 6.0 copy-start.385
  1203.3 5.8 copy-start.400
  1210.9 5.5 copy-start.193
  1212.0 3.4 collective-permute-start.3
  1216.5 10.0 slice-start.10
  1216.5 11.9 slice-start.22
  1218.0 16.4 copy-start.386
  1219.4 7.0 slice-start.11
  1219.4 9.0 slice-start.23
  1245.2 87.8 %copy-start.113 = (f32[128,1024]{0,1:T(8,128)}, f32[128,1024]{0,1:T(8,128)S(1)}, u32[]{:S(2)}) copy-start(f32[128,1024]{0,1:T(8,128)S(1)} %get-tuple-element.5085) | copy-start | bytes 1572868 | tf_op jit(solution)/shard_map/cond
  1245.4 89.8 %copy-start.25 = (f32[128,1024]{0,1:T(8,128)}, f32[128,1024]{0,1:T(8,128)S(1)}, u32[]{:S(2)}) copy-start(f32[128,1024]{0,1:T(8,128)S(1)} %fusion.441) | copy-start | bytes 1572868 | tf_op jit(solution)/shard_map/cond
  1355.7 5.0 copy-start.36
  1355.7 5.0 copy-start.138
  1355.7 5.0 copy-start.356
  1409.8 5.8 copy-start.91
  1444.0 190.4 %reduce-scatter.11.cloned.1.call-start = ((), (), s32[]{:S(2)}) async-start(), calls=%async_computation.11 | async-start | bytes 13647872 | tf_op jit(solution)/shard_map/reduce_scatter | solution.py:34
  1491.3 223.0 %reduce-scatter.13.cloned.1.call-start = ((), (), s32[]{:S(2)}) async-start(), calls=%async_computation.12 | async-start | bytes 4456448 | tf_op jit(solution)/shard_map/reduce_scatter | solution.py:597
  1496.1 301.3 %reduce-scatter.17.cloned.1.call-start = ((), (), s32[]{:S(2)}) async-start(), calls=%async_computation.14 | async-start | bytes 6127616 | tf_op jit(solution)/shard_map/reduce_scatter | solution.py:615
  1502.0 371.0 %reduce-scatter.19.cloned.1.call-start = ((), (), s32[]{:S(2)}) async-start(), calls=%async_computation.15 | async-start | bytes 278528
  1506.6 441.7 %reduce-scatter.21.cloned.1.call-start = ((), (), s32[]{:S(2)}) async-start(), calls=%async_computation.16 | async-start | bytes 557056
  1507.8 504.6 %all-reduce.102.cloned.1.call-start = ((), (), s32[]{:S(2)}) async-start(), calls=%async_computation.17 | async-start | bytes 4259840 | tf_op jit(solution)/shard_map/psum | solution.py:621
  1800.2 50.6 %all-to-all-start = ((f32[64,1,16]{2,1,0:T(1,128)}), f32[64,1,16]{2,1,0:T(1,128)S(1)}, u32[]{:S(2)}, u32[]{:S(2)}) async-start(f32[64,1,16]{2,1,0:T(1,128)} %broadcast_in_dim.1274), calls=%async_computation.1 | async-start | bytes 65536 | tf_op jit(solution)/shard_map/all_to_all | solution.py:56
  1850.7 170.3 %copy-start.162 = (f32[1,2,1,128,1024]{4,3,2,1,0:T(8,128)}, f32[1,2,1,128,1024]{4,3,2,1,0:T(8,128)S(1)}, u32[]{:S(2)}) copy-start(f32[1,2,1,128,1024]{4,3,2,1,0:T(8,128)S(1)} %bitcast_dynamic-update-slice_fusion.65) | copy-start | bytes 3145732
  2012.4 6.9 copy-start.180
  2012.4 7.8 copy-start.177
  2012.4 8.7 copy-start.176
  2015.7 6.3 copy-start.175
  (261 other events, 615.6 us)
Sparse Core Ops, SparseCore 0:
  10.7 91.2 all-gather.8
  104.7 90.5 all-gather.4
  197.5 51.2 all-gather.6
  250.8 58.5 all-gather.10
  1444.1 92.1 reduce-scatter.14
  1539.9 94.4 reduce-scatter.10
  1637.7 76.5 reduce-scatter.12
  1718.1 79.3 reduce-scatter.16
  1801.6 71.4 reduce-scatter.18
  1876.6 71.6 reduce-scatter.20
  1952.5 59.7 all-reduce.101
where the time goes:
time: 2030 us
  waiting for transfers between devices  950 us (47%)
  other arithmetic  437 us (22%)
  local copies, waits for them, and re-layouts  258 us (13%)
  matrix products  186 us (9%)
  blocking collectives  144 us (7%)
  loops' own time  21.7 us (1%)
    ppermute x4, waiting for transfers between devices, shifted(): return lax.ppermute(value, axis, pairs)  358 us
    another operation x10, other arithmetic, advance(): lax.linalg.triangular_solve(system, target, left_side=True, lower=True, u...  326 us
    reduce_scatter x2, waiting for transfers between devices, sent_together_2(): filled = lax.psum_scatter(both, axis, scatter_dimension=dim, tiled=True)  124 us
    unnamed x13, waiting for transfers between devices  97 us
    reduce_scatter x1, waiting for transfers between devices, per_device(): lax.psum_scatter(full[15].astype(jnp.bfloat16), 'fsdp', scatter_dimension...  83.2 us
    all_gather x2, waiting for transfers between devices, sent_together(): lax.all_gather(both, axis, axis=dim, tiled=True)  76.4 us
    reduce_scatter x1, waiting for transfers between devices, per_device(): lax.psum_scatter(full[11].astype(jnp.bfloat16), 'fsdp', scatter_dimension...  76.1 us
    all_gather x1, waiting for transfers between devices, fetch(): lax.all_gather(w_ffdown, 'fsdp', axis=1, tiled=True)  60.6 us
  transfers between devices with their start and end apart: 16, of which 14 were waited for; matrix products, arithmetic and copies ran while one was open for 6% of the time, Pallas kernels for 0%

commit v1 on v0

v1 whole, which is shorter than its diff:
```python
import functools

import jax
import jax.numpy as jnp
from jax import lax
from jax.experimental import pallas as pl
from jax.experimental.pallas import tpu as pltpu
from jax.sharding import PartitionSpec as P

F32 = jnp.float32
BF16 = jnp.bfloat16
PAD = 128
LANES = 128
VMEM_LIMIT = 56 * 1024 * 1024


def mm(left, right, left_dim=1, right_dim=0):
    return lax.dot_general(
        left.astype(BF16),
        right.astype(BF16),
        (((left_dim,), (right_dim,)), ((), ())),
        preferred_element_type=F32,
    )


def halves(value):
    high = value.astype(BF16)
    return high, (value - high.astype(F32)).astype(BF16)


def mm_fine(left, right):
    left_high, left_low = halves(left)
    right_high, right_low = halves(right)
    return mm(left_high, right_high) + (mm(left_high, right_low) + mm(left_low, right_high))


def mm_ones(ones, value):
    high = value.astype(BF16)
    rest = value - high.astype(F32)
    middle = rest.astype(BF16)
    low = (rest - middle.astype(F32)).astype(BF16)
    return mm(ones, high) + (mm(ones, middle) + mm(ones, low))


def grids(length):
    rows = lax.broadcasted_iota(jnp.int32, (length, length), 0)
    cols = lax.broadcasted_iota(jnp.int32, (length, length), 1)
    return rows, cols


def lower_inverse(strict_part, rows, cols):
    length = strict_part.shape[0]
    unit = (rows == cols).astype(F32)
    base = 8
    nil = jnp.where(rows // base == cols // base, strict_part, 0.0)
    square = mm_fine(nil, nil)
    inverse = unit - nil
    inverse = inverse + mm_fine(inverse, square)
    inverse = inverse + mm_fine(inverse, mm_fine(square, square))
    size = base
    while size < length:
        joined = (rows // (2 * size) == cols // (2 * size)) & (rows // size != cols // size)
        corner = jnp.where(joined, strict_part, 0.0)
        inverse = inverse - mm_fine(inverse, mm_fine(corner, inverse))
        size *= 2
    return inverse


def shift_down(value, by):
    if by == 0:
        return value
    rows = lax.broadcasted_iota(jnp.int32, value.shape, 0)
    return jnp.where(rows >= by, pltpu.roll(value, by, 0), 0.0)


def shift_up(value, by):
    if by == 0:
        return value
    length = value.shape[0]
    rows = lax.broadcasted_iota(jnp.int32, value.shape, 0)
    return jnp.where(rows < length - by, pltpu.roll(value, length - by, 0), 0.0)


def conv_forward(value, taps):
    count = len(taps)
    total = taps[count - 1] * value
    for j in range(count - 1):
        total = total + taps[j] * shift_down(value, count - 1 - j)
    return total


def conv_backward(value, taps, grad):
    count = len(taps)
    grad_value = taps[count - 1] * grad
    grad_taps = []
    for j in range(count):
        by = count - 1 - j
        if by:
            grad_value = grad_value + taps[j] * shift_up(grad, by)
        grad_taps.append(jnp.sum(grad * shift_down(value, by), axis=0, keepdims=True))
    return grad_value, grad_taps


def silu_slope(value, gate):
    return gate * (1.0 + value * (1.0 - gate))


def pick_lane(block, lane):
    lanes = lax.broadcasted_iota(jnp.int32, block.shape, 1)
    return jnp.sum(jnp.where(lanes == lane, block, 0.0), axis=1, keepdims=True)


def softplus(value):
    return jnp.maximum(value, 0.0) + jnp.log1p(jnp.exp(-jnp.abs(value)))


def head_states(query_pre, key_pre, value_pre, alpha, beta, taps, rate, bias, masks):
    rows, cols, lower, strict = masks
    key_size = query_pre.shape[-1]
    query_conv = conv_forward(query_pre, taps[0])
    key_conv = conv_forward(key_pre, taps[1])
    value_conv = conv_forward(value_pre, taps[2])
    query_gate = jax.nn.sigmoid(query_conv)
    key_gate = jax.nn.sigmoid(key_conv)
    value_gate = jax.nn.sigmoid(value_conv)
    query_act = query_conv * query_gate
    key_act = key_conv * key_gate
    values = value_conv * value_gate
    query_scale = lax.rsqrt(jnp.sum(query_act * query_act, axis=-1, keepdims=True) + 1e-06)
    key_scale = lax.rsqrt(jnp.sum(key_act * key_act, axis=-1, keepdims=True) + 1e-06)
    query_unit = query_act * query_scale
    keys = key_act * key_scale
    queries = query_unit * key_size ** (-0.5)
    strength = jax.nn.sigmoid(beta)
    decay = -rate * softplus(alpha + bias)
    running = mm_ones(lower.astype(BF16), jnp.broadcast_to(decay, rows.shape))
    spread = running - running.T
    ratios = jnp.exp(jnp.where(lower, spread, 0.0)) * lower.astype(F32)
    key_key = mm(keys, keys, 1, 1)
    query_key = mm(queries, keys, 1, 1)
    key_ratio = jnp.where(strict, key_key * ratios, 0.0)
    weighting = query_key * ratios
    return dict(
        query_conv=query_conv,
        key_conv=key_conv,
        value_conv=value_conv,
        query_gate=query_gate,
        key_gate=key_gate,
        value_gate=value_gate,
        query_scale=query_scale,
        key_scale=key_scale,
        query_unit=query_unit,
        queries=queries,
        keys=keys,
        values=values,
        strength=strength,
        decay=decay,
        ratios=ratios,
        key_ratio=key_ratio,
        weighting=weighting,
    )


def read_taps(ref, lo, hi):
    return [ref[j : j + 1, lo:hi] for j in range(4)]


def mixer_forward_kernel(
    heads, length, query_ref, key_ref, value_ref, gate_ref, ab_ref, tq_ref, tk_ref, tv_ref, head_ref, gain_ref, mixed_ref, inverse_ref
):
    step = pl.program_id(0)
    per_step = inverse_ref.shape[0]
    sequences = query_ref.shape[0] // length
    key_size = query_ref.shape[1] // per_step
    value_size = value_ref.shape[1] // per_step
    rows, cols = grids(length)
    masks = (rows, cols, rows >= cols, rows > cols)
    gain = gain_ref[0:1, :]
    for local in range(per_step):
        head = step * per_step + local
        kc = slice(local * key_size, (local + 1) * key_size)
        vc = slice(local * value_size, (local + 1) * value_size)
        rate = jnp.exp(pick_lane(head_ref[0:1, :], head))
        bias = pick_lane(head_ref[1:2, :], head)
        taps = (
            read_taps(tq_ref, kc.start, kc.stop),
            read_taps(tk_ref, kc.start, kc.stop),
            read_taps(tv_ref, vc.start, vc.stop),
        )
        for seq in range(sequences):
            tr = slice(seq * length, (seq + 1) * length)
            ab = ab_ref[tr, :]
            alpha = pick_lane(ab, head)
            beta = pick_lane(ab, heads + head)
            s = head_states(
                query_ref[tr, kc], key_ref[tr, kc], value_ref[tr, vc], alpha, beta, taps, rate, bias, masks
            )
            inverse = lower_inverse(s["strength"] * s["key_ratio"], rows, cols)
            inverse_ref[local, seq] = inverse
            updates = mm(inverse, s["strength"] * s["values"])
            recur = mm(s["weighting"], updates)
            scale = lax.rsqrt(jnp.mean(recur * recur, axis=-1, keepdims=True) + 0.002)
            gate = gate_ref[tr, vc]
            mixed = recur * scale * gain * (gate * jax.nn.sigmoid(gate))
            mixed_ref[tr, vc] = mixed.astype(mixed_ref.dtype)


def mixer_backward_kernel(
    heads,
    length,
    query_ref,
    key_ref,
    value_ref,
    gate_ref,
    ab_ref,
    tq_ref,
    tk_ref,
    tv_ref,
    head_ref,
    gain_ref,
    inverse_ref,
    grad_ref,
    pre_a_ref,
    pre_b_ref,
    gtq_ref,
    gtk_ref,
    gtv_ref,
    ghead_ref,
    ggain_ref,
    gab_ref,
):
    step = pl.program_id(0)
    per_step = inverse_ref.shape[0]
    sequences = query_ref.shape[0] // length
    key_size = query_ref.shape[1] // per_step
    value_size = value_ref.shape[1] // per_step
    key_cols = heads * key_size
    value_cols = heads * value_size
    rows, cols = grids(length)
    lower, strict = rows >= cols, rows > cols
    masks = (rows, cols, lower, strict)
    upper = (rows <= cols).astype(BF16)
    gain = gain_ref[0:1, :]

    @pl.when(step == 0)
    def _():
        ghead_ref[...] = jnp.zeros_like(ghead_ref)
        ggain_ref[...] = jnp.zeros_like(ggain_ref)
        gab_ref[...] = jnp.zeros_like(gab_ref)

    lanes = lax.broadcasted_iota(jnp.int32, (length, LANES), 1)
    lane_row = lax.broadcasted_iota(jnp.int32, (1, LANES), 1)
    for local in range(per_step):
        head = step * per_step + local
        kc = slice(local * key_size, (local + 1) * key_size)
        vc = slice(local * value_size, (local + 1) * value_size)
        rate = jnp.exp(pick_lane(head_ref[0:1, :], head))
        bias = pick_lane(head_ref[1:2, :], head)
        taps = (
            read_taps(tq_ref, kc.start, kc.stop),
            read_taps(tk_ref, kc.start, kc.stop),
            read_taps(tv_ref, vc.start, vc.stop),
        )
        tap_totals = None
        gain_total = None
        rate_total = None
        bias_total = None
        for seq in range(sequences):
            tr = slice(seq * length, (seq + 1) * length)
            ab = ab_ref[tr, :]
            alpha = pick_lane(ab, head)
            beta = pick_lane(ab, heads + head)
            query_pre, key_pre, value_pre = query_ref[tr, kc], key_ref[tr, kc], value_ref[tr, vc]
            s = head_states(query_pre, key_pre, value_pre, alpha, beta, taps, rate, bias, masks)
            strength, keys, queries, values = s["strength"], s["keys"], s["queries"], s["values"]
            inverse = inverse_ref[local, seq]
            updates = mm(inverse, strength * values)
            recur = mm(s["weighting"], updates)
            scale = lax.rsqrt(jnp.mean(recur * recur, axis=-1, keepdims=True) + 0.002)
            normal = recur * scale
            gate = gate_ref[tr, vc]
            gate_sig = jax.nn.sigmoid(gate)
            gate_act = gate * gate_sig
            grad = grad_ref[tr, vc]
            grad_normal = grad * normal
            gain_part = jnp.sum(grad_normal * gate_act, axis=0, keepdims=True)
            grad_gate = grad_normal * gain * silu_slope(gate, gate_sig)
            grad_norm = grad * gain * gate_act
            grad_recur = scale * (grad_norm - normal * jnp.mean(grad_norm * normal, axis=-1, keepdims=True))
            grad_weight = jnp.where(lower, mm(grad_recur, updates, 1, 1), 0.0)
            grad_updates = mm(s["weighting"], grad_recur, 0, 0)
            grad_target = mm(inverse, grad_updates, 0, 0)
            grad_values = strength * grad_target
            grad_system = jnp.where(strict, -mm(grad_target, updates, 1, 1), 0.0)
            ratio_part = grad_system * s["key_ratio"]
            grad_strength = jnp.sum(grad_target * values, axis=-1, keepdims=True) + jnp.sum(
                ratio_part, axis=-1, keepdims=True
            )
            grad_kk = grad_system * strength * s["ratios"]
            grad_qk = grad_weight * s["ratios"]
            through = jnp.where(strict, ratio_part * strength + grad_weight * s["weighting"], 0.0)
            grad_running = jnp.sum(through - through.T, axis=-1, keepdims=True)
            grad_decay = mm_ones(upper, jnp.broadcast_to(grad_running, rows.shape))[:, 0:1]
            grad_keys = mm(grad_kk + grad_kk.T, keys) + mm(grad_qk, queries, 0, 0)
            grad_queries = mm(grad_qk, keys) * key_size ** (-0.5)
            query_unit = s["query_unit"]
            grad_query_act = s["query_scale"] * (
                grad_queries - query_unit * jnp.sum(grad_queries * query_unit, axis=-1, keepdims=True)
            )
            grad_key_act = s["key_scale"] * (
                grad_keys - keys * jnp.sum(grad_keys * keys, axis=-1, keepdims=True)
            )
            grad_query_pre, query_taps = conv_backward(
                query_pre, taps[0], grad_query_act * silu_slope(s["query_conv"], s["query_gate"])
            )
            grad_key_pre, key_taps = conv_backward(
                key_pre, taps[1], grad_key_act * silu_slope(s["key_conv"], s["key_gate"])
            )
            grad_value_pre, value_taps = conv_backward(
                value_pre, taps[2], grad_values * silu_slope(s["value_conv"], s["value_gate"])
            )
            grad_beta = grad_strength * strength * (1.0 - strength)
            grad_inner = -rate * grad_decay * jax.nn.sigmoid(alpha + bias)
            rate_part = jnp.sum(grad_decay * s["decay"], axis=0, keepdims=True)
            bias_part = jnp.sum(grad_inner, axis=0, keepdims=True)

            def put(ref, first, block):
                start = pl.multiple_of(first, LANES)
                ref[tr, pl.ds(start, block.shape[1])] = block.astype(ref.dtype)

            put(pre_a_ref, value_cols + head * key_size, grad_query_pre)
            put(pre_b_ref, value_cols + head * key_size, grad_key_pre)
            put(pre_a_ref, head * value_size, grad_value_pre)
            put(pre_b_ref, head * value_size, grad_gate)
            gab_ref[tr, :] = gab_ref[tr, :] + (
                jnp.where(lanes == head, grad_inner, 0.0) + jnp.where(lanes == heads + head, grad_beta, 0.0)
            )
            parts = (query_taps, key_taps, value_taps)
            if tap_totals is None:
                tap_totals, gain_total, rate_total, bias_total = parts, gain_part, rate_part, bias_part
            else:
                tap_totals = tuple(
                    [a + b for a, b in zip(one, two)] for one, two in zip(tap_totals, parts)
                )
                gain_total = gain_total + gain_part
                rate_total = rate_total + rate_part
                bias_total = bias_total + bias_part
        for j in range(4):
            gtq_ref[j : j + 1, kc] = tap_totals[0][j]
            gtk_ref[j : j + 1, kc] = tap_totals[1][j]
            gtv_ref[j : j + 1, vc] = tap_totals[2][j]
        ggain_ref[0:1, :] = ggain_ref[0:1, :] + gain_total
        ghead_ref[0:1, :] = ghead_ref[0:1, :] + jnp.where(lane_row == head, rate_total, 0.0)
        ghead_ref[1:2, :] = ghead_ref[1:2, :] + jnp.where(lane_row == head, bias_total, 0.0)

    @pl.when(step == heads // per_step - 1)
    def _():
        first = key_cols + value_cols
        pre_a_ref[:, first : first + LANES] = gab_ref[...].astype(pre_a_ref.dtype)


HEADS_PER_STEP = 2


def mixer_specs(tokens, heads, key_size, value_size):
    per_step = HEADS_PER_STEP
    wide_key, wide_value = per_step * key_size, per_step * value_size
    key_first = heads * value_size // wide_key
    ab_first = (heads * value_size + heads * key_size) // LANES
    return [
        pl.BlockSpec((tokens, wide_key), lambda h: (0, key_first + h)),
        pl.BlockSpec((tokens, wide_key), lambda h: (0, key_first + h)),
        pl.BlockSpec((tokens, wide_value), lambda h: (0, h)),
        pl.BlockSpec((tokens, wide_value), lambda h: (0, h)),
        pl.BlockSpec((tokens, LANES), lambda h: (0, ab_first)),
        pl.BlockSpec((8, wide_key), lambda h: (0, h)),
        pl.BlockSpec((8, wide_key), lambda h: (0, h)),
        pl.BlockSpec((8, wide_value), lambda h: (0, h)),
        pl.BlockSpec((8, LANES), lambda h: (0, 0)),
        pl.BlockSpec((8, value_size), lambda h: (0, 0)),
    ]


def mixer_forward(pre_a, pre_b, small, length, heads, key_size, value_size):
    tokens = pre_a.shape[0]
    per_step = HEADS_PER_STEP
    return pl.pallas_call(
        functools.partial(mixer_forward_kernel, heads, length),
        grid=(heads // per_step,),
        in_specs=mixer_specs(tokens, heads, key_size, value_size),
        out_specs=[
            pl.BlockSpec((tokens, per_step * value_size), lambda h: (0, h)),
            pl.BlockSpec((per_step, tokens // length, length, length), lambda h: (h, 0, 0, 0)),
        ],
        out_shape=[
            jax.ShapeDtypeStruct((tokens, heads * value_size), BF16),
            jax.ShapeDtypeStruct((heads, tokens // length, length, length), F32),
        ],
        compiler_params=pltpu.CompilerParams(vmem_limit_bytes=VMEM_LIMIT),
        name="mixer_forward",
    )(pre_a, pre_b, pre_a, pre_b, pre_a, *small)


def mixer_backward(pre_a, pre_b, small, inverse, grad, length, heads, key_size, value_size):
    tokens, width_a = pre_a.shape
    width_b = pre_b.shape[1]
    per_step = HEADS_PER_STEP
    wide_key, wide_value = per_step * key_size, per_step * value_size
    fixed = lambda h: (0, 0)
    moving = lambda h: (0, h)
    return pl.pallas_call(
        functools.partial(mixer_backward_kernel, heads, length),
        grid=(heads // per_step,),
        in_specs=mixer_specs(tokens, heads, key_size, value_size)
        + [
            pl.BlockSpec((per_step, tokens // length, length, length), lambda h: (h, 0, 0, 0)),
            pl.BlockSpec((tokens, wide_value), moving),
        ],
        out_specs=[
            pl.BlockSpec((tokens, width_a), fixed),
            pl.BlockSpec((tokens, width_b), fixed),
            pl.BlockSpec((8, wide_key), moving),
            pl.BlockSpec((8, wide_key), moving),
            pl.BlockSpec((8, wide_value), moving),
            pl.BlockSpec((8, LANES), fixed),
            pl.BlockSpec((8, value_size), fixed),
        ],
        out_shape=[
            jax.ShapeDtypeStruct((tokens, width_a), BF16),
            jax.ShapeDtypeStruct((tokens, width_b), BF16),
            jax.ShapeDtypeStruct((8, heads * key_size), F32),
            jax.ShapeDtypeStruct((8, heads * key_size), F32),
            jax.ShapeDtypeStruct((8, heads * value_size), F32),
            jax.ShapeDtypeStruct((8, LANES), F32),
            jax.ShapeDtypeStruct((8, value_size), F32),
        ],
        scratch_shapes=[pltpu.VMEM((tokens, LANES), F32)],
        compiler_params=pltpu.CompilerParams(vmem_limit_bytes=VMEM_LIMIT),
        name="mixer_backward",
    )(pre_a, pre_b, pre_a, pre_b, pre_a, *small, inverse, grad)


def swapped(value):
    return lax.ppermute(value, "section", [(0, 1), (1, 0)])


def pair_sum(value):
    return value + swapped(value)


SIDE = 4


class Ring:
    def __init__(self, axis):
        if axis == "y":
            self.name, self.position = "rep", lax.axis_index("rep")
            self.pairs = lambda by: [(y, (y + by) % SIDE) for y in range(SIDE)]
            return
        self.name = "fsdp"
        index = lax.axis_index("fsdp")
        z, x = index // SIDE, index % SIDE
        if axis == "x":
            self.position = x
            step = lambda z, x, by: z * SIDE + (x + by) % SIDE
        else:
            self.position = z
            step = lambda z, x, by: (z + by) % SIDE * SIDE + x
        self.pairs = lambda by: [
            (z * SIDE + x, step(z, x, by)) for z in range(SIDE) for x in range(SIDE)
        ]

    def move(self, value, by):
        return lax.ppermute(value, self.name, self.pairs(by))


def ring_gather(block, ring):
    count = block.shape[0] // 2
    from_left = ring.move(block, 1)
    from_right = ring.move(block, -1)
    far_first = ring.move(from_left[:count], 1)
    far_last = ring.move(from_right[count:], -1)
    return block, from_right, far_first, far_last, from_left


def torus_gather(shard, x_first):
    rows = shard.shape[0]
    if x_first:
        block = jnp.concatenate(ring_gather(shard, Ring("x")), axis=0)
        pieces = ring_gather(block, Ring("z"))
        return jnp.concatenate(pieces, axis=0), pieces[1]
    block = jnp.concatenate(ring_gather(shard, Ring("z")), axis=0)
    own, right, far_first, far_last, left = ring_gather(block, Ring("x"))
    cut = lambda piece, k: piece[k * rows : (k + 1) * rows]
    rows_of = []
    for kz in range(SIDE):
        far = cut(far_first, kz) if kz < SIDE // 2 else cut(far_last, kz - SIDE // 2)
        rows_of += [cut(own, kz), cut(right, kz), far, cut(left, kz)]
    return jnp.concatenate(rows_of, axis=0), right


def added(first, *others):
    total = first.astype(F32)
    for other in others:
        total = total + other.astype(F32)
    return total.astype(BF16)


def ring_scatter(parts, ring):
    ahead, behind, rest, own = parts
    count = own.shape[0] // 2
    from_left = ring.move(ahead, 1)
    from_right = ring.move(behind, -1)
    next_left = ring.move(added(rest[:count], from_left[:count]), 1)
    next_right = ring.move(added(rest[count:], from_right[:count]), -1)
    return jnp.concatenate(
        [
            added(own[:count], next_left, from_right[count:]),
            added(own[count:], from_left[count:], next_right),
        ],
        axis=0,
    )


def torus_scatter(chunks, x_first):
    first, second = ("x", "z") if x_first else ("z", "x")

    def parts(total, make):
        quarter, half = total // SIDE, total // SIDE // 2
        join = lambda one, two: make([(one, one + half), (two, two + half)])
        return [
            join(2 * quarter, quarter + half),
            join(2 * quarter + half, 3 * quarter),
            join(quarter, 3 * quarter + half),
            make([(0, quarter)]),
        ]

    block = ring_scatter(parts(chunks.total, chunks.make), Ring(first))
    make = lambda cuts: jnp.concatenate([block[i:j] for i, j in cuts], axis=0)
    return ring_scatter(parts(block.shape[0], make), Ring(second))


class Chunks:
    def __init__(self, products):
        self.products = products
        self.total = products[0][0].shape[1]

    def make(self, cuts):
        blocks = []
        for left, right, extra in self.products:
            rows = jnp.concatenate([left[:, i:j] for i, j in cuts], axis=1)
            block = dot_tn(rows, right)
            if extra is not None:
                block = block + jnp.concatenate([extra[i:j] for i, j in cuts], axis=0)
            blocks.append(block.astype(BF16))
        return jnp.concatenate(blocks, axis=1)


def own_order(rows):
    index = lax.axis_index("fsdp")
    z, x = index // SIDE, index % SIDE
    place = jnp.arange(SIDE * SIDE * rows, dtype=jnp.int32)
    by_z, by_x, offset = place // (SIDE * rows), place // rows % SIDE, place % rows
    source = ((z + by_z) % SIDE * SIDE + (x + by_x) % SIDE) * rows + offset
    return (place[:, None] == source[None, :]).astype(BF16)


def flipped_order(rows):
    place = jnp.arange(SIDE * SIDE * rows, dtype=jnp.int32)
    by_x, by_z, offset = place // (SIDE * rows), place // rows % SIDE, place % rows
    source = (by_z * SIDE + by_x) * rows + offset
    return (place[:, None] == source[None, :]).astype(BF16)


def rep_sum(value):
    near = [(0, 1), (1, 0), (2, 3), (3, 2)]
    across = [(0, 3), (3, 0), (1, 2), (2, 1)]
    count = value.shape[0] // 2
    done = []
    for part, order in ((value[:count], (near, across)), (value[count:], (across, near))):
        for pairs in order:
            part = added(part, lax.ppermute(part, "rep", pairs))
        done.append(part)
    return jnp.concatenate(done, axis=0)


def dot(left, right):
    return jnp.dot(left, right, preferred_element_type=F32)


def dot_nt(left, right):
    return lax.dot_general(left, right, (((1,), (1,)), ((), ())), preferred_element_type=F32)


def dot_tn(left, right):
    return lax.dot_general(left, right, (((0,), (0,)), ((), ())), preferred_element_type=F32)


def inverse_rms(value):
    return lax.rsqrt(jnp.mean(value * value, axis=-1, keepdims=True) + 1e-06)


def norm_backward(value, gain, grad):
    scale = inverse_rms(value)
    unit = value * scale
    inner = grad * gain
    grad_value = scale * (inner - unit * jnp.mean(inner * unit, axis=-1, keepdims=True))
    return grad_value, jnp.sum(grad * unit, axis=0)


def per_device(
    inputs,
    out_grad,
    mixer_norm_gain,
    w_query,
    w_key,
    w_value,
    w_gate,
    w_alpha,
    w_beta,
    log_rate,
    dt_bias,
    conv_query,
    conv_key,
    conv_value,
    out_gain,
    w_out,
    gain_ffn,
    w_ffgate,
    w_ffup,
    w_ffdown,
):
    core = lax.axis_index("section")
    first_core = core == 0
    micro, _, length, width = inputs.shape
    tokens = micro * length
    members = lax.axis_size("fsdp")
    cores = 2
    all_heads = log_rate.shape[1]
    heads = all_heads // cores
    key_size = w_query.shape[2] // all_heads
    value_size = w_value.shape[2] // all_heads
    key_cols, value_cols = heads * key_size, heads * value_size
    ffn_cols = w_ffgate.shape[2] // cores
    rows = w_query.shape[1]
    taps = conv_query.shape[1]
    out_rows, down_rows = w_out.shape[1], w_ffdown.shape[1]
    value_split = conv_value.shape[2] // rows
    gain_rows = out_gain.shape[1]

    def choose(first, second):
        return jnp.where(first_core, first, second)

    small_cols = jnp.concatenate(
        [
            mixer_norm_gain[0][:, None],
            gain_ffn[0][:, None],
            conv_query[0].T,
            conv_key[0].T,
            conv_value[0].reshape(taps * value_split, rows).T,
            jnp.pad(out_gain[0], (0, rows - gain_rows))[:, None],
        ],
        axis=1,
    )
    small_count = small_cols.shape[1]
    ab_cols = 2 * heads
    spare = PAD - ab_cols - small_count
    main_a = value_cols + key_cols
    split = 2 * LANES
    out_first, down_first = ffn_cols, ffn_cols + value_cols

    lane_rows = out_rows + down_rows
    both_t = jnp.concatenate([w_out[0].T, w_ffdown[0].T], axis=1)
    both_t = jnp.pad(both_t, ((0, 0), (0, -lane_rows % LANES))).reshape(members, rows, -1)
    both_t = lax.all_to_all(both_t, "fsdp", split_axis=0, concat_axis=0, tiled=True)
    out_t = both_t[:, :, :out_rows].transpose(1, 0, 2).reshape(rows, members * out_rows)
    down_t = both_t[:, :, out_rows:lane_rows].transpose(1, 0, 2).reshape(rows, members * down_rows)

    def cut(w, k):
        n = w.shape[1] // cores
        return w[:, k * n : (k + 1) * n]

    def in_piece(k):
        return jnp.concatenate(
            [cut(w[0], k) for w in (w_value, w_query, w_alpha, w_beta)]
            + [small_cols, jnp.zeros((rows, spare), BF16)]
            + [cut(w[0], k) for w in (w_gate, w_key)],
            axis=1,
        )

    def ffn_piece(k):
        down = cut(down_t, k)
        return jnp.concatenate(
            [cut(w_ffgate[0], k), cut(out_t, k), down[:, :split], cut(w_ffup[0], k), down[:, split:]], axis=1
        )

    def both(make):
        left, right = make(0), make(1)
        own, sent = choose(left, right), choose(right, left)
        received = swapped(sent)
        return choose(own, received), choose(received, own)

    in_pieces = both(in_piece)
    ffn_pieces = both(ffn_piece)
    in_a = main_a + PAD
    ffn_a = down_first + split
    rate_rows = jnp.stack([log_rate[0], dt_bias[0]])
    other_rates = swapped(rate_rows)
    rates = (choose(rate_rows, other_rates), choose(other_rates, rate_rows))
    order = own_order(rows)
    flip = flipped_order(rows)

    def ordered(value):
        return dot(value, order)

    def unordered(value):
        high = value.astype(BF16)
        rest = value - high.astype(F32)
        middle = rest.astype(BF16)
        low = (rest - middle.astype(F32)).astype(BF16)
        return dot_nt(high, order) + (dot_nt(middle, order) + dot_nt(low, order))

    def flipped(value):
        return dot(value, flip).astype(BF16)

    def after(value, token):
        return value if token is None else lax.optimization_barrier((value, token))[0]

    def fetch(pieces, wide, token):
        pieces = after(pieces, token)
        full_a, token_a = torus_gather(pieces[:, :wide], True)
        full_b, token_b = torus_gather(pieces[:, wide:], False)
        return full_a, full_b, (token_a, token_b)

    def small_params(in_full, layer):
        first = main_a + ab_cols
        small_own = in_full[:, first : first + small_count].T
        small = dot_nt(small_own, order)
        at = 2
        conv_q = small[at : at + taps]
        conv_k = small[at + taps : at + 2 * taps]
        at += 2 * taps
        conv_v = small[at : at + taps * value_split].reshape(taps, value_split, members, rows)
        conv_v = conv_v.transpose(0, 2, 1, 3).reshape(taps, members * value_split * rows)
        at += taps * value_split
        gain_out = small[at].reshape(members, rows)[:, :gain_rows].reshape(1, members * gain_rows)

        def own_cols(value, count):
            mine = choose(value[:, :count], value[:, count:])
            return jnp.pad(mine, ((0, 8 - value.shape[0]), (0, 0)))

        rate = own_cols(rates[layer], heads)
        smalls = (
            own_cols(conv_q, key_cols),
            own_cols(conv_k, key_cols),
            own_cols(conv_v, value_cols),
            jnp.pad(rate, ((0, 0), (0, LANES - heads))),
            jnp.pad(gain_out, ((0, 7), (0, 0))),
        )
        return small_own[0].astype(F32), small_own[1].astype(F32), smalls

    def forward_layer(source, in_full, ffn_full, params):
        in_w, in_v = in_full
        ffn_w, ffn_v = ffn_full
        gain_mix, gain_in, smalls = params
        normed = (source * inverse_rms(source) * gain_mix).astype(BF16)
        pre_a, pre_b = dot(normed, in_w), dot(normed, in_v)
        mixed, inverse = mixer_forward(pre_a, pre_b, smalls, length, heads, key_size, value_size)
        after_mix = source + pair_sum(dot_nt(mixed, ffn_w[:, out_first:down_first]))
        normed_ffn = (after_mix * inverse_rms(after_mix) * gain_in).astype(BF16)
        gate_act = dot(normed_ffn, ffn_w[:, :ffn_cols])
        up_act = dot(normed_ffn, ffn_v[:, :ffn_cols])
        hidden = (gate_act * jax.nn.sigmoid(gate_act) * up_act).astype(BF16)
        part = dot_nt(hidden[:, :split], ffn_w[:, down_first:]) + dot_nt(hidden[:, split:], ffn_v[:, ffn_cols:])
        layer_out = after_mix + pair_sum(part)
        return layer_out, (source, normed, pre_a, pre_b, inverse, mixed, after_mix, normed_ffn, gate_act, up_act, hidden)

    def backward_layer(grad_top, saved, in_full, ffn_full, params):
        source, normed, pre_a, pre_b, inverse, mixed, after_mix, normed_ffn, gate_act, up_act, hidden = saved
        in_w, in_v = in_full
        ffn_w, ffn_v = ffn_full
        gain_mix, gain_in, smalls = params
        down_grad = grad_top.astype(BF16)
        hidden_grad = jnp.concatenate(
            [dot(down_grad, ffn_w[:, down_first:]), dot(down_grad, ffn_v[:, ffn_cols:])], axis=1
        )
        gate_sig = jax.nn.sigmoid(gate_act)
        gate_grad = (hidden_grad * up_act * silu_slope(gate_act, gate_sig)).astype(BF16)
        up_grad = (hidden_grad * (gate_act * gate_sig)).astype(BF16)
        ffn_in_grad = pair_sum(dot_nt(gate_grad, ffn_w[:, :ffn_cols]) + dot_nt(up_grad, ffn_v[:, :ffn_cols]))
        residual, grad_gain_ffn = norm_backward(after_mix, gain_in, ffn_in_grad)
        mix_grad = grad_top + residual
        mix_low = mix_grad.astype(BF16)
        mixed_grad = dot(mix_low, ffn_w[:, out_first:down_first])
        grad_ffn = (
            torus_scatter(
                Chunks(
                    [
                        (flipped(normed_ffn), gate_grad, None),
                        (flipped(mix_low), mixed, None),
                        (flipped(down_grad), hidden[:, :split], None),
                    ]
                ),
                True,
            ),
            torus_scatter(Chunks([(normed_ffn, up_grad, None), (down_grad, hidden[:, split:], None)]), False),
        )
        grad_ffn = rep_sum(jnp.concatenate(grad_ffn, axis=1))
        pre_a_grad, pre_b_grad, gtq, gtk, gtv, ghead, ggain = mixer_backward(
            pre_a, pre_b, smalls, inverse, mixed_grad, length, heads, key_size, value_size
        )
        normed_grad = pair_sum(dot_nt(pre_a_grad, in_w) + dot_nt(pre_b_grad, in_v))
        source_part, grad_gain_mix = norm_backward(source, gain_mix, normed_grad)
        source_grad = mix_grad + source_part

        def whole_cols(value):
            zeros = jnp.zeros_like(value)
            return choose(
                jnp.concatenate([value, zeros], axis=1), jnp.concatenate([zeros, value], axis=1)
            )

        conv_v = whole_cols(gtv[:taps]).reshape(taps, members, value_split, rows)
        conv_v = conv_v.transpose(0, 2, 1, 3).reshape(taps * value_split, members * rows)
        gain_out = ggain[0].reshape(members, gain_rows)
        head_part = whole_cols(ghead[:2, :heads]).reshape(1, 2 * all_heads)
        head_part = jnp.broadcast_to(head_part, (members, 2 * all_heads))
        tail = jnp.concatenate(
            [gain_out, head_part, jnp.zeros((members, rows - gain_rows - 2 * all_heads), F32)], axis=1
        )
        once = first_core.astype(F32)
        gains = jnp.stack([grad_gain_mix, grad_gain_ffn]) * once
        others = jnp.concatenate(
            [whole_cols(gtq[:taps]), whole_cols(gtk[:taps]), conv_v, tail.reshape(1, members * rows)], axis=0
        )
        small = jnp.concatenate([gains.astype(BF16), ordered(others.astype(BF16)).astype(BF16)], axis=0)
        small = jnp.concatenate(
            [jnp.zeros((ab_cols, width), BF16), small, jnp.zeros((spare, width), BF16)], axis=0
        )
        small = lax.dot_general(flip, small, (((0,), (1,)), ((), ())), preferred_element_type=F32)
        turned = flipped(normed)
        grad_in = (
            torus_scatter(
                Chunks([(turned, pre_a_grad[:, :main_a], None), (turned, pre_a_grad[:, main_a:], small)]), True
            ),
            torus_scatter(Chunks([(normed, pre_b_grad, None)]), False),
        )
        grad_in = rep_sum(jnp.concatenate(grad_in, axis=1))
        return source_grad, grad_in, grad_ffn

    def to_owner(first, second):
        own = choose(first, second)
        received = swapped(choose(second, first))
        return choose(own, received), choose(received, own)

    source = ordered(inputs.reshape(tokens, width))
    in_0a, in_0b, token = fetch(in_pieces[0], in_a, None)
    ffn_0a, ffn_0b, token = fetch(ffn_pieces[0], ffn_a, token)
    in_1a, in_1b, token = fetch(in_pieces[1], in_a, token)
    ffn_1a, ffn_1b, token = fetch(ffn_pieces[1], ffn_a, token)
    in_0, ffn_0, in_1, ffn_1 = (in_0a, in_0b), (ffn_0a, ffn_0b), (in_1a, in_1b), (ffn_1a, ffn_1b)
    params_0, params_1 = small_params(in_0a, 0), small_params(in_1a, 1)
    first_out, first_saved = forward_layer(source, in_0, ffn_0, params_0)
    middle = first_out.astype(BF16).astype(F32)
    block_out, second_saved = forward_layer(middle, in_1, ffn_1, params_1)
    cotangent = ordered(out_grad.reshape(tokens, width))
    second_grad, second_in, second_ffn = backward_layer(cotangent, second_saved, in_1, ffn_1, params_1)
    input_grad, first_in, first_ffn = backward_layer(
        second_grad.astype(BF16).astype(F32), first_saved, in_0, ffn_0, params_0
    )
    in_left, in_right = to_owner(first_in, second_in)
    ffn_left, ffn_right = to_owner(first_ffn, second_ffn)

    def joined(left, right, first, count):
        span = slice(first, first + count)
        return jnp.concatenate([left[:, span], right[:, span]], axis=1).astype(F32)[None]

    gate_first = main_a + PAD
    up_first = down_first + split
    down_rest = up_first + ffn_cols
    full_out = jnp.concatenate(
        [side[:, out_first:down_first] for side in (ffn_left, ffn_right)], axis=1
    ).reshape(rows, members, out_rows)
    full_down = jnp.concatenate(
        [part for side in (ffn_left, ffn_right) for part in (side[:, down_first:up_first], side[:, down_rest:])], axis=1
    ).reshape(rows, members, down_rows)
    back = jnp.concatenate([full_out, full_down], axis=2).transpose(1, 0, 2)
    back = jnp.pad(back, ((0, 0), (0, 0), (0, -lane_rows % LANES)))
    back = lax.all_to_all(back, "fsdp", split_axis=0, concat_axis=0, tiled=True).reshape(width, -1)
    grad_out = back[:, :out_rows].T.astype(F32)
    grad_down = back[:, out_rows:lane_rows].T.astype(F32)

    first = main_a + ab_cols
    small = in_left[:, first : first + small_count].astype(F32) + in_right[:, first : first + small_count].astype(F32)
    small = small.T
    tail = small[small_count - 1]
    conv_at = 2 + 2 * taps
    head_grads = tail[gain_rows : gain_rows + 2 * all_heads].reshape(2, all_heads)
    edges = unordered(choose(input_grad, block_out)).reshape(1, micro, 1, length, width)
    return (
        edges,
        small[0][None],
        joined(in_left, in_right, value_cols, key_cols),
        joined(in_left, in_right, gate_first + value_cols, key_cols),
        joined(in_left, in_right, 0, value_cols),
        joined(in_left, in_right, gate_first, value_cols),
        joined(in_left, in_right, main_a, heads),
        joined(in_left, in_right, main_a + heads, heads),
        head_grads[0:1],
        head_grads[1:2],
        small[2 : 2 + taps][None],
        small[2 + taps : 2 + 2 * taps][None],
        small[conv_at : conv_at + taps * value_split].reshape(1, taps, value_split * rows),
        tail[:gain_rows][None],
        grad_out[None],
        small[1][None],
        joined(ffn_left, ffn_right, 0, ffn_cols),
        joined(ffn_left, ffn_right, up_first, ffn_cols),
        grad_down[None],
    )


def solution(mesh):
    across = P("section", "fsdp", None)
    lanes = P("section", None, "fsdp")
    vector = P("section", "fsdp")
    rates = P("section", None)
    tokens = P(None, ("rep", "fsdp"), None, None)
    placed = (
        (tokens, tokens, vector)
        + (across,) * 6
        + (rates, rates, lanes, lanes, lanes, vector, across, vector, across, across, across)
    )
    return jax.shard_map(
        per_device,
        mesh=mesh,
        in_specs=placed,
        out_specs=(P("section", None, ("rep", "fsdp"), None, None), vector)
        + (across,) * 6
        + (rates, rates, lanes, lanes, lanes, vector, across, vector, across, across, across),
        check_vma=False,
    )
```

time: 2030 us -> 948 us (0.47)
  waiting for transfers between devices: 950 us -> 300 us
  other arithmetic: 437 us -> 64.6 us
  starting transfers between devices: 16.6 us -> 216 us
  blocking collectives: 144 us -> 0 us
  local copies, waits for them, and re-layouts: 258 us -> 142 us
  Pallas kernels: 0 us -> 73.1 us
  matrix products: 186 us -> 134 us
  loops' own time: 21.7 us -> 0 us
    another operation x18 -> x5, other arithmetic: 330 us -> 3.33 us  [the longest x10 326 us: advance(): lax.linalg.triangular_solve(system, target, left_side=True, lower=True, u...]
    reduce_scatter x4 -> x0, waiting for transfers between devices: 284 us -> none  [the longest x2 124 us: sent_together_2(): filled = lax.psum_scatter(both, axis, scatter_dimension=dim, tiled=True)]
    ppermute x4 -> x157, starting transfers between devices: 7.69 us -> 202 us  [the longest x128 167 us: move(): return lax.ppermute(value, self.name, self.pairs(by))]
    all_gather x4 -> x0, waiting for transfers between devices: 173 us -> none  [the longest x2 76.4 us: sent_together(): lax.all_gather(both, axis, axis=dim, tiled=True)]
    unnamed x13 -> x0, waiting for transfers between devices: 97 us -> none
    pallas_call x0 -> x4, Pallas kernels: none -> 73.1 us  [the longest x2 42 us: mixer_forward(): pl.pallas_call(functools.partial(mixer_forward_kernel, heads, length), gr...]
    ppermute x4 -> x157, waiting for transfers between devices: 358 us -> 288 us  [the longest x128 261 us: move(): return lax.ppermute(value, self.name, self.pairs(by))]
    unnamed x109 -> x505, local copies, waits for them, and re-layouts: 8.62 us -> 55.8 us
  transfers between devices with their start and end apart: 16 -> 159, of which waited for: 14 -> 56; matrix products, arithmetic and copies ran while one was open for 6% -> 33% of each run, Pallas kernels for 0% -> 8%
where the time goes in v1:
time: 948 us; the launch traced here: 935 us
  waiting for transfers between devices  300 us (32%)
  starting transfers between devices  216 us (23%)
  local copies, waits for them, and re-layouts  142 us (15%)
  matrix products  134 us (14%)
  Pallas kernels  73.1 us (8%)
  other arithmetic  64.6 us (7%)
    ppermute x128, waiting for transfers between devices, move(): return lax.ppermute(value, self.name, self.pairs(by))  261 us
    ppermute x128, starting transfers between devices, move(): return lax.ppermute(value, self.name, self.pairs(by))  167 us
    dot_general x64, matrix products, dot_tn(): lax.dot_general(left, right, (((0,), (0,)), ((), ())), preferred_element_...  62.3 us
    unnamed x505, local copies, waits for them, and re-layouts  55.8 us
    pallas_call x2, Pallas kernels, mixer_forward(): pl.pallas_call(functools.partial(mixer_forward_kernel, heads, length), gr...  42 us
    dot_general x26, matrix products, dot(): return jnp.dot(left, right, preferred_element_type=F32)  39.2 us
    ppermute x16, starting transfers between devices, rep_sum(): part = added(part, lax.ppermute(part, 'rep', pairs))  32.5 us
    pallas_call x2, Pallas kernels, mixer_backward(): pl.pallas_call(functools.partial(mixer_backward_kernel, heads, length), g...  31.1 us
  transfers between devices with their start and end apart: 159, of which 56 were waited for; matrix products, arithmetic and copies ran while one was open for 33% of the time, Pallas kernels for 8%

profile of v1, /device:TPU:0, one launch (start us, length us, event | category | flops | bytes accessed | tf_op | source)
XLA Modules:
  0.0 935.5 jit_solution(1748333458375387314)
XLA Ops:
  13.6 8.0 all-to-all-start
  40.2 4.8 collective-permute-done.10
  45.1 3.3 collective-permute-start.12
  71.6 5.8 collective-permute-done.14
  78.5 12.0 %collective-permute-start.15 = (bf16[128,1536]{1,0:T(8,128)(2,1)S(1)}, bf16[128,1536]{1,0:T(8,128)(2,1)S(1)}, u32[]{:S(2)}, u32[]{:S(2)}) collective-permute-start(bf16[128,1536]{1,0:T(8,128)(2,1)S(1)} %slice.1921), channel_id=1, source_target_pairs={{0,1},{1,2},{2,3},{3,0},{4,5},{5,6},{6,7},{7,4},{8,9},{9,10},{10,1... | collective-permute-start | bytes 1179656 | tf_op jit(solution)/shard_map/ppermute | solution.py:474
  91.6 3.3 collective-permute-start.16
  108.7 3.3 collective-permute-start.8
  113.5 3.2 collective-permute-start.31
  118.2 3.2 collective-permute-start.22
  131.5 21.1 %mixer_forward.2 = (bf16[256,1024]{1,0:T(8,128)(2,1)}, f32[4,2,128,128]{3,2,1,0:T(8,128)}) custom-call(f32[256,1664]{1,0:T(8,128)} %fusion.407.query_ref.value_ref.ab_ref, f32[256,1536]{1,0:T(8,128)} %fusion.408.key_ref.gate_ref, f32[256,1664]{1,0:T(8,128)} %fusion.407.query_ref.value_ref.ab_ref, f32[256,1536]{1,0:T(8,128)} %fusion.408.key_ref.gate_ref, ...), custom_call_target="tpu_custom_call" | custom-call | tf_op jit(solution)/shard_map/mixer_forward/pallas_call | solution.py:387
  164.1 20.1 %collective-permute-done.33 = bf16[256,2560]{1,0:T(8,128)(2,1)S(1)} collective-permute-done((bf16[256,2560]{1,0:T(8,128)(2,1)}, bf16[256,2560]{1,0:T(8,128)(2,1)S(1)}, u32[]{:S(2)}, u32[]{:S(2)}) %collective-permute-start.33) | collective-permute-done | bytes 1310752 | tf_op jit(solution)/shard_map/ppermute | solution.py:474
  193.6 4.9 collective-permute-done.46
  198.9 6.7 collective-permute-done.38
  205.6 6.2 collective-permute-done.47
  211.9 5.7 collective-permute-done.48
  217.6 7.1 collective-permute-done.39
  225.6 3.8 collective-permute-done.40
  237.8 9.4 %collective-permute-done.50 = bf16[256,1536]{1,0:T(8,128)(2,1)S(1)} collective-permute-done((bf16[256,1536]{1,0:T(8,128)(2,1)S(1)}, bf16[256,1536]{1,0:T(8,128)(2,1)S(1)}, u32[]{:S(2)}, u32[]{:S(2)}) %collective-permute-start.50) | collective-permute-done | bytes 786464 | tf_op jit(solution)/shard_map/ppermute | solution.py:474
  247.4 3.3 collective-permute-start.52
  254.7 4.9 collective-permute-done.51
  269.0 3.2 collective-permute-start.65
  293.8 4.5 multiply_convert_fusion.5
  314.0 20.9 %mixer_forward.3 = (bf16[256,1024]{1,0:T(8,128)(2,1)}, f32[4,2,128,128]{3,2,1,0:T(8,128)}) custom-call(f32[256,1664]{1,0:T(8,128)} %fusion.409.query_ref.value_ref.ab_ref, f32[256,1536]{1,0:T(8,128)} %fusion.410.key_ref.gate_ref, f32[256,1664]{1,0:T(8,128)} %fusion.409.query_ref.value_ref.ab_ref, f32[256,1536]{1,0:T(8,128)} %fusion.410.key_ref.gate_ref, ...), custom_call_target="tpu_custom_call" | custom-call | tf_op jit(solution)/shard_map/mixer_forward/pallas_call | solution.py:387
  353.1 3.2 collective-permute-done.68
  380.8 3.7 collective-permute-start.146
  404.0 15.4 %mixer_backward.2 = (bf16[256,1664]{1,0:T(8,128)(2,1)}, bf16[256,1536]{1,0:T(8,128)(2,1)}, f32[8,512]{1,0:T(8,128)}, f32[8,512]{1,0:T(8,128)}, f32[8,1024]{1,0:T...) custom-call(f32[256,1664]{1,0:T(8,128)} %fusion.409.query_ref.value_ref.ab_ref, f32[256,1536]{1,0:T(8,128)} %fusion.410.key_ref.gate_ref, ...), custom_call_target="tpu_custom_call" | custom-call | tf_op jit(solution)/shard_map/mixer_backward/pallas_call | solution.py:411
  429.9 3.4 collective-permute-start.105
  460.1 9.7 %collective-permute-done.145 = bf16[128,2560]{1,0:T(8,128)(2,1)} collective-permute-done((bf16[128,2560]{1,0:T(8,128)(2,1)}, bf16[128,2560]{1,0:T(8,128)(2,1)}, u32[]{:S(2)}, u32[]{:S(2)}) %collective-permute-start.145) | collective-permute-done | bytes 655392 | tf_op jit(solution)/shard_map/ppermute | solution.py:474
  472.0 3.2 collective-permute-start.106
  505.6 3.5 collective-permute-done.109
  516.3 5.0 collective-permute-done.108
  527.4 17.6 %collective-permute-done.150 = bf16[64,2560]{1,0:T(8,128)(2,1)S(1)} collective-permute-done((bf16[64,2560]{1,0:T(8,128)(2,1)S(1)}, bf16[64,2560]{1,0:T(8,128)(2,1)S(1)}, u32[]{:S(2)}, u32[]{:S(2)}) %collective-permute-start.150) | collective-permute-done | bytes 327712 | tf_op jit(solution)/shard_map/ppermute | solution.py:474
  546.2 3.2 collective-permute-start.151
  551.6 3.5 collective-permute-done.148
  566.2 15.7 %mixer_backward.3 = (bf16[256,1664]{1,0:T(8,128)(2,1)}, bf16[256,1536]{1,0:T(8,128)(2,1)}, f32[8,512]{1,0:T(8,128)}, f32[8,512]{1,0:T(8,128)}, f32[8,1024]{1,0:T...) custom-call(f32[256,1664]{1,0:T(8,128)} %fusion.407.query_ref.value_ref.ab_ref, f32[256,1536]{1,0:T(8,128)} %fusion.408.key_ref.gate_ref, ...), custom_call_target="tpu_custom_call" | custom-call | tf_op jit(solution)/shard_map/mixer_backward/pallas_call | solution.py:411
  611.3 4.4 convolution_add_fusion.2
  631.8 5.5 collective-permute-done.149
  637.2 3.2 collective-permute-start.143
  641.6 3.7 collective-permute-done.143
  649.7 17.5 %collective-permute-done.141 = bf16[32,2688]{1,0:T(8,128)(2,1)S(1)} collective-permute-done((bf16[32,2688]{1,0:T(8,128)(2,1)S(1)}, bf16[32,2688]{1,0:T(8,128)(2,1)S(1)}, u32[]{:S(2)}, u32[]{:S(2)}) %collective-permute-start.141) | collective-permute-done | bytes 172064 | tf_op jit(solution)/shard_map/ppermute | solution.py:474
  672.3 6.6 collective-permute-done.125
  683.8 3.5 collective-permute-done.154
  687.5 3.3 collective-permute-start.86
  710.5 5.0 collective-permute-done.153
  717.6 19.6 %collective-permute-done.89 = bf16[64,1536]{1,0:T(8,128)(2,1)S(1)} collective-permute-done((bf16[64,1536]{1,0:T(8,128)(2,1)S(1)}, bf16[64,1536]{1,0:T(8,128)(2,1)S(1)}, u32[]{:S(2)}, u32[]{:S(2)}) %collective-permute-start.89) | collective-permute-done | bytes 196640 | tf_op jit(solution)/shard_map/ppermute | solution.py:474
  737.4 3.3 collective-permute-start.90
  741.0 18.5 %collective-permute-done.87 = bf16[64,1536]{1,0:T(8,128)(2,1)S(1)} collective-permute-done((bf16[64,1536]{1,0:T(8,128)(2,1)S(1)}, bf16[64,1536]{1,0:T(8,128)(2,1)S(1)}, u32[]{:S(2)}, u32[]{:S(2)}) %collective-permute-start.87) | collective-permute-done | bytes 196640 | tf_op jit(solution)/shard_map/ppermute | solution.py:474
  763.1 19.1 %collective-permute-done.88 = bf16[32,1536]{1,0:T(8,128)(2,1)S(1)} collective-permute-done((bf16[32,1536]{1,0:T(8,128)(2,1)S(1)}, bf16[32,1536]{1,0:T(8,128)(2,1)S(1)}, u32[]{:S(2)}, u32[]{:S(2)}) %collective-permute-start.88) | collective-permute-done | bytes 98336 | tf_op jit(solution)/shard_map/ppermute | solution.py:474
  782.3 3.3 collective-permute-start.130
  785.7 4.5 collective-permute-done.130
  790.2 3.8 collective-permute-start.131
  794.1 9.3 collective-permute-done.128
  805.6 8.7 collective-permute-done.119
  815.1 5.9 collective-permute-done.129
  825.0 3.9 collective-permute-done.122
  835.1 3.4 collective-permute-start.121
  842.9 3.2 collective-permute-start.101
  847.6 13.9 %collective-permute-start.134 = (bf16[32,5248]{1,0:T(8,128)(2,1)S(1)}, bf16[32,5248]{1,0:T(8,128)(2,1)S(1)}, u32[]{:S(2)}, u32[]{:S(2)}) collective-permute-start(bf16[32,5248]{1,0:T(8,128)(2,1)S(1)} %get-tuple-element.188), channel_id=1, source_target_pairs={{0,48},{48,0},{16,32},{32,16},{1,49},{49,1},{17,33},{33,17},{2,50}... | collective-permute-start | bytes 1007624 | tf_op jit(solution)/shard_map/ppermute | solution.py:582
  863.0 3.3 collective-permute-done.82
  876.7 5.1 collective-permute-done.91
  885.2 3.5 collective-permute-done.113
  891.1 4.8 collective-permute-done.112
  912.6 5.7 all-to-all-start.1
  921.2 11.7 %all-to-all-done.1 = bf16[16,64,384]{2,1,0:T(8,128)(2,1)S(1)} async-done(((bf16[16,64,384]{2,1,0:T(8,128)(2,1)}), bf16[16,64,384]{2,1,0:T(8,128)(2,1)S(1)}, u32[]{:S(2)}, u32[]{:S(2)}) %all-to-all-start.1) | async-done | bytes 786464 | tf_op jit(solution)/shard_map/all_to_all | solution.py:888
  (1225 shorter events, 466.5 us)
Async XLA Ops:
  13.6 45.5 %all-to-all-start = ((bf16[16,64,384]{2,1,0:T(8,128)(2,1)}), bf16[16,64,384]{2,1,0:T(8,128)(2,1)}, u32[]{:S(2)}, u32[]{:S(2)}) async-start(bf16[16,64,384]{2,1,0:T(8,128)(2,1)} %bitcast.28), calls=%async_computation | async-start | bytes 1572864 | tf_op jit(solution)/shard_map/all_to_all | solution.py:675
  57.0 33.5 %collective-permute-start.13 = (bf16[256,1536]{1,0:T(8,128)(2,1)}, bf16[256,1536]{1,0:T(8,128)(2,1)}, u32[]{:S(2)}, u32[]{:S(2)}) collective-permute-start(bf16[256,1536]{1,0:T(8,128)(2,1)} %constant_dynamic-update-slice_fusion.14), channel_id=1, source_target_pairs={{0,3},{1,0},{2,1},{3,2},{4,7},{5,4},{6,5},{7,6},{8,11},{9,8},{10,9... | collective-permute-start | bytes 2359304 | tf_op jit(solution)/shard_map/ppermute | solution.py:474
  68.2 27.6 %collective-permute-start.5 = (bf16[256,1664]{1,0:T(8,128)(2,1)S(1)}, bf16[256,1664]{1,0:T(8,128)(2,1)S(1)}, u32[]{:S(2)}, u32[]{:S(2)}) collective-permute-start(bf16[256,1664]{1,0:T(8,128)(2,1)S(1)} %get-tuple-element.335), channel_id=1, source_target_pairs={{0,12},{1,13},{2,14},{3,15},{4,0},{5,1},{6,2},{7,3},{8,4},{9,5},{1... | collective-permute-start | bytes 2555912 | tf_op jit(solution)/shard_map/ppermute | solution.py:474
  70.6 28.9 %collective-permute-start.6 = (bf16[256,1664]{1,0:T(8,128)(2,1)S(1)}, bf16[256,1664]{1,0:T(8,128)(2,1)S(1)}, u32[]{:S(2)}, u32[]{:S(2)}) collective-permute-start(bf16[256,1664]{1,0:T(8,128)(2,1)S(1)} %get-tuple-element.335), channel_id=1, source_target_pairs={{0,4},{1,5},{2,6},{3,7},{4,8},{5,9},{6,10},{7,11},{8,12},{9,13},{1... | collective-permute-start | bytes 2555912 | tf_op jit(solution)/shard_map/ppermute | solution.py:474
  78.5 21.3 %collective-permute-start.15 = (bf16[128,1536]{1,0:T(8,128)(2,1)S(1)}, bf16[128,1536]{1,0:T(8,128)(2,1)S(1)}, u32[]{:S(2)}, u32[]{:S(2)}) collective-permute-start(bf16[128,1536]{1,0:T(8,128)(2,1)S(1)} %slice.1921), channel_id=1, source_target_pairs={{0,1},{1,2},{2,3},{3,0},{4,5},{5,6},{6,7},{7,4},{8,9},{9,10},{10,1... | collective-permute-start | bytes 1179656 | tf_op jit(solution)/shard_map/ppermute | solution.py:474
  112.7 39.8 %collective-permute-start.30 = (bf16[32,2560]{1,0:T(8,128)(2,1)}, bf16[32,2560]{1,0:T(8,128)(2,1)S(1)}, u32[]{:S(2)}, u32[]{:S(2)}) collective-permute-start(bf16[32,2560]{1,0:T(8,128)(2,1)} %slice.1962), channel_id=1, source_target_pairs={{0,4},{1,5},{2,6},{3,7},{4,8},{5,9},{6,10},{7,11},{8,12},{9,13},{1... | collective-permute-start | bytes 491528 | tf_op jit(solution)/shard_map/ppermute | solution.py:474
  113.5 39.8 %collective-permute-start.31 = (bf16[32,2560]{1,0:T(8,128)(2,1)}, bf16[32,2560]{1,0:T(8,128)(2,1)S(1)}, u32[]{:S(2)}, u32[]{:S(2)}) collective-permute-start(bf16[32,2560]{1,0:T(8,128)(2,1)} %slice.1963), channel_id=1, source_target_pairs={{0,12},{1,13},{2,14},{3,15},{4,0},{5,1},{6,2},{7,3},{8,4},{9,5},{1... | collective-permute-start | bytes 491528 | tf_op jit(solution)/shard_map/ppermute | solution.py:474
  117.4 39.3 %collective-permute-start.21 = (bf16[32,2688]{1,0:T(8,128)(2,1)}, bf16[32,2688]{1,0:T(8,128)(2,1)}, u32[]{:S(2)}, u32[]{:S(2)}) collective-permute-start(bf16[32,2688]{1,0:T(8,128)(2,1)} %slice.1955), channel_id=1, source_target_pairs={{0,1},{1,2},{2,3},{3,0},{4,5},{5,6},{6,7},{7,4},{8,9},{9,10},{10,1... | collective-permute-start | bytes 516104 | tf_op jit(solution)/shard_map/ppermute | solution.py:474
  118.2 40.1 %collective-permute-start.22 = (bf16[32,2688]{1,0:T(8,128)(2,1)S(1)}, bf16[32,2688]{1,0:T(8,128)(2,1)S(1)}, u32[]{:S(2)}, u32[]{:S(2)}) collective-permute-start(bf16[32,2688]{1,0:T(8,128)(2,1)S(1)} %slice.1956), channel_id=1, source_target_pairs={{0,3},{1,0},{2,1},{3,2},{4,7},{5,4},{6,5},{7,6},{8,11},{9,8},{10,9... | collective-permute-start | bytes 516104 | tf_op jit(solution)/shard_map/ppermute | solution.py:474
  154.6 31.2 %collective-permute-start.32 = (bf16[256,2560]{1,0:T(8,128)(2,1)}, bf16[256,2560]{1,0:T(8,128)(2,1)S(1)}, u32[]{:S(2)}, u32[]{:S(2)}) collective-permute-start(bf16[256,2560]{1,0:T(8,128)(2,1)} %constant_dynamic-update-slice_fusion.60), channel_id=1, source_target_pairs={{0,3},{1,0},{2,1},{3,2},{4,7},{5,4},{6,5},{7,6},{8,11},{9,8},{10,9... | collective-permute-start | bytes 3932168 | tf_op jit(solution)/shard_map/ppermute | solution.py:474
  155.2 29.0 %collective-permute-start.33 = (bf16[256,2560]{1,0:T(8,128)(2,1)}, bf16[256,2560]{1,0:T(8,128)(2,1)S(1)}, u32[]{:S(2)}, u32[]{:S(2)}) collective-permute-start(bf16[256,2560]{1,0:T(8,128)(2,1)} %constant_dynamic-update-slice_fusion.60), channel_id=1, source_target_pairs={{0,1},{1,2},{2,3},{3,0},{4,5},{5,6},{6,7},{7,4},{8,9},{9,10},{10,1... | collective-permute-start | bytes 3932168 | tf_op jit(solution)/shard_map/ppermute | solution.py:474
  159.7 28.0 %collective-permute-start.23 = (bf16[256,2688]{1,0:T(8,128)(2,1)S(1)}, bf16[256,2688]{1,0:T(8,128)(2,1)S(1)}, u32[]{:S(2)}, u32[]{:S(2)}) collective-permute-start(bf16[256,2688]{1,0:T(8,128)(2,1)S(1)} %get-tuple-element.321), channel_id=1, source_target_pairs={{0,12},{1,13},{2,14},{3,15},{4,0},{5,1},{6,2},{7,3},{8,4},{9,5},{1... | collective-permute-start | bytes 4128776 | tf_op jit(solution)/shard_map/ppermute | solution.py:474
  162.4 28.2 %collective-permute-start.24 = (bf16[256,2688]{1,0:T(8,128)(2,1)S(1)}, bf16[256,2688]{1,0:T(8,128)(2,1)S(1)}, u32[]{:S(2)}, u32[]{:S(2)}) collective-permute-start(bf16[256,2688]{1,0:T(8,128)(2,1)S(1)} %get-tuple-element.321), channel_id=1, source_target_pairs={{0,4},{1,5},{2,6},{3,7},{4,8},{5,9},{6,10},{7,11},{8,12},{9,13},{1... | collective-permute-start | bytes 4128776 | tf_op jit(solution)/shard_map/ppermute | solution.py:474
  184.2 47.3 %collective-permute-start.34 = (bf16[128,2560]{1,0:T(8,128)(2,1)S(1)}, bf16[128,2560]{1,0:T(8,128)(2,1)S(1)}, u32[]{:S(2)}, u32[]{:S(2)}) collective-permute-start(bf16[128,2560]{1,0:T(8,128)(2,1)S(1)} %slice.1965), channel_id=1, source_target_pairs={{0,1},{1,2},{2,3},{3,0},{4,5},{5,6},{6,7},{7,4},{8,9},{9,10},{10,1... | collective-permute-start | bytes 1966088 | tf_op jit(solution)/shard_map/ppermute | solution.py:474
  185.9 46.1 %collective-permute-start.35 = (bf16[128,2560]{1,0:T(8,128)(2,1)S(1)}, bf16[128,2560]{1,0:T(8,128)(2,1)S(1)}, u32[]{:S(2)}, u32[]{:S(2)}) collective-permute-start(bf16[128,2560]{1,0:T(8,128)(2,1)S(1)} %slice.1972), channel_id=1, source_target_pairs={{0,3},{1,0},{2,1},{3,2},{4,7},{5,4},{6,5},{7,6},{8,11},{9,8},{10,9... | collective-permute-start | bytes 1966088 | tf_op jit(solution)/shard_map/ppermute | solution.py:474
  198.6 34.9 %collective-permute-start.25 = (bf16[128,2688]{1,0:T(8,128)(2,1)S(1)}, bf16[128,2688]{1,0:T(8,128)(2,1)S(1)}, u32[]{:S(2)}, u32[]{:S(2)}) collective-permute-start(bf16[128,2688]{1,0:T(8,128)(2,1)S(1)} %slice.1957), channel_id=1, source_target_pairs={{0,4},{1,5},{2,6},{3,7},{4,8},{5,9},{6,10},{7,11},{8,12},{9,13},{1... | collective-permute-start | bytes 2064392 | tf_op jit(solution)/shard_map/ppermute | solution.py:474
  205.6 28.8 %collective-permute-start.26 = (bf16[128,2688]{1,0:T(8,128)(2,1)S(1)}, bf16[128,2688]{1,0:T(8,128)(2,1)S(1)}, u32[]{:S(2)}, u32[]{:S(2)}) collective-permute-start(bf16[128,2688]{1,0:T(8,128)(2,1)S(1)} %slice.1958), channel_id=1, source_target_pairs={{0,12},{1,13},{2,14},{3,15},{4,0},{5,1},{6,2},{7,3},{8,4},{9,5},{1... | collective-permute-start | bytes 2064392 | tf_op jit(solution)/shard_map/ppermute | solution.py:474
  237.8 51.0 %collective-permute-start.27 = (f32[256,1024]{0,1:T(8,128)}, f32[256,1024]{0,1:T(8,128)}, u32[]{:S(2)}, u32[]{:S(2)}) collective-permute-start(f32[256,1024]{0,1:T(8,128)} %fusion.74), channel_id=1, source_target_pairs={{0,64},{64,0},{1,65},{65,1},{2,66},{66,2},{3,67},{67,3},{4,68},{68... | collective-permute-start | bytes 3145736 | tf_op jit(solution)/shard_map/ppermute | solution.py:444
  284.2 55.6 %collective-permute-start.66 = (bf16[256,2560]{1,0:T(8,128)(2,1)}, bf16[256,2560]{1,0:T(8,128)(2,1)}, u32[]{:S(2)}, u32[]{:S(2)}) collective-permute-start(bf16[256,2560]{1,0:T(8,128)(2,1)} %constant_dynamic-update-slice_fusion.120), channel_id=1, source_target_pairs={{0,3},{1,0},{2,1},{3,2},{4,7},{5,4},{6,5},{7,6},{8,11},{9,8},{10,9... | collective-permute-start | bytes 3932168 | tf_op jit(solution)/shard_map/ppermute | solution.py:474
  284.3 53.1 %collective-permute-start.67 = (bf16[256,2560]{1,0:T(8,128)(2,1)}, bf16[256,2560]{1,0:T(8,128)(2,1)}, u32[]{:S(2)}, u32[]{:S(2)}) collective-permute-start(bf16[256,2560]{1,0:T(8,128)(2,1)} %constant_dynamic-update-slice_fusion.120), channel_id=1, source_target_pairs={{0,1},{1,2},{2,3},{3,0},{4,5},{5,6},{6,7},{7,4},{8,9},{9,10},{10,1... | collective-permute-start | bytes 3932168 | tf_op jit(solution)/shard_map/ppermute | solution.py:474
  303.6 42.6 %collective-permute-start.57 = (bf16[256,2688]{1,0:T(8,128)(2,1)}, bf16[256,2688]{1,0:T(8,128)(2,1)}, u32[]{:S(2)}, u32[]{:S(2)}) collective-permute-start(bf16[256,2688]{1,0:T(8,128)(2,1)} %get-tuple-element.317), channel_id=1, source_target_pairs={{0,12},{1,13},{2,14},{3,15},{4,0},{5,1},{6,2},{7,3},{8,4},{9,5},{1... | collective-permute-start | bytes 4128776 | tf_op jit(solution)/shard_map/ppermute | solution.py:474
  303.7 41.1 %collective-permute-start.58 = (bf16[256,2688]{1,0:T(8,128)(2,1)}, bf16[256,2688]{1,0:T(8,128)(2,1)}, u32[]{:S(2)}, u32[]{:S(2)}) collective-permute-start(bf16[256,2688]{1,0:T(8,128)(2,1)} %get-tuple-element.317), channel_id=1, source_target_pairs={{0,4},{1,5},{2,6},{3,7},{4,8},{5,9},{6,10},{7,11},{8,12},{9,13},{1... | collective-permute-start | bytes 4128776 | tf_op jit(solution)/shard_map/ppermute | solution.py:474
  341.0 20.1 %collective-permute-start.69 = (bf16[128,2560]{1,0:T(8,128)(2,1)S(1)}, bf16[128,2560]{1,0:T(8,128)(2,1)S(1)}, u32[]{:S(2)}, u32[]{:S(2)}) collective-permute-start(bf16[128,2560]{1,0:T(8,128)(2,1)S(1)} %slice.2030), channel_id=1, source_target_pairs={{0,3},{1,0},{2,1},{3,2},{4,7},{5,4},{6,5},{7,6},{8,11},{9,8},{10,9... | collective-permute-start | bytes 1966088 | tf_op jit(solution)/shard_map/ppermute | solution.py:474
  380.8 77.5 %collective-permute-start.146 = (bf16[256,2560]{1,0:T(8,128)(2,1)}, bf16[256,2560]{1,0:T(8,128)(2,1)}, u32[]{:S(2)}, u32[]{:S(2)}) collective-permute-start(bf16[256,2560]{1,0:T(8,128)(2,1)} %pad_maximum_fusion.13), channel_id=1, source_target_pairs={{0,12},{1,13},{2,14},{3,15},{4,0},{5,1},{6,2},{7,3},{8,4},{9,5},{1... | collective-permute-start | bytes 3932168 | tf_op jit(solution)/shard_map/ppermute | solution.py:474
  386.4 60.1 %collective-permute-start.144 = (bf16[256,2560]{1,0:T(8,128)(2,1)}, bf16[256,2560]{1,0:T(8,128)(2,1)}, u32[]{:S(2)}, u32[]{:S(2)}) collective-permute-start(bf16[256,2560]{1,0:T(8,128)(2,1)} %pad_maximum_fusion.12), channel_id=1, source_target_pairs={{0,4},{1,5},{2,6},{3,7},{4,8},{5,9},{6,10},{7,11},{8,12},{9,13},{1... | collective-permute-start | bytes 3932168 | tf_op jit(solution)/shard_map/ppermute | solution.py:474
  387.8 308.1 %collective-permute-start.74 = (f32[256,1024]{0,1:T(8,128)}, f32[256,1024]{0,1:T(8,128)}, u32[]{:S(2)}, u32[]{:S(2)}) collective-permute-start(f32[256,1024]{0,1:T(8,128)} %convolution_add_fusion), channel_id=1, source_target_pairs={{0,64},{64,0},{1,65},{65,1},{2,66},{66,2},{3,67},{67,3},{4,68},{68... | collective-permute-start | bytes 3145736 | tf_op jit(solution)/shard_map/ppermute | solution.py:444
  429.9 24.9 %collective-permute-start.105 = (bf16[256,1536]{1,0:T(8,128)(2,1)}, bf16[256,1536]{1,0:T(8,128)(2,1)}, u32[]{:S(2)}, u32[]{:S(2)}) collective-permute-start(bf16[256,1536]{1,0:T(8,128)(2,1)} %convolution_convert_fusion), channel_id=1, source_target_pairs={{0,12},{1,13},{2,14},{3,15},{4,0},{5,1},{6,2},{7,3},{8,4},{9,5},{1... | collective-permute-start | bytes 2359304 | tf_op jit(solution)/shard_map/ppermute | solution.py:474
  434.6 21.9 %collective-permute-start.103 = (bf16[256,1536]{1,0:T(8,128)(2,1)}, bf16[256,1536]{1,0:T(8,128)(2,1)}, u32[]{:S(2)}, u32[]{:S(2)}) collective-permute-start(bf16[256,1536]{1,0:T(8,128)(2,1)} %convolution_convert_fusion.1), channel_id=1, source_target_pairs={{0,4},{1,5},{2,6},{3,7},{4,8},{5,9},{6,10},{7,11},{8,12},{9,13},{1... | collective-permute-start | bytes 2359304 | tf_op jit(solution)/shard_map/ppermute | solution.py:474
  448.6 21.1 %collective-permute-start.145 = (bf16[128,2560]{1,0:T(8,128)(2,1)}, bf16[128,2560]{1,0:T(8,128)(2,1)}, u32[]{:S(2)}, u32[]{:S(2)}) collective-permute-start(bf16[128,2560]{1,0:T(8,128)(2,1)} %add_convert_fusion.11), channel_id=1, source_target_pairs={{0,4},{1,5},{2,6},{3,7},{4,8},{5,9},{6,10},{7,11},{8,12},{9,13},{1... | collective-permute-start | bytes 1966088 | tf_op jit(solution)/shard_map/ppermute | solution.py:474
  456.5 58.1 %collective-permute-start.138 = (bf16[256,2688]{1,0:T(8,128)(2,1)}, bf16[256,2688]{1,0:T(8,128)(2,1)S(1)}, u32[]{:S(2)}, u32[]{:S(2)}) collective-permute-start(bf16[256,2688]{1,0:T(8,128)(2,1)} %pad_maximum_fusion.9), channel_id=1, source_target_pairs={{0,3},{1,0},{2,1},{3,2},{4,7},{5,4},{6,5},{7,6},{8,11},{9,8},{10,9... | collective-permute-start | bytes 4128776 | tf_op jit(solution)/shard_map/ppermute | solution.py:474
  458.3 56.2 %collective-permute-start.136 = (bf16[256,2688]{1,0:T(8,128)(2,1)}, bf16[256,2688]{1,0:T(8,128)(2,1)S(1)}, u32[]{:S(2)}, u32[]{:S(2)}) collective-permute-start(bf16[256,2688]{1,0:T(8,128)(2,1)} %pad_maximum_fusion.8), channel_id=1, source_target_pairs={{0,1},{1,2},{2,3},{3,0},{4,5},{5,6},{6,7},{7,4},{8,9},{9,10},{10,1... | collective-permute-start | bytes 4128776 | tf_op jit(solution)/shard_map/ppermute | solution.py:474
  469.8 32.0 %collective-permute-start.104 = (bf16[128,1536]{1,0:T(8,128)(2,1)S(1)}, bf16[128,1536]{1,0:T(8,128)(2,1)S(1)}, u32[]{:S(2)}, u32[]{:S(2)}) collective-permute-start(bf16[128,1536]{1,0:T(8,128)(2,1)S(1)} %get-tuple-element.179), channel_id=1, source_target_pairs={{0,4},{1,5},{2,6},{3,7},{4,8},{5,9},{6,10},{7,11},{8,12},{9,13},{1... | collective-permute-start | bytes 1179656 | tf_op jit(solution)/shard_map/ppermute | solution.py:474
  472.0 29.8 %collective-permute-start.106 = (bf16[128,1536]{1,0:T(8,128)(2,1)S(1)}, bf16[128,1536]{1,0:T(8,128)(2,1)S(1)}, u32[]{:S(2)}, u32[]{:S(2)}) collective-permute-start(bf16[128,1536]{1,0:T(8,128)(2,1)S(1)} %get-tuple-element.180), channel_id=1, source_target_pairs={{0,12},{1,13},{2,14},{3,15},{4,0},{5,1},{6,2},{7,3},{8,4},{9,5},{1... | collective-permute-start | bytes 1179656 | tf_op jit(solution)/shard_map/ppermute | solution.py:474
  513.9 45.3 %collective-permute-start.72 = (f32[256,1024]{0,1:T(8,128)S(1)}, f32[256,1024]{0,1:T(8,128)S(1)}, u32[]{:S(2)}, u32[]{:S(2)}) collective-permute-start(f32[256,1024]{0,1:T(8,128)S(1)} %fusion.92), channel_id=1, source_target_pairs={{0,64},{64,0},{1,65},{65,1},{2,66},{66,2},{3,67},{67,3},{4,68},{68... | collective-permute-start | bytes 3145736 | tf_op jit(solution)/shard_map/ppermute | solution.py:444
  515.0 31.1 %collective-permute-start.137 = (bf16[128,2688]{1,0:T(8,128)(2,1)S(1)}, bf16[128,2688]{1,0:T(8,128)(2,1)S(1)}, u32[]{:S(2)}, u32[]{:S(2)}) collective-permute-start(bf16[128,2688]{1,0:T(8,128)(2,1)S(1)} %get-tuple-element.151), channel_id=1, source_target_pairs={{0,1},{1,2},{2,3},{3,0},{4,5},{5,6},{6,7},{7,4},{8,9},{9,10},{10,1... | collective-permute-start | bytes 2064392 | tf_op jit(solution)/shard_map/ppermute | solution.py:474
  521.4 24.8 %collective-permute-start.139 = (bf16[128,2688]{1,0:T(8,128)(2,1)S(1)}, bf16[128,2688]{1,0:T(8,128)(2,1)S(1)}, u32[]{:S(2)}, u32[]{:S(2)}) collective-permute-start(bf16[128,2688]{1,0:T(8,128)(2,1)S(1)} %get-tuple-element.152), channel_id=1, source_target_pairs={{0,3},{1,0},{2,1},{3,2},{4,7},{5,4},{6,5},{7,6},{8,11},{9,8},{10,9... | collective-permute-start | bytes 2064392 | tf_op jit(solution)/shard_map/ppermute | solution.py:474
  545.1 125.6 %collective-permute-start.126 = (bf16[256,2560]{1,0:T(8,128)(2,1)}, bf16[256,2560]{1,0:T(8,128)(2,1)}, u32[]{:S(2)}, u32[]{:S(2)}) collective-permute-start(bf16[256,2560]{1,0:T(8,128)(2,1)} %pad_maximum_fusion.11), channel_id=1, source_target_pairs={{0,12},{1,13},{2,14},{3,15},{4,0},{5,1},{6,2},{7,3},{8,4},{9,5},{1... | collective-permute-start | bytes 3932168 | tf_op jit(solution)/shard_map/ppermute | solution.py:474
  555.1 91.3 %collective-permute-start.124 = (bf16[256,2560]{1,0:T(8,128)(2,1)}, bf16[256,2560]{1,0:T(8,128)(2,1)}, u32[]{:S(2)}, u32[]{:S(2)}) collective-permute-start(bf16[256,2560]{1,0:T(8,128)(2,1)} %pad_maximum_fusion.10), channel_id=1, source_target_pairs={{0,4},{1,5},{2,6},{3,7},{4,8},{5,9},{6,10},{7,11},{8,12},{9,13},{1... | collective-permute-start | bytes 3932168 | tf_op jit(solution)/shard_map/ppermute | solution.py:474
  556.2 74.2 %collective-permute-start.142 = (bf16[64,2688]{1,0:T(8,128)(2,1)}, bf16[64,2688]{1,0:T(8,128)(2,1)}, u32[]{:S(2)}, u32[]{:S(2)}) collective-permute-start(bf16[64,2688]{1,0:T(8,128)(2,1)} %concatenate.789), channel_id=1, source_target_pairs={{0,12},{1,13},{2,14},{3,15},{4,0},{5,1},{6,2},{7,3},{8,4},{9,5},{1... | collective-permute-start | bytes 1032200 | tf_op jit(solution)/shard_map/ppermute | solution.py:474
  559.2 82.3 %collective-permute-start.140 = (bf16[64,2688]{1,0:T(8,128)(2,1)}, bf16[64,2688]{1,0:T(8,128)(2,1)}, u32[]{:S(2)}, u32[]{:S(2)}) collective-permute-start(bf16[64,2688]{1,0:T(8,128)(2,1)} %pad_maximum_fusion.32), channel_id=1, source_target_pairs={{0,4},{1,5},{2,6},{3,7},{4,8},{5,9},{6,10},{7,11},{8,12},{9,13},{1... | collective-permute-start | bytes 1032200 | tf_op jit(solution)/shard_map/ppermute | solution.py:474
  641.5 26.8 %collective-permute-start.85 = (bf16[256,1536]{1,0:T(8,128)(2,1)S(1)}, bf16[256,1536]{1,0:T(8,128)(2,1)S(1)}, u32[]{:S(2)}, u32[]{:S(2)}) collective-permute-start(bf16[256,1536]{1,0:T(8,128)(2,1)S(1)} %copy-done.87), channel_id=1, source_target_pairs={{0,12},{1,13},{2,14},{3,15},{4,0},{5,1},{6,2},{7,3},{8,4},{9,5},{1... | collective-permute-start | bytes 2359304 | tf_op jit(solution)/shard_map/ppermute | solution.py:474
  645.3 23.3 %collective-permute-start.83 = (bf16[256,1536]{1,0:T(8,128)(2,1)S(1)}, bf16[256,1536]{1,0:T(8,128)(2,1)S(1)}, u32[]{:S(2)}, u32[]{:S(2)}) collective-permute-start(bf16[256,1536]{1,0:T(8,128)(2,1)S(1)} %convolution_convert_fusion.9), channel_id=1, source_target_pairs={{0,4},{1,5},{2,6},{3,7},{4,8},{5,9},{6,10},{7,11},{8,12},{9,13},{1... | collective-permute-start | bytes 2359304 | tf_op jit(solution)/shard_map/ppermute | solution.py:474
  646.5 20.7 %collective-permute-start.141 = (bf16[32,2688]{1,0:T(8,128)(2,1)S(1)}, bf16[32,2688]{1,0:T(8,128)(2,1)S(1)}, u32[]{:S(2)}, u32[]{:S(2)}) collective-permute-start(bf16[32,2688]{1,0:T(8,128)(2,1)S(1)} %get-tuple-element.163), channel_id=1, source_target_pairs={{0,4},{1,5},{2,6},{3,7},{4,8},{5,9},{6,10},{7,11},{8,12},{9,13},{1... | collective-permute-start | bytes 516104 | tf_op jit(solution)/shard_map/ppermute | solution.py:474
  668.3 69.0 %collective-permute-start.118 = (bf16[256,2688]{1,0:T(8,128)(2,1)S(1)}, bf16[256,2688]{1,0:T(8,128)(2,1)S(1)}, u32[]{:S(2)}, u32[]{:S(2)}) collective-permute-start(bf16[256,2688]{1,0:T(8,128)(2,1)S(1)} %pad_maximum_fusion.5), channel_id=1, source_target_pairs={{0,3},{1,0},{2,1},{3,2},{4,7},{5,4},{6,5},{7,6},{8,11},{9,8},{10,9... | collective-permute-start | bytes 4128776 | tf_op jit(solution)/shard_map/ppermute | solution.py:474
  668.6 68.7 %collective-permute-start.116 = (bf16[256,2688]{1,0:T(8,128)(2,1)S(1)}, bf16[256,2688]{1,0:T(8,128)(2,1)S(1)}, u32[]{:S(2)}, u32[]{:S(2)}) collective-permute-start(bf16[256,2688]{1,0:T(8,128)(2,1)S(1)} %pad_maximum_fusion.4), channel_id=1, source_target_pairs={{0,1},{1,2},{2,3},{3,0},{4,5},{5,6},{6,7},{7,4},{8,9},{9,10},{10,1... | collective-permute-start | bytes 4128776 | tf_op jit(solution)/shard_map/ppermute | solution.py:474
  687.3 19.8 %collective-permute-start.84 = (bf16[128,1536]{1,0:T(8,128)(2,1)S(1)}, bf16[128,1536]{1,0:T(8,128)(2,1)S(1)}, u32[]{:S(2)}, u32[]{:S(2)}) collective-permute-start(bf16[128,1536]{1,0:T(8,128)(2,1)S(1)} %get-tuple-element.175), channel_id=1, source_target_pairs={{0,4},{1,5},{2,6},{3,7},{4,8},{5,9},{6,10},{7,11},{8,12},{9,13},{1... | collective-permute-start | bytes 1179656 | tf_op jit(solution)/shard_map/ppermute | solution.py:474
  687.5 22.6 %collective-permute-start.86 = (bf16[128,1536]{1,0:T(8,128)(2,1)S(1)}, bf16[128,1536]{1,0:T(8,128)(2,1)S(1)}, u32[]{:S(2)}, u32[]{:S(2)}) collective-permute-start(bf16[128,1536]{1,0:T(8,128)(2,1)S(1)} %get-tuple-element.176), channel_id=1, source_target_pairs={{0,12},{1,13},{2,14},{3,15},{4,0},{5,1},{6,2},{7,3},{8,4},{9,5},{1... | collective-permute-start | bytes 1179656 | tf_op jit(solution)/shard_map/ppermute | solution.py:474
  695.9 65.8 %collective-permute-start.127 = (bf16[128,2560]{1,0:T(8,128)(2,1)S(1)}, bf16[128,2560]{1,0:T(8,128)(2,1)S(1)}, u32[]{:S(2)}, u32[]{:S(2)}) collective-permute-start(bf16[128,2560]{1,0:T(8,128)(2,1)S(1)} %get-tuple-element.154), channel_id=1, source_target_pairs={{0,12},{1,13},{2,14},{3,15},{4,0},{5,1},{6,2},{7,3},{8,4},{9,5},{1... | collective-permute-start | bytes 1966088 | tf_op jit(solution)/shard_map/ppermute | solution.py:474
  715.5 106.7 %collective-permute-start.77 = (bf16[256,1664]{1,0:T(8,128)(2,1)S(1)}, bf16[256,1664]{1,0:T(8,128)(2,1)S(1)}, u32[]{:S(2)}, u32[]{:S(2)}) collective-permute-start(bf16[256,1664]{1,0:T(8,128)(2,1)S(1)} %pad_maximum_fusion.15), channel_id=1, source_target_pairs={{0,3},{1,0},{2,1},{3,2},{4,7},{5,4},{6,5},{7,6},{8,11},{9,8},{10,9... | collective-permute-start | bytes 2555912 | tf_op jit(solution)/shard_map/ppermute | solution.py:474
  717.3 20.0 %collective-permute-start.89 = (bf16[64,1536]{1,0:T(8,128)(2,1)S(1)}, bf16[64,1536]{1,0:T(8,128)(2,1)S(1)}, u32[]{:S(2)}, u32[]{:S(2)}) collective-permute-start(bf16[64,1536]{1,0:T(8,128)(2,1)S(1)} %concatenate.773), channel_id=1, source_target_pairs={{0,3},{1,0},{2,1},{3,2},{4,7},{5,4},{6,5},{7,6},{8,11},{9,8},{10,9... | collective-permute-start | bytes 589832 | tf_op jit(solution)/shard_map/ppermute | solution.py:474
  737.2 45.0 %collective-permute-start.75 = (bf16[256,1664]{1,0:T(8,128)(2,1)S(1)}, bf16[256,1664]{1,0:T(8,128)(2,1)S(1)}, u32[]{:S(2)}, u32[]{:S(2)}) collective-permute-start(bf16[256,1664]{1,0:T(8,128)(2,1)S(1)} %pad_maximum_fusion.14), channel_id=1, source_target_pairs={{0,1},{1,2},{2,3},{3,0},{4,5},{5,6},{6,7},{7,4},{8,9},{9,10},{10,1... | collective-permute-start | bytes 2555912 | tf_op jit(solution)/shard_map/ppermute | solution.py:474
  737.3 22.2 %collective-permute-start.87 = (bf16[64,1536]{1,0:T(8,128)(2,1)S(1)}, bf16[64,1536]{1,0:T(8,128)(2,1)S(1)}, u32[]{:S(2)}, u32[]{:S(2)}) collective-permute-start(bf16[64,1536]{1,0:T(8,128)(2,1)S(1)} %pad_maximum_fusion.37), channel_id=1, source_target_pairs={{0,1},{1,2},{2,3},{3,0},{4,5},{5,6},{6,7},{7,4},{8,9},{9,10},{10,1... | collective-permute-start | bytes 589832 | tf_op jit(solution)/shard_map/ppermute | solution.py:474
  737.4 23.6 %collective-permute-start.90 = (bf16[32,1536]{1,0:T(8,128)(2,1)S(1)}, bf16[32,1536]{1,0:T(8,128)(2,1)S(1)}, u32[]{:S(2)}, u32[]{:S(2)}) collective-permute-start(bf16[32,1536]{1,0:T(8,128)(2,1)S(1)} %add_convert_fusion.78), channel_id=1, source_target_pairs={{0,3},{1,0},{2,1},{3,2},{4,7},{5,4},{6,5},{7,6},{8,11},{9,8},{10,9... | collective-permute-start | bytes 294920 | tf_op jit(solution)/shard_map/ppermute | solution.py:474
  759.5 72.3 %collective-permute-start.97 = (bf16[256,1664]{1,0:T(8,128)(2,1)S(1)}, bf16[256,1664]{1,0:T(8,128)(2,1)S(1)}, u32[]{:S(2)}, u32[]{:S(2)}) collective-permute-start(bf16[256,1664]{1,0:T(8,128)(2,1)S(1)} %pad_maximum_fusion.17), channel_id=1, source_target_pairs={{0,3},{1,0},{2,1},{3,2},{4,7},{5,4},{6,5},{7,6},{8,11},{9,8},{10,9... | collective-permute-start | bytes 2555912 | tf_op jit(solution)/shard_map/ppermute | solution.py:474
  761.0 29.2 %collective-permute-start.95 = (bf16[256,1664]{1,0:T(8,128)(2,1)S(1)}, bf16[256,1664]{1,0:T(8,128)(2,1)S(1)}, u32[]{:S(2)}, u32[]{:S(2)}) collective-permute-start(bf16[256,1664]{1,0:T(8,128)(2,1)S(1)} %pad_maximum_fusion.16), channel_id=1, source_target_pairs={{0,1},{1,2},{2,3},{3,0},{4,5},{5,6},{6,7},{7,4},{8,9},{9,10},{10,1... | collective-permute-start | bytes 2555912 | tf_op jit(solution)/shard_map/ppermute | solution.py:474
  761.6 20.6 %collective-permute-start.88 = (bf16[32,1536]{1,0:T(8,128)(2,1)S(1)}, bf16[32,1536]{1,0:T(8,128)(2,1)S(1)}, u32[]{:S(2)}, u32[]{:S(2)}) collective-permute-start(bf16[32,1536]{1,0:T(8,128)(2,1)S(1)} %get-tuple-element.209), channel_id=1, source_target_pairs={{0,1},{1,2},{2,3},{3,0},{4,5},{5,6},{6,7},{7,4},{8,9},{9,10},{10,1... | collective-permute-start | bytes 294920 | tf_op jit(solution)/shard_map/ppermute | solution.py:474
  782.2 23.3 %collective-permute-start.117 = (bf16[128,2688]{1,0:T(8,128)(2,1)S(1)}, bf16[128,2688]{1,0:T(8,128)(2,1)S(1)}, u32[]{:S(2)}, u32[]{:S(2)}) collective-permute-start(bf16[128,2688]{1,0:T(8,128)(2,1)S(1)} %get-tuple-element.147), channel_id=1, source_target_pairs={{0,1},{1,2},{2,3},{3,0},{4,5},{5,6},{6,7},{7,4},{8,9},{9,10},{10,1... | collective-permute-start | bytes 2064392 | tf_op jit(solution)/shard_map/ppermute | solution.py:474
  805.5 26.3 %collective-permute-start.96 = (bf16[128,1664]{1,0:T(8,128)(2,1)S(1)}, bf16[128,1664]{1,0:T(8,128)(2,1)S(1)}, u32[]{:S(2)}, u32[]{:S(2)}) collective-permute-start(bf16[128,1664]{1,0:T(8,128)(2,1)S(1)} %add_convert_fusion.20), channel_id=1, source_target_pairs={{0,1},{1,2},{2,3},{3,0},{4,5},{5,6},{6,7},{7,4},{8,9},{9,10},{10,1... | collective-permute-start | bytes 1277960 | tf_op jit(solution)/shard_map/ppermute | solution.py:474
  842.9 20.0 %collective-permute-start.79 = (bf16[64,1664]{1,0:T(8,128)(2,1)S(1)}, bf16[64,1664]{1,0:T(8,128)(2,1)S(1)}, u32[]{:S(2)}, u32[]{:S(2)}) collective-permute-start(bf16[64,1664]{1,0:T(8,128)(2,1)S(1)} %pad_maximum_fusion.35), channel_id=1, source_target_pairs={{0,4},{1,5},{2,6},{3,7},{4,8},{5,9},{6,10},{7,11},{8,12},{9,13},{1... | collective-permute-start | bytes 638984 | tf_op jit(solution)/shard_map/ppermute | solution.py:474
  846.2 21.2 %collective-permute-start.99 = (bf16[64,1664]{1,0:T(8,128)(2,1)S(1)}, bf16[64,1664]{1,0:T(8,128)(2,1)S(1)}, u32[]{:S(2)}, u32[]{:S(2)}) collective-permute-start(bf16[64,1664]{1,0:T(8,128)(2,1)S(1)} %pad_maximum_fusion.36), channel_id=1, source_target_pairs={{0,4},{1,5},{2,6},{3,7},{4,8},{5,9},{6,10},{7,11},{8,12},{9,13},{1... | collective-permute-start | bytes 638984 | tf_op jit(solution)/shard_map/ppermute | solution.py:474
  846.5 22.1 %collective-permute-start.132 = (bf16[32,5248]{1,0:T(8,128)(2,1)S(1)}, bf16[32,5248]{1,0:T(8,128)(2,1)S(1)}, u32[]{:S(2)}, u32[]{:S(2)}) collective-permute-start(bf16[32,5248]{1,0:T(8,128)(2,1)S(1)} %get-tuple-element.187), channel_id=1, source_target_pairs={{0,16},{16,0},{32,48},{48,32},{1,17},{17,1},{33,49},{49,33},{2,18}... | collective-permute-start | bytes 1007624 | tf_op jit(solution)/shard_map/ppermute | solution.py:582
  847.6 22.5 %collective-permute-start.134 = (bf16[32,5248]{1,0:T(8,128)(2,1)S(1)}, bf16[32,5248]{1,0:T(8,128)(2,1)S(1)}, u32[]{:S(2)}, u32[]{:S(2)}) collective-permute-start(bf16[32,5248]{1,0:T(8,128)(2,1)S(1)} %get-tuple-element.188), channel_id=1, source_target_pairs={{0,48},{48,0},{16,32},{32,16},{1,49},{49,1},{17,33},{33,17},{2,50}... | collective-permute-start | bytes 1007624 | tf_op jit(solution)/shard_map/ppermute | solution.py:582
  870.3 19.8 %collective-permute-start.133 = (bf16[32,5248]{1,0:T(8,128)(2,1)S(1)}, bf16[32,5248]{1,0:T(8,128)(2,1)S(1)}, u32[]{:S(2)}, u32[]{:S(2)}) collective-permute-start(bf16[32,5248]{1,0:T(8,128)(2,1)S(1)} %get-tuple-element.185), channel_id=1, source_target_pairs={{0,48},{48,0},{16,32},{32,16},{1,49},{49,1},{17,33},{33,17},{2,50}... | collective-permute-start | bytes 1007624 | tf_op jit(solution)/shard_map/ppermute | solution.py:582
  912.6 20.4 %all-to-all-start.1 = ((bf16[16,64,384]{2,1,0:T(8,128)(2,1)}), bf16[16,64,384]{2,1,0:T(8,128)(2,1)S(1)}, u32[]{:S(2)}, u32[]{:S(2)}) async-start(bf16[16,64,384]{2,1,0:T(8,128)(2,1)} %pad.83), calls=%async_computation.1 | async-start | bytes 1572864 | tf_op jit(solution)/shard_map/all_to_all | solution.py:888
  (288 other events, 3231.9 us)

commit v2 on v1

--- a/solution.py
+++ b/solution.py
@@ -735,7 +735,7 @@
     def small_params(in_full, layer):
         first = main_a + ab_cols
         small_own = in_full[:, first : first + small_count].T
-        small = dot_nt(small_own, order)
+        small = small_own.astype(F32) if layer else dot_nt(small_own, order)
         at = 2
         conv_q = small[at : at + taps]
         conv_k = small[at + taps : at + 2 * taps]
@@ -775,7 +775,11 @@
         layer_out = after_mix + pair_sum(part)
         return layer_out, (source, normed, pre_a, pre_b, inverse, mixed, after_mix, normed_ffn, gate_act, up_act, hidden)
 
-    def backward_layer(grad_top, saved, in_full, ffn_full, params):
+    def scattered(blocks):
+        full = jnp.concatenate([block.astype(BF16) for block in blocks], axis=1)
+        return lax.psum_scatter(full, "fsdp", scatter_dimension=0, tiled=True)
+
+    def backward_layer(grad_top, saved, in_full, ffn_full, params, by_ring):
         source, normed, pre_a, pre_b, inverse, mixed, after_mix, normed_ffn, gate_act, up_act, hidden = saved
         in_w, in_v = in_full
         ffn_w, ffn_v = ffn_full
@@ -792,20 +796,32 @@
         mix_grad = grad_top + residual
         mix_low = mix_grad.astype(BF16)
         mixed_grad = dot(mix_low, ffn_w[:, out_first:down_first])
-        grad_ffn = (
-            torus_scatter(
-                Chunks(
-                    [
-                        (flipped(normed_ffn), gate_grad, None),
-                        (flipped(mix_low), mixed, None),
-                        (flipped(down_grad), hidden[:, :split], None),
-                    ]
+        if by_ring:
+            grad_ffn = (
+                torus_scatter(
+                    Chunks(
+                        [
+                            (flipped(normed_ffn), gate_grad, None),
+                            (flipped(mix_low), mixed, None),
+                            (flipped(down_grad), hidden[:, :split], None),
+                        ]
+                    ),
+                    True,
                 ),
-                True,
-            ),
-            torus_scatter(Chunks([(normed_ffn, up_grad, None), (down_grad, hidden[:, split:], None)]), False),
-        )
-        grad_ffn = rep_sum(jnp.concatenate(grad_ffn, axis=1))
+                torus_scatter(Chunks([(normed_ffn, up_grad, None), (down_grad, hidden[:, split:], None)]), False),
+            )
+            grad_ffn = jnp.concatenate(grad_ffn, axis=1)
+        else:
+            grad_ffn = scattered(
+                [
+                    dot_tn(normed_ffn, gate_grad),
+                    dot_tn(mix_low, mixed),
+                    dot_tn(down_grad, hidden[:, :split]),
+                    dot_tn(normed_ffn, up_grad),
+                    dot_tn(down_grad, hidden[:, split:]),
+                ]
+            )
+        grad_ffn = rep_sum(grad_ffn)
         pre_a_grad, pre_b_grad, gtq, gtk, gtv, ghead, ggain = mixer_backward(
             pre_a, pre_b, smalls, inverse, mixed_grad, length, heads, key_size, value_size
         )
@@ -832,19 +848,31 @@
         others = jnp.concatenate(
             [whole_cols(gtq[:taps]), whole_cols(gtk[:taps]), conv_v, tail.reshape(1, members * rows)], axis=0
         )
-        small = jnp.concatenate([gains.astype(BF16), ordered(others.astype(BF16)).astype(BF16)], axis=0)
+        others = others.astype(BF16)
+        others = ordered(others).astype(BF16) if by_ring else others
+        small = jnp.concatenate([gains.astype(BF16), others], axis=0)
         small = jnp.concatenate(
             [jnp.zeros((ab_cols, width), BF16), small, jnp.zeros((spare, width), BF16)], axis=0
         )
-        small = lax.dot_general(flip, small, (((0,), (1,)), ((), ())), preferred_element_type=F32)
-        turned = flipped(normed)
-        grad_in = (
-            torus_scatter(
-                Chunks([(turned, pre_a_grad[:, :main_a], None), (turned, pre_a_grad[:, main_a:], small)]), True
-            ),
-            torus_scatter(Chunks([(normed, pre_b_grad, None)]), False),
-        )
-        grad_in = rep_sum(jnp.concatenate(grad_in, axis=1))
+        if by_ring:
+            small = lax.dot_general(flip, small, (((0,), (1,)), ((), ())), preferred_element_type=F32)
+            turned = flipped(normed)
+            grad_in = (
+                torus_scatter(
+                    Chunks([(turned, pre_a_grad[:, :main_a], None), (turned, pre_a_grad[:, main_a:], small)]), True
+                ),
+                torus_scatter(Chunks([(normed, pre_b_grad, None)]), False),
+            )
+            grad_in = jnp.concatenate(grad_in, axis=1)
+        else:
+            grad_in = scattered(
+                [
+                    dot_tn(normed, pre_a_grad[:, :main_a]),
+                    dot_tn(normed, pre_a_grad[:, main_a:]) + small.T.astype(F32),
+                    dot_tn(normed, pre_b_grad),
+                ]
+            )
+        grad_in = rep_sum(grad_in)
         return source_grad, grad_in, grad_ffn
 
     def to_owner(first, second):
@@ -855,17 +883,18 @@
     source = ordered(inputs.reshape(tokens, width))
     in_0a, in_0b, token = fetch(in_pieces[0], in_a, None)
     ffn_0a, ffn_0b, token = fetch(ffn_pieces[0], ffn_a, token)
-    in_1a, in_1b, token = fetch(in_pieces[1], in_a, token)
-    ffn_1a, ffn_1b, token = fetch(ffn_pieces[1], ffn_a, token)
-    in_0, ffn_0, in_1, ffn_1 = (in_0a, in_0b), (ffn_0a, ffn_0b), (in_1a, in_1b), (ffn_1a, ffn_1b)
-    params_0, params_1 = small_params(in_0a, 0), small_params(in_1a, 1)
+    in_1 = lax.all_gather(in_pieces[1], "fsdp", axis=0, tiled=True)
+    ffn_1 = lax.all_gather(ffn_pieces[1], "fsdp", axis=0, tiled=True)
+    in_0, ffn_0 = (in_0a, in_0b), (ffn_0a, ffn_0b)
+    in_1, ffn_1 = (in_1[:, :in_a], in_1[:, in_a:]), (ffn_1[:, :ffn_a], ffn_1[:, ffn_a:])
+    params_0, params_1 = small_params(in_0a, 0), small_params(in_1[0], 1)
     first_out, first_saved = forward_layer(source, in_0, ffn_0, params_0)
-    middle = first_out.astype(BF16).astype(F32)
+    middle = dot_nt(first_out.astype(BF16), order)
     block_out, second_saved = forward_layer(middle, in_1, ffn_1, params_1)
-    cotangent = ordered(out_grad.reshape(tokens, width))
-    second_grad, second_in, second_ffn = backward_layer(cotangent, second_saved, in_1, ffn_1, params_1)
+    cotangent = out_grad.reshape(tokens, width).astype(F32)
+    second_grad, second_in, second_ffn = backward_layer(cotangent, second_saved, in_1, ffn_1, params_1, False)
     input_grad, first_in, first_ffn = backward_layer(
-        second_grad.astype(BF16).astype(F32), first_saved, in_0, ffn_0, params_0
+        ordered(second_grad.astype(BF16)), first_saved, in_0, ffn_0, params_0, True
     )
     in_left, in_right = to_owner(first_in, second_in)
     ffn_left, ffn_right = to_owner(first_ffn, second_ffn)
@@ -895,7 +924,7 @@
     tail = small[small_count - 1]
     conv_at = 2 + 2 * taps
     head_grads = tail[gain_rows : gain_rows + 2 * all_heads].reshape(2, all_heads)
-    edges = unordered(choose(input_grad, block_out)).reshape(1, micro, 1, length, width)
+    edges = choose(unordered(input_grad), block_out).reshape(1, micro, 1, length, width)
     return (
         edges,
         small[0][None],

time: 948 us -> 858 us (0.905)
  starting transfers between devices: 216 us -> 121 us
  waiting for transfers between devices: 300 us -> 319 us
  between operations: 5.55 us -> 17.1 us
  matrix products: 134 us -> 123 us
  local copies, waits for them, and re-layouts: 142 us -> 132 us
    ppermute x128 -> x64, starting transfers between devices: 167 us -> 82.4 us  [move(): return lax.ppermute(value, self.name, self.pairs(by))]
    dot_general x64 -> x40, matrix products: 62.3 us -> 48.4 us  [dot_tn(): lax.dot_general(left, right, (((0,), (0,)), ((), ())), preferred_element_...]
    ppermute x16, starting transfers between devices: 32.5 us -> 18.8 us  [rep_sum(): part = added(part, lax.ppermute(part, 'rep', pairs))]
    ppermute x13, waiting for transfers between devices: 1.44 us -> 12.8 us  [swapped(): return lax.ppermute(value, 'section', [(0, 1), (1, 0)])]
    ppermute x16, waiting for transfers between devices: 25.4 us -> 35.3 us  [rep_sum(): part = added(part, lax.ppermute(part, 'rep', pairs))]
    convert_element_type x56 -> x34, other arithmetic: 24.6 us -> 16 us  [added(): return total.astype(BF16)]
    unnamed x505 -> x366, local copies, waits for them, and re-layouts: 55.8 us -> 51.9 us
    ppermute x128 -> x64, waiting for transfers between devices: 261 us -> 258 us  [move(): return lax.ppermute(value, self.name, self.pairs(by))]
  transfers between devices with their start and end apart: 159 -> 99, of which waited for: 56 -> 47; matrix products, arithmetic and copies ran while one was open for 33% -> 28% of each run, Pallas kernels for 8% -> 5%
where the time goes in v2:
time: 858 us; the launch traced here: 846 us
  waiting for transfers between devices  319 us (37%)
  local copies, waits for them, and re-layouts  132 us (15%)
  matrix products  123 us (14%)
  starting transfers between devices  121 us (14%)
  Pallas kernels  72.7 us (8%)
  other arithmetic  61.5 us (7%)
  between operations  17.1 us (2%)
    ppermute x64, waiting for transfers between devices, move(): return lax.ppermute(value, self.name, self.pairs(by))  258 us
    ppermute x64, starting transfers between devices, move(): return lax.ppermute(value, self.name, self.pairs(by))  82.4 us
    unnamed x366, local copies, waits for them, and re-layouts  51.9 us
    dot_general x40, matrix products, dot_tn(): lax.dot_general(left, right, (((0,), (0,)), ((), ())), preferred_element_...  48.4 us
    pallas_call x2, Pallas kernels, mixer_forward(): pl.pallas_call(functools.partial(mixer_forward_kernel, heads, length), gr...  41.9 us
    dot_general x21, matrix products, dot(): return jnp.dot(left, right, preferred_element_type=F32)  37.8 us
    ppermute x16, waiting for transfers between devices, rep_sum(): part = added(part, lax.ppermute(part, 'rep', pairs))  35.3 us
    dot_general x19, matrix products, dot_nt(): lax.dot_general(left, right, (((1,), (1,)), ((), ())), preferred_element_...  33.8 us
  transfers between devices with their start and end apart: 99, of which 47 were waited for; matrix products, arithmetic and copies ran while one was open for 28% of the time, Pallas kernels for 5%

profile of v2, /device:TPU:0, one launch (start us, length us, event | category | flops | bytes accessed | tf_op | source)
XLA Modules:
  0.0 846.0 jit_solution(13068474378956729339)
XLA Ops:
  22.1 8.0 all-to-all-start
  33.5 3.1 collective-permute-start.9
  37.4 2.7 collective-permute-start.1
  40.1 11.8 %collective-permute-done.10 = bf16[64,1536]{1,0:T(8,128)(2,1)S(1)} collective-permute-done((bf16[64,1536]{1,0:T(8,128)(2,1)S(1)}, bf16[64,1536]{1,0:T(8,128)(2,1)S(1)}, u32[]{:S(2)}, u32[]{:S(2)}) %collective-permute-start.10) | collective-permute-done | bytes 196640 | tf_op jit(solution)/shard_map/ppermute | solution.py:474
  52.1 3.3 collective-permute-start.12
  77.1 25.5 %collective-permute-done.14 = bf16[256,1536]{1,0:T(8,128)(2,1)} collective-permute-done((bf16[256,1536]{1,0:T(8,128)(2,1)}, bf16[256,1536]{1,0:T(8,128)(2,1)}, u32[]{:S(2)}, u32[]{:S(2)}) %collective-permute-start.14) | collective-permute-done | bytes 786464 | tf_op jit(solution)/shard_map/ppermute | solution.py:474
  104.9 3.1 collective-permute-start.16
  141.2 2.9 collective-permute-start.31
  147.1 4.1 collective-permute-done.7
  151.2 2.8 collective-permute-start.22
  168.8 2.6 collective-permute-start.23
  176.4 20.9 %mixer_forward.2 = (bf16[256,1024]{1,0:T(8,128)(2,1)}, f32[4,2,128,128]{3,2,1,0:T(8,128)}) custom-call(f32[256,1664]{1,0:T(8,128)} %fusion.278.query_ref.value_ref.ab_ref, f32[256,1536]{1,0:T(8,128)} %fusion.279.key_ref.gate_ref, f32[256,1664]{1,0:T(8,128)} %fusion.278.query_ref.value_ref.ab_ref, f32[256,1536]{1,0:T(8,128)} %fusion.279.key_ref.gate_ref, ...), custom_call_target="tpu_custom_call" | custom-call | tf_op jit(solution)/shard_map/mixer_forward/pallas_call | solution.py:387
  197.3 26.3 %collective-permute-done.33 = bf16[256,2560]{1,0:T(8,128)(2,1)S(1)} collective-permute-done((bf16[256,2560]{1,0:T(8,128)(2,1)}, bf16[256,2560]{1,0:T(8,128)(2,1)S(1)}, u32[]{:S(2)}, u32[]{:S(2)}) %collective-permute-start.33) | collective-permute-done | bytes 1310752 | tf_op jit(solution)/shard_map/ppermute | solution.py:474
  223.8 3.3 collective-permute-start.35
  227.9 6.5 collective-permute-done.24
  234.5 3.3 collective-permute-start.26
  239.0 7.9 collective-permute-done.34
  251.0 2.6 collective-permute-done.27
  267.1 4.2 fusion.23.key_ref.gate_ref
  273.6 20.9 %mixer_forward.3 = (bf16[256,1024]{1,0:T(8,128)(2,1)}, f32[4,2,128,128]{3,2,1,0:T(8,128)}) custom-call(f32[256,1664]{1,0:T(8,128)} %fusion.19.query_ref.value_ref.ab_ref, f32[256,1536]{1,0:T(8,128)} %fusion.23.key_ref.gate_ref, f32[256,1664]{1,0:T(8,128)} %fusion.19.query_ref.value_ref.ab_ref, f32[256,1536]{1,0:T(8,128)} %fusion.23.key_ref.gate_ref, ...), custom_call_target="tpu_custom_call" | custom-call | tf_op jit(solution)/shard_map/mixer_forward/pallas_call | solution.py:387
  299.3 2.8 convolution_bitcast_fusion
  313.9 15.3 %mixer_backward.2 = (bf16[256,1664]{1,0:T(8,128)(2,1)}, bf16[256,1536]{1,0:T(8,128)(2,1)}, f32[8,512]{1,0:T(8,128)}, f32[8,512]{1,0:T(8,128)}, f32[8,1024]{1,0:T...) custom-call(f32[256,1664]{1,0:T(8,128)} %fusion.19.query_ref.value_ref.ab_ref, f32[256,1536]{1,0:T(8,128)} %fusion.23.key_ref.gate_ref, ...), custom_call_target="tpu_custom_call" | custom-call | tf_op jit(solution)/shard_map/mixer_backward/pallas_call | solution.py:411
  329.2 3.2 fusion.21
  332.5 3.3 fusion.83
  350.7 3.9 convolution_convert_fusion.3
  357.1 3.0 multiply_reduce_fusion.2
  363.4 3.3 fusion.67.grad_ref
  366.7 15.6 %mixer_backward.3 = (bf16[256,1664]{1,0:T(8,128)(2,1)}, bf16[256,1536]{1,0:T(8,128)(2,1)}, f32[8,512]{1,0:T(8,128)}, f32[8,512]{1,0:T(8,128)}, f32[8,1024]{1,0:T...) custom-call(f32[256,1664]{1,0:T(8,128)} %fusion.278.query_ref.value_ref.ab_ref, f32[256,1536]{1,0:T(8,128)} %fusion.279.key_ref.gate_ref, ...), custom_call_target="tpu_custom_call" | custom-call | tf_op jit(solution)/shard_map/mixer_backward/pallas_call | solution.py:411
  393.6 3.8 convolution_convert_fusion.2
  412.6 2.9 multiply_reduce_fusion.3
  419.2 2.6 concatenate.471
  423.1 6.5 pad_maximum_fusion
  435.4 2.6 fusion.56
  441.0 2.6 fusion.13
  446.9 2.6 fusion.14
  463.6 3.0 collective-permute-start.78
  492.4 3.2 collective-permute-start.53
  505.4 8.2 collective-permute-done.76
  515.3 14.3 %collective-permute-done.53 = bf16[256,1536]{1,0:T(8,128)(2,1)S(1)} collective-permute-done((bf16[256,1536]{1,0:T(8,128)(2,1)}, bf16[256,1536]{1,0:T(8,128)(2,1)S(1)}, u32[]{:S(2)}, u32[]{:S(2)}) %collective-permute-start.53) | collective-permute-done | bytes 786464 | tf_op jit(solution)/shard_map/ppermute | solution.py:474
  534.9 23.5 %collective-permute-done.77 = bf16[128,2560]{1,0:T(8,128)(2,1)S(1)} collective-permute-done((bf16[128,2560]{1,0:T(8,128)(2,1)S(1)}, bf16[128,2560]{1,0:T(8,128)(2,1)S(1)}, u32[]{:S(2)}, u32[]{:S(2)}) %collective-permute-start.77) | collective-permute-done | bytes 655392 | tf_op jit(solution)/shard_map/ppermute | solution.py:474
  558.6 2.8 add_convert_fusion.6
  563.8 2.8 fusion.3
  573.6 3.8 add_select_fusion
  580.7 46.6 %collective-permute-done.57 = bf16[64,1536]{1,0:T(8,128)(2,1)S(1)} collective-permute-done((bf16[64,1536]{1,0:T(8,128)(2,1)S(1)}, bf16[64,1536]{1,0:T(8,128)(2,1)S(1)}, u32[]{:S(2)}, u32[]{:S(2)}) %collective-permute-start.57) | collective-permute-done | bytes 196640 | tf_op jit(solution)/shard_map/ppermute | solution.py:474
  633.4 30.8 %collective-permute-done.55 = bf16[64,1536]{1,0:T(8,128)(2,1)S(1)} collective-permute-done((bf16[64,1536]{1,0:T(8,128)(2,1)S(1)}, bf16[64,1536]{1,0:T(8,128)(2,1)S(1)}, u32[]{:S(2)}, u32[]{:S(2)}) %collective-permute-start.55) | collective-permute-done | bytes 196640 | tf_op jit(solution)/shard_map/ppermute | solution.py:474
  664.2 3.2 collective-permute-start.71
  669.2 14.5 %collective-permute-done.56 = bf16[32,1536]{1,0:T(8,128)(2,1)S(1)} collective-permute-done((bf16[32,1536]{1,0:T(8,128)(2,1)S(1)}, bf16[32,1536]{1,0:T(8,128)(2,1)S(1)}, u32[]{:S(2)}, u32[]{:S(2)}) %collective-permute-start.56) | collective-permute-done | bytes 98336 | tf_op jit(solution)/shard_map/ppermute | solution.py:474
  683.9 7.3 collective-permute-done.82
  691.2 3.5 collective-permute-start.83
  694.9 5.0 collective-permute-done.80
  702.2 4.2 collective-permute-start.74
  706.5 5.6 collective-permute-done.81
  713.0 3.8 collective-permute-start.75
  718.6 2.7 collective-permute-done.75
  721.5 3.8 collective-permute-done.46
  728.7 2.7 collective-permute-done.49
  747.2 2.7 collective-permute-done.86
  755.7 2.9 collective-permute-done.85
  762.4 3.5 collective-permute-done.63
  770.2 4.9 collective-permute-done.64
  789.1 6.1 collective-permute-done.88
  800.2 8.2 collective-permute-done.89
  814.4 7.7 all-to-all-start.1
  824.0 12.7 %all-to-all-done.1 = bf16[16,64,384]{2,1,0:T(8,128)(2,1)S(1)} async-done(((bf16[16,64,384]{2,1,0:T(8,128)(2,1)}), bf16[16,64,384]{2,1,0:T(8,128)(2,1)S(1)}, u32[]{:S(2)}, u32[]{:S(2)}) %all-to-all-start.1) | async-done | bytes 786464 | tf_op jit(solution)/shard_map/all_to_all | solution.py:917
  (863 shorter events, 345.4 us)
Async XLA Ops:
  7.2 255.5 %all-gather.3.cloned.1.call-start = ((), (), s32[]{:S(2)}) async-start(), calls=%async_computation.4 | async-start | bytes 6963200 | tf_op jit(solution)/shard_map/all_gather | solution.py:886
  22.1 43.4 %all-to-all-start = ((bf16[16,64,384]{2,1,0:T(8,128)(2,1)}), bf16[16,64,384]{2,1,0:T(8,128)(2,1)}, u32[]{:S(2)}, u32[]{:S(2)}) async-start(bf16[16,64,384]{2,1,0:T(8,128)(2,1)} %bitcast.27), calls=%async_computation | async-start | bytes 1572864 | tf_op jit(solution)/shard_map/all_to_all | solution.py:675
  30.1 264.5 %all-gather.5.cloned.1.call-start = ((), (), s32[]{:S(2)}) async-start(), calls=%async_computation.5 | async-start | bytes 11419648 | tf_op jit(solution)/shard_map/all_gather | solution.py:887
  33.5 18.5 %collective-permute-start.9 = (bf16[64,1536]{1,0:T(8,128)(2,1)S(1)}, bf16[64,1536]{1,0:T(8,128)(2,1)S(1)}, u32[]{:S(2)}, u32[]{:S(2)}) collective-permute-start(bf16[64,1536]{1,0:T(8,128)(2,1)S(1)} %get-tuple-element.288), channel_id=1, source_target_pairs={{0,12},{1,13},{2,14},{3,15},{4,0},{5,1},{6,2},{7,3},{8,4},{9,5},{1... | collective-permute-start | bytes 589832 | tf_op jit(solution)/shard_map/ppermute | solution.py:474
  36.6 15.3 %collective-permute-start.10 = (bf16[64,1536]{1,0:T(8,128)(2,1)S(1)}, bf16[64,1536]{1,0:T(8,128)(2,1)S(1)}, u32[]{:S(2)}, u32[]{:S(2)}) collective-permute-start(bf16[64,1536]{1,0:T(8,128)(2,1)S(1)} %get-tuple-element.288), channel_id=1, source_target_pairs={{0,4},{1,5},{2,6},{3,7},{4,8},{5,9},{6,10},{7,11},{8,12},{9,13},{1... | collective-permute-start | bytes 589832 | tf_op jit(solution)/shard_map/ppermute | solution.py:474
  37.4 20.8 %collective-permute-start.1 = (bf16[64,1664]{1,0:T(8,128)(2,1)S(1)}, bf16[64,1664]{1,0:T(8,128)(2,1)S(1)}, u32[]{:S(2)}, u32[]{:S(2)}) collective-permute-start(bf16[64,1664]{1,0:T(8,128)(2,1)S(1)} %get-tuple-element.293), channel_id=1, source_target_pairs={{0,3},{1,0},{2,1},{3,2},{4,7},{5,4},{6,5},{7,6},{8,11},{9,8},{10,9... | collective-permute-start | bytes 638984 | tf_op jit(solution)/shard_map/ppermute | solution.py:474
  40.1 15.9 %collective-permute-start.2 = (bf16[64,1664]{1,0:T(8,128)(2,1)S(1)}, bf16[64,1664]{1,0:T(8,128)(2,1)S(1)}, u32[]{:S(2)}, u32[]{:S(2)}) collective-permute-start(bf16[64,1664]{1,0:T(8,128)(2,1)S(1)} %get-tuple-element.293), channel_id=1, source_target_pairs={{0,1},{1,2},{2,3},{3,0},{4,5},{5,6},{6,7},{7,4},{8,9},{9,10},{10,1... | collective-permute-start | bytes 638984 | tf_op jit(solution)/shard_map/ppermute | solution.py:474
  56.7 13.2 %collective-permute-start.3 = (bf16[32,1664]{1,0:T(8,128)(2,1)}, bf16[32,1664]{1,0:T(8,128)(2,1)}, u32[]{:S(2)}, u32[]{:S(2)}) collective-permute-start(bf16[32,1664]{1,0:T(8,128)(2,1)} %slice.1244), channel_id=1, source_target_pairs={{0,1},{1,2},{2,3},{3,0},{4,5},{5,6},{6,7},{7,4},{8,9},{9,10},{10,1... | collective-permute-start | bytes 319496 | tf_op jit(solution)/shard_map/ppermute | solution.py:474
  58.8 12.6 %collective-permute-start.4 = (bf16[32,1664]{1,0:T(8,128)(2,1)}, bf16[32,1664]{1,0:T(8,128)(2,1)}, u32[]{:S(2)}, u32[]{:S(2)}) collective-permute-start(bf16[32,1664]{1,0:T(8,128)(2,1)} %slice.1245), channel_id=1, source_target_pairs={{0,3},{1,0},{2,1},{3,2},{4,7},{5,4},{6,5},{7,6},{8,11},{9,8},{10,9... | collective-permute-start | bytes 319496 | tf_op jit(solution)/shard_map/ppermute | solution.py:474
  63.4 40.3 %collective-permute-start.13 = (bf16[256,1536]{1,0:T(8,128)(2,1)}, bf16[256,1536]{1,0:T(8,128)(2,1)}, u32[]{:S(2)}, u32[]{:S(2)}) collective-permute-start(bf16[256,1536]{1,0:T(8,128)(2,1)} %constant_dynamic-update-slice_fusion.14), channel_id=1, source_target_pairs={{0,3},{1,0},{2,1},{3,2},{4,7},{5,4},{6,5},{7,6},{8,11},{9,8},{10,9... | collective-permute-start | bytes 2359304 | tf_op jit(solution)/shard_map/ppermute | solution.py:474
  64.7 37.9 %collective-permute-start.14 = (bf16[256,1536]{1,0:T(8,128)(2,1)}, bf16[256,1536]{1,0:T(8,128)(2,1)}, u32[]{:S(2)}, u32[]{:S(2)}) collective-permute-start(bf16[256,1536]{1,0:T(8,128)(2,1)} %constant_dynamic-update-slice_fusion.14), channel_id=1, source_target_pairs={{0,1},{1,2},{2,3},{3,0},{4,5},{5,6},{6,7},{7,4},{8,9},{9,10},{10,1... | collective-permute-start | bytes 2359304 | tf_op jit(solution)/shard_map/ppermute | solution.py:474
  73.8 35.9 %collective-permute-start.5 = (bf16[256,1664]{1,0:T(8,128)(2,1)}, bf16[256,1664]{1,0:T(8,128)(2,1)}, u32[]{:S(2)}, u32[]{:S(2)}) collective-permute-start(bf16[256,1664]{1,0:T(8,128)(2,1)} %get-tuple-element.312), channel_id=1, source_target_pairs={{0,12},{1,13},{2,14},{3,15},{4,0},{5,1},{6,2},{7,3},{8,4},{9,5},{1... | collective-permute-start | bytes 2555912 | tf_op jit(solution)/shard_map/ppermute | solution.py:474
  74.0 40.6 %collective-permute-start.6 = (bf16[256,1664]{1,0:T(8,128)(2,1)}, bf16[256,1664]{1,0:T(8,128)(2,1)}, u32[]{:S(2)}, u32[]{:S(2)}) collective-permute-start(bf16[256,1664]{1,0:T(8,128)(2,1)} %get-tuple-element.312), channel_id=1, source_target_pairs={{0,4},{1,5},{2,6},{3,7},{4,8},{5,9},{6,10},{7,11},{8,12},{9,13},{1... | collective-permute-start | bytes 2555912 | tf_op jit(solution)/shard_map/ppermute | solution.py:474
  77.1 681.6 %reduce-scatter.7.cloned.1.call-start = ((), (), s32[]{:S(2)}) async-start(), calls=%async_computation.7 | async-start | bytes 6963200 | tf_op jit(solution)/shard_map/reduce_scatter | solution.py:780
  103.7 15.3 %collective-permute-start.15 = (bf16[128,1536]{1,0:T(8,128)(2,1)S(1)}, bf16[128,1536]{1,0:T(8,128)(2,1)S(1)}, u32[]{:S(2)}, u32[]{:S(2)}) collective-permute-start(bf16[128,1536]{1,0:T(8,128)(2,1)S(1)} %slice.1254), channel_id=1, source_target_pairs={{0,1},{1,2},{2,3},{3,0},{4,5},{5,6},{6,7},{7,4},{8,9},{9,10},{10,1... | collective-permute-start | bytes 1179656 | tf_op jit(solution)/shard_map/ppermute | solution.py:474
  104.9 24.3 %collective-permute-start.16 = (bf16[128,1536]{1,0:T(8,128)(2,1)S(1)}, bf16[128,1536]{1,0:T(8,128)(2,1)S(1)}, u32[]{:S(2)}, u32[]{:S(2)}) collective-permute-start(bf16[128,1536]{1,0:T(8,128)(2,1)S(1)} %slice.1261), channel_id=1, source_target_pairs={{0,3},{1,0},{2,1},{3,2},{4,7},{5,4},{6,5},{7,6},{8,11},{9,8},{10,9... | collective-permute-start | bytes 1179656 | tf_op jit(solution)/shard_map/ppermute | solution.py:474
  110.5 34.3 %collective-permute-start.19 = (bf16[64,2688]{1,0:T(8,128)(2,1)S(1)}, bf16[64,2688]{1,0:T(8,128)(2,1)S(1)}, u32[]{:S(2)}, u32[]{:S(2)}) collective-permute-start(bf16[64,2688]{1,0:T(8,128)(2,1)S(1)} %get-tuple-element.231), channel_id=1, source_target_pairs={{0,3},{1,0},{2,1},{3,2},{4,7},{5,4},{6,5},{7,6},{8,11},{9,8},{10,9... | collective-permute-start | bytes 1032200 | tf_op jit(solution)/shard_map/ppermute | solution.py:474
  112.7 28.5 %collective-permute-start.20 = (bf16[64,2688]{1,0:T(8,128)(2,1)S(1)}, bf16[64,2688]{1,0:T(8,128)(2,1)S(1)}, u32[]{:S(2)}, u32[]{:S(2)}) collective-permute-start(bf16[64,2688]{1,0:T(8,128)(2,1)S(1)} %get-tuple-element.231), channel_id=1, source_target_pairs={{0,1},{1,2},{2,3},{3,0},{4,5},{5,6},{6,7},{7,4},{8,9},{9,10},{10,1... | collective-permute-start | bytes 1032200 | tf_op jit(solution)/shard_map/ppermute | solution.py:474
  114.7 25.4 %collective-permute-start.28 = (bf16[64,2560]{1,0:T(8,128)(2,1)S(1)}, bf16[64,2560]{1,0:T(8,128)(2,1)S(1)}, u32[]{:S(2)}, u32[]{:S(2)}) collective-permute-start(bf16[64,2560]{1,0:T(8,128)(2,1)S(1)} %get-tuple-element.226), channel_id=1, source_target_pairs={{0,12},{1,13},{2,14},{3,15},{4,0},{5,1},{6,2},{7,3},{8,4},{9,5},{1... | collective-permute-start | bytes 983048 | tf_op jit(solution)/shard_map/ppermute | solution.py:474
  119.0 18.7 %collective-permute-start.29 = (bf16[64,2560]{1,0:T(8,128)(2,1)S(1)}, bf16[64,2560]{1,0:T(8,128)(2,1)S(1)}, u32[]{:S(2)}, u32[]{:S(2)}) collective-permute-start(bf16[64,2560]{1,0:T(8,128)(2,1)S(1)} %get-tuple-element.226), channel_id=1, source_target_pairs={{0,4},{1,5},{2,6},{3,7},{4,8},{5,9},{6,10},{7,11},{8,12},{9,13},{1... | collective-permute-start | bytes 983048 | tf_op jit(solution)/shard_map/ppermute | solution.py:474
  129.3 21.9 %collective-permute-start.7 = (bf16[128,1664]{1,0:T(8,128)(2,1)S(1)}, bf16[128,1664]{1,0:T(8,128)(2,1)S(1)}, u32[]{:S(2)}, u32[]{:S(2)}) collective-permute-start(bf16[128,1664]{1,0:T(8,128)(2,1)S(1)} %slice.1246), channel_id=1, source_target_pairs={{0,4},{1,5},{2,6},{3,7},{4,8},{5,9},{6,10},{7,11},{8,12},{9,13},{1... | collective-permute-start | bytes 1277960 | tf_op jit(solution)/shard_map/ppermute | solution.py:474
  137.7 16.2 %collective-permute-start.8 = (bf16[128,1664]{1,0:T(8,128)(2,1)S(1)}, bf16[128,1664]{1,0:T(8,128)(2,1)S(1)}, u32[]{:S(2)}, u32[]{:S(2)}) collective-permute-start(bf16[128,1664]{1,0:T(8,128)(2,1)S(1)} %slice.1247), channel_id=1, source_target_pairs={{0,12},{1,13},{2,14},{3,15},{4,0},{5,1},{6,2},{7,3},{8,4},{9,5},{1... | collective-permute-start | bytes 1277960 | tf_op jit(solution)/shard_map/ppermute | solution.py:474
  140.1 20.3 %collective-permute-start.30 = (bf16[32,2560]{1,0:T(8,128)(2,1)}, bf16[32,2560]{1,0:T(8,128)(2,1)S(1)}, u32[]{:S(2)}, u32[]{:S(2)}) collective-permute-start(bf16[32,2560]{1,0:T(8,128)(2,1)} %slice.1295), channel_id=1, source_target_pairs={{0,4},{1,5},{2,6},{3,7},{4,8},{5,9},{6,10},{7,11},{8,12},{9,13},{1... | collective-permute-start | bytes 491528 | tf_op jit(solution)/shard_map/ppermute | solution.py:474
  141.2 19.8 %collective-permute-start.31 = (bf16[32,2560]{1,0:T(8,128)(2,1)}, bf16[32,2560]{1,0:T(8,128)(2,1)S(1)}, u32[]{:S(2)}, u32[]{:S(2)}) collective-permute-start(bf16[32,2560]{1,0:T(8,128)(2,1)} %slice.1296), channel_id=1, source_target_pairs={{0,12},{1,13},{2,14},{3,15},{4,0},{5,1},{6,2},{7,3},{8,4},{9,5},{1... | collective-permute-start | bytes 491528 | tf_op jit(solution)/shard_map/ppermute | solution.py:474
  144.8 19.7 %collective-permute-start.21 = (bf16[32,2688]{1,0:T(8,128)(2,1)}, bf16[32,2688]{1,0:T(8,128)(2,1)}, u32[]{:S(2)}, u32[]{:S(2)}) collective-permute-start(bf16[32,2688]{1,0:T(8,128)(2,1)} %slice.1288), channel_id=1, source_target_pairs={{0,1},{1,2},{2,3},{3,0},{4,5},{5,6},{6,7},{7,4},{8,9},{9,10},{10,1... | collective-permute-start | bytes 516104 | tf_op jit(solution)/shard_map/ppermute | solution.py:474
  151.2 15.0 %collective-permute-start.22 = (bf16[32,2688]{1,0:T(8,128)(2,1)}, bf16[32,2688]{1,0:T(8,128)(2,1)}, u32[]{:S(2)}, u32[]{:S(2)}) collective-permute-start(bf16[32,2688]{1,0:T(8,128)(2,1)} %slice.1289), channel_id=1, source_target_pairs={{0,3},{1,0},{2,1},{3,2},{4,7},{5,4},{6,5},{7,6},{8,11},{9,8},{10,9... | collective-permute-start | bytes 516104 | tf_op jit(solution)/shard_map/ppermute | solution.py:474
  162.5 61.3 %collective-permute-start.32 = (bf16[256,2560]{1,0:T(8,128)(2,1)}, bf16[256,2560]{1,0:T(8,128)(2,1)S(1)}, u32[]{:S(2)}, u32[]{:S(2)}) collective-permute-start(bf16[256,2560]{1,0:T(8,128)(2,1)} %constant_dynamic-update-slice_fusion.44), channel_id=1, source_target_pairs={{0,3},{1,0},{2,1},{3,2},{4,7},{5,4},{6,5},{7,6},{8,11},{9,8},{10,9... | collective-permute-start | bytes 3932168 | tf_op jit(solution)/shard_map/ppermute | solution.py:474
  163.6 60.0 %collective-permute-start.33 = (bf16[256,2560]{1,0:T(8,128)(2,1)}, bf16[256,2560]{1,0:T(8,128)(2,1)S(1)}, u32[]{:S(2)}, u32[]{:S(2)}) collective-permute-start(bf16[256,2560]{1,0:T(8,128)(2,1)} %constant_dynamic-update-slice_fusion.44), channel_id=1, source_target_pairs={{0,1},{1,2},{2,3},{3,0},{4,5},{5,6},{6,7},{7,4},{8,9},{9,10},{10,1... | collective-permute-start | bytes 3932168 | tf_op jit(solution)/shard_map/ppermute | solution.py:474
  168.8 65.7 %collective-permute-start.23 = (bf16[256,2688]{1,0:T(8,128)(2,1)}, bf16[256,2688]{1,0:T(8,128)(2,1)S(1)}, u32[]{:S(2)}, u32[]{:S(2)}) collective-permute-start(bf16[256,2688]{1,0:T(8,128)(2,1)} %get-tuple-element.302), channel_id=1, source_target_pairs={{0,12},{1,13},{2,14},{3,15},{4,0},{5,1},{6,2},{7,3},{8,4},{9,5},{1... | collective-permute-start | bytes 4128776 | tf_op jit(solution)/shard_map/ppermute | solution.py:474
  171.4 62.9 %collective-permute-start.24 = (bf16[256,2688]{1,0:T(8,128)(2,1)}, bf16[256,2688]{1,0:T(8,128)(2,1)S(1)}, u32[]{:S(2)}, u32[]{:S(2)}) collective-permute-start(bf16[256,2688]{1,0:T(8,128)(2,1)} %get-tuple-element.302), channel_id=1, source_target_pairs={{0,4},{1,5},{2,6},{3,7},{4,8},{5,9},{6,10},{7,11},{8,12},{9,13},{1... | collective-permute-start | bytes 4128776 | tf_op jit(solution)/shard_map/ppermute | solution.py:474
  223.7 23.2 %collective-permute-start.34 = (bf16[128,2560]{1,0:T(8,128)(2,1)S(1)}, bf16[128,2560]{1,0:T(8,128)(2,1)S(1)}, u32[]{:S(2)}, u32[]{:S(2)}) collective-permute-start(bf16[128,2560]{1,0:T(8,128)(2,1)S(1)} %slice.1298), channel_id=1, source_target_pairs={{0,1},{1,2},{2,3},{3,0},{4,5},{5,6},{6,7},{7,4},{8,9},{9,10},{10,1... | collective-permute-start | bytes 1966088 | tf_op jit(solution)/shard_map/ppermute | solution.py:474
  223.8 23.4 %collective-permute-start.35 = (bf16[128,2560]{1,0:T(8,128)(2,1)S(1)}, bf16[128,2560]{1,0:T(8,128)(2,1)S(1)}, u32[]{:S(2)}, u32[]{:S(2)}) collective-permute-start(bf16[128,2560]{1,0:T(8,128)(2,1)S(1)} %slice.1305), channel_id=1, source_target_pairs={{0,3},{1,0},{2,1},{3,2},{4,7},{5,4},{6,5},{7,6},{8,11},{9,8},{10,9... | collective-permute-start | bytes 1966088 | tf_op jit(solution)/shard_map/ppermute | solution.py:474
  234.4 14.9 %collective-permute-start.25 = (bf16[128,2688]{1,0:T(8,128)(2,1)S(1)}, bf16[128,2688]{1,0:T(8,128)(2,1)S(1)}, u32[]{:S(2)}, u32[]{:S(2)}) collective-permute-start(bf16[128,2688]{1,0:T(8,128)(2,1)S(1)} %slice.1290), channel_id=1, source_target_pairs={{0,4},{1,5},{2,6},{3,7},{4,8},{5,9},{6,10},{7,11},{8,12},{9,13},{1... | collective-permute-start | bytes 2064392 | tf_op jit(solution)/shard_map/ppermute | solution.py:474
  234.5 15.1 %collective-permute-start.26 = (bf16[128,2688]{1,0:T(8,128)(2,1)S(1)}, bf16[128,2688]{1,0:T(8,128)(2,1)S(1)}, u32[]{:S(2)}, u32[]{:S(2)}) collective-permute-start(bf16[128,2688]{1,0:T(8,128)(2,1)S(1)} %slice.1291), channel_id=1, source_target_pairs={{0,12},{1,13},{2,14},{3,15},{4,0},{5,1},{6,2},{7,3},{8,4},{9,5},{1... | collective-permute-start | bytes 2064392 | tf_op jit(solution)/shard_map/ppermute | solution.py:474
  386.8 25.8 %collective-permute-start.41 = (f32[256,1024]{0,1:T(8,128)}, f32[256,1024]{0,1:T(8,128)}, u32[]{:S(2)}, u32[]{:S(2)}) collective-permute-start(f32[256,1024]{0,1:T(8,128)} %convolution_add_fusion.2), channel_id=1, source_target_pairs={{0,64},{64,0},{1,65},{65,1},{2,66},{66,2},{3,67},{67,3},{4,68},{68... | collective-permute-start | bytes 3145736 | tf_op jit(solution)/shard_map/ppermute | solution.py:444
  429.6 354.5 %reduce-scatter.5.cloned.1.call-start = ((), (), s32[]{:S(2)}) async-start(), calls=%async_computation.6 | async-start | bytes 11419648 | tf_op jit(solution)/shard_map/reduce_scatter | solution.py:780
  440.4 132.1 %collective-permute-start.42 = (f32[256,1024]{1,0:T(8,128)}, f32[256,1024]{1,0:T(8,128)}, u32[]{:S(2)}, u32[]{:S(2)}) collective-permute-start(f32[256,1024]{1,0:T(8,128)} %convolution_add_fusion), channel_id=1, source_target_pairs={{0,64},{64,0},{1,65},{65,1},{2,66},{66,2},{3,67},{67,3},{4,68},{68... | collective-permute-start | bytes 3145736 | tf_op jit(solution)/shard_map/ppermute | solution.py:444
  463.6 71.3 %collective-permute-start.78 = (bf16[256,2560]{1,0:T(8,128)(2,1)}, bf16[256,2560]{1,0:T(8,128)(2,1)}, u32[]{:S(2)}, u32[]{:S(2)}) collective-permute-start(bf16[256,2560]{1,0:T(8,128)(2,1)} %pad_maximum_fusion.8), channel_id=1, source_target_pairs={{0,12},{1,13},{2,14},{3,15},{4,0},{5,1},{6,2},{7,3},{8,4},{9,5},{1... | collective-permute-start | bytes 3932168 | tf_op jit(solution)/shard_map/ppermute | solution.py:474
  468.5 45.1 %collective-permute-start.76 = (bf16[256,2560]{1,0:T(8,128)(2,1)}, bf16[256,2560]{1,0:T(8,128)(2,1)}, u32[]{:S(2)}, u32[]{:S(2)}) collective-permute-start(bf16[256,2560]{1,0:T(8,128)(2,1)} %pad_maximum_fusion.7), channel_id=1, source_target_pairs={{0,4},{1,5},{2,6},{3,7},{4,8},{5,9},{6,10},{7,11},{8,12},{9,13},{1... | collective-permute-start | bytes 3932168 | tf_op jit(solution)/shard_map/ppermute | solution.py:474
  492.4 37.2 %collective-permute-start.53 = (bf16[256,1536]{1,0:T(8,128)(2,1)}, bf16[256,1536]{1,0:T(8,128)(2,1)S(1)}, u32[]{:S(2)}, u32[]{:S(2)}) collective-permute-start(bf16[256,1536]{1,0:T(8,128)(2,1)} %convolution_convert_fusion.5), channel_id=1, source_target_pairs={{0,12},{1,13},{2,14},{3,15},{4,0},{5,1},{6,2},{7,3},{8,4},{9,5},{1... | collective-permute-start | bytes 2359304 | tf_op jit(solution)/shard_map/ppermute | solution.py:474
  497.0 36.4 %collective-permute-start.51 = (bf16[256,1536]{1,0:T(8,128)(2,1)S(1)}, bf16[256,1536]{1,0:T(8,128)(2,1)S(1)}, u32[]{:S(2)}, u32[]{:S(2)}) collective-permute-start(bf16[256,1536]{1,0:T(8,128)(2,1)S(1)} %convolution_convert_fusion.6), channel_id=1, source_target_pairs={{0,4},{1,5},{2,6},{3,7},{4,8},{5,9},{6,10},{7,11},{8,12},{9,13},{1... | collective-permute-start | bytes 2359304 | tf_op jit(solution)/shard_map/ppermute | solution.py:474
  514.9 43.6 %collective-permute-start.77 = (bf16[128,2560]{1,0:T(8,128)(2,1)S(1)}, bf16[128,2560]{1,0:T(8,128)(2,1)S(1)}, u32[]{:S(2)}, u32[]{:S(2)}) collective-permute-start(bf16[128,2560]{1,0:T(8,128)(2,1)S(1)} %add_convert_fusion.7), channel_id=1, source_target_pairs={{0,4},{1,5},{2,6},{3,7},{4,8},{5,9},{6,10},{7,11},{8,12},{9,13},{1... | collective-permute-start | bytes 1966088 | tf_op jit(solution)/shard_map/ppermute | solution.py:474
  529.6 98.7 %collective-permute-start.70 = (bf16[256,2688]{1,0:T(8,128)(2,1)}, bf16[256,2688]{1,0:T(8,128)(2,1)}, u32[]{:S(2)}, u32[]{:S(2)}) collective-permute-start(bf16[256,2688]{1,0:T(8,128)(2,1)} %pad_maximum_fusion.6), channel_id=1, source_target_pairs={{0,3},{1,0},{2,1},{3,2},{4,7},{5,4},{6,5},{7,6},{8,11},{9,8},{10,9... | collective-permute-start | bytes 4128776 | tf_op jit(solution)/shard_map/ppermute | solution.py:474
  533.3 96.1 %collective-permute-start.68 = (bf16[256,2688]{1,0:T(8,128)(2,1)}, bf16[256,2688]{1,0:T(8,128)(2,1)}, u32[]{:S(2)}, u32[]{:S(2)}) collective-permute-start(bf16[256,2688]{1,0:T(8,128)(2,1)} %pad_maximum_fusion.5), channel_id=1, source_target_pairs={{0,1},{1,2},{2,3},{3,0},{4,5},{5,6},{6,7},{7,4},{8,9},{9,10},{10,1... | collective-permute-start | bytes 4128776 | tf_op jit(solution)/shard_map/ppermute | solution.py:474
  534.9 42.9 %collective-permute-start.52 = (bf16[128,1536]{1,0:T(8,128)(2,1)}, bf16[128,1536]{1,0:T(8,128)(2,1)}, u32[]{:S(2)}, u32[]{:S(2)}) collective-permute-start(bf16[128,1536]{1,0:T(8,128)(2,1)} %get-tuple-element.212), channel_id=1, source_target_pairs={{0,4},{1,5},{2,6},{3,7},{4,8},{5,9},{6,10},{7,11},{8,12},{9,13},{1... | collective-permute-start | bytes 1179656 | tf_op jit(solution)/shard_map/ppermute | solution.py:474
  558.4 19.8 %collective-permute-start.54 = (bf16[128,1536]{1,0:T(8,128)(2,1)}, bf16[128,1536]{1,0:T(8,128)(2,1)}, u32[]{:S(2)}, u32[]{:S(2)}) collective-permute-start(bf16[128,1536]{1,0:T(8,128)(2,1)} %get-tuple-element.213), channel_id=1, source_target_pairs={{0,12},{1,13},{2,14},{3,15},{4,0},{5,1},{6,2},{7,3},{8,4},{9,5},{1... | collective-permute-start | bytes 1179656 | tf_op jit(solution)/shard_map/ppermute | solution.py:474
  572.5 95.0 %collective-permute-start.79 = (bf16[128,2560]{1,0:T(8,128)(2,1)S(1)}, bf16[128,2560]{1,0:T(8,128)(2,1)S(1)}, u32[]{:S(2)}, u32[]{:S(2)}) collective-permute-start(bf16[128,2560]{1,0:T(8,128)(2,1)S(1)} %copy-done.77), channel_id=1, source_target_pairs={{0,12},{1,13},{2,14},{3,15},{4,0},{5,1},{6,2},{7,3},{8,4},{9,5},{1... | collective-permute-start | bytes 1966088 | tf_op jit(solution)/shard_map/ppermute | solution.py:474
  577.8 139.0 %collective-permute-start.45 = (bf16[256,1664]{1,0:T(8,128)(2,1)S(1)}, bf16[256,1664]{1,0:T(8,128)(2,1)S(1)}, u32[]{:S(2)}, u32[]{:S(2)}) collective-permute-start(bf16[256,1664]{1,0:T(8,128)(2,1)S(1)} %pad_maximum_fusion.10), channel_id=1, source_target_pairs={{0,3},{1,0},{2,1},{3,2},{4,7},{5,4},{6,5},{7,6},{8,11},{9,8},{10,9... | collective-permute-start | bytes 2555912 | tf_op jit(solution)/shard_map/ppermute | solution.py:474
  579.7 47.6 %collective-permute-start.57 = (bf16[64,1536]{1,0:T(8,128)(2,1)S(1)}, bf16[64,1536]{1,0:T(8,128)(2,1)S(1)}, u32[]{:S(2)}, u32[]{:S(2)}) collective-permute-start(bf16[64,1536]{1,0:T(8,128)(2,1)S(1)} %concatenate.538), channel_id=1, source_target_pairs={{0,3},{1,0},{2,1},{3,2},{4,7},{5,4},{6,5},{7,6},{8,11},{9,8},{10,9... | collective-permute-start | bytes 589832 | tf_op jit(solution)/shard_map/ppermute | solution.py:474
  627.3 63.9 %collective-permute-start.43 = (bf16[256,1664]{1,0:T(8,128)(2,1)S(1)}, bf16[256,1664]{1,0:T(8,128)(2,1)S(1)}, u32[]{:S(2)}, u32[]{:S(2)}) collective-permute-start(bf16[256,1664]{1,0:T(8,128)(2,1)S(1)} %pad_maximum_fusion.9), channel_id=1, source_target_pairs={{0,1},{1,2},{2,3},{3,0},{4,5},{5,6},{6,7},{7,4},{8,9},{9,10},{10,1... | collective-permute-start | bytes 2555912 | tf_op jit(solution)/shard_map/ppermute | solution.py:474
  628.3 35.9 %collective-permute-start.55 = (bf16[64,1536]{1,0:T(8,128)(2,1)S(1)}, bf16[64,1536]{1,0:T(8,128)(2,1)S(1)}, u32[]{:S(2)}, u32[]{:S(2)}) collective-permute-start(bf16[64,1536]{1,0:T(8,128)(2,1)S(1)} %pad_maximum_fusion.23), channel_id=1, source_target_pairs={{0,1},{1,2},{2,3},{3,0},{4,5},{5,6},{6,7},{7,4},{8,9},{9,10},{10,1... | collective-permute-start | bytes 589832 | tf_op jit(solution)/shard_map/ppermute | solution.py:474
  629.4 34.8 %collective-permute-start.58 = (bf16[32,1536]{1,0:T(8,128)(2,1)S(1)}, bf16[32,1536]{1,0:T(8,128)(2,1)S(1)}, u32[]{:S(2)}, u32[]{:S(2)}) collective-permute-start(bf16[32,1536]{1,0:T(8,128)(2,1)S(1)} %add_convert_fusion.49), channel_id=1, source_target_pairs={{0,3},{1,0},{2,1},{3,2},{4,7},{5,4},{6,5},{7,6},{8,11},{9,8},{10,9... | collective-permute-start | bytes 294920 | tf_op jit(solution)/shard_map/ppermute | solution.py:474
  664.2 36.1 %collective-permute-start.69 = (bf16[128,2688]{1,0:T(8,128)(2,1)S(1)}, bf16[128,2688]{1,0:T(8,128)(2,1)S(1)}, u32[]{:S(2)}, u32[]{:S(2)}) collective-permute-start(bf16[128,2688]{1,0:T(8,128)(2,1)S(1)} %get-tuple-element.196), channel_id=1, source_target_pairs={{0,1},{1,2},{2,3},{3,0},{4,5},{5,6},{6,7},{7,4},{8,9},{9,10},{10,1... | collective-permute-start | bytes 2064392 | tf_op jit(solution)/shard_map/ppermute | solution.py:474
  664.2 36.1 %collective-permute-start.71 = (bf16[128,2688]{1,0:T(8,128)(2,1)S(1)}, bf16[128,2688]{1,0:T(8,128)(2,1)S(1)}, u32[]{:S(2)}, u32[]{:S(2)}) collective-permute-start(bf16[128,2688]{1,0:T(8,128)(2,1)S(1)} %get-tuple-element.197), channel_id=1, source_target_pairs={{0,3},{1,0},{2,1},{3,2},{4,7},{5,4},{6,5},{7,6},{8,11},{9,8},{10,9... | collective-permute-start | bytes 2064392 | tf_op jit(solution)/shard_map/ppermute | solution.py:474
  667.5 16.1 %collective-permute-start.56 = (bf16[32,1536]{1,0:T(8,128)(2,1)S(1)}, bf16[32,1536]{1,0:T(8,128)(2,1)S(1)}, u32[]{:S(2)}, u32[]{:S(2)}) collective-permute-start(bf16[32,1536]{1,0:T(8,128)(2,1)S(1)} %get-tuple-element.234), channel_id=1, source_target_pairs={{0,1},{1,2},{2,3},{3,0},{4,5},{5,6},{6,7},{7,4},{8,9},{9,10},{10,1... | collective-permute-start | bytes 294920 | tf_op jit(solution)/shard_map/ppermute | solution.py:474
  699.8 17.0 %collective-permute-start.44 = (bf16[128,1664]{1,0:T(8,128)(2,1)S(1)}, bf16[128,1664]{1,0:T(8,128)(2,1)S(1)}, u32[]{:S(2)}, u32[]{:S(2)}) collective-permute-start(bf16[128,1664]{1,0:T(8,128)(2,1)S(1)} %add_convert_fusion.13), channel_id=1, source_target_pairs={{0,1},{1,2},{2,3},{3,0},{4,5},{5,6},{6,7},{7,4},{8,9},{9,10},{10,1... | collective-permute-start | bytes 1277960 | tf_op jit(solution)/shard_map/ppermute | solution.py:474
  700.0 12.1 %collective-permute-start.81 = (bf16[32,2560]{1,0:T(8,128)(2,1)S(1)}, bf16[32,2560]{1,0:T(8,128)(2,1)S(1)}, u32[]{:S(2)}, u32[]{:S(2)}) collective-permute-start(bf16[32,2560]{1,0:T(8,128)(2,1)S(1)} %get-tuple-element.206), channel_id=1, source_target_pairs={{0,1},{1,2},{2,3},{3,0},{4,5},{5,6},{6,7},{7,4},{8,9},{9,10},{10,1... | collective-permute-start | bytes 491528 | tf_op jit(solution)/shard_map/ppermute | solution.py:474
  702.2 10.8 %collective-permute-start.74 = (bf16[64,2688]{1,0:T(8,128)(2,1)S(1)}, bf16[64,2688]{1,0:T(8,128)(2,1)S(1)}, u32[]{:S(2)}, u32[]{:S(2)}) collective-permute-start(bf16[64,2688]{1,0:T(8,128)(2,1)S(1)} %concatenate.542), channel_id=1, source_target_pairs={{0,12},{1,13},{2,14},{3,15},{4,0},{5,1},{6,2},{7,3},{8,4},{9,5},{1... | collective-permute-start | bytes 1032200 | tf_op jit(solution)/shard_map/ppermute | solution.py:474
  706.4 12.2 %collective-permute-start.72 = (bf16[64,2688]{1,0:T(8,128)(2,1)S(1)}, bf16[64,2688]{1,0:T(8,128)(2,1)S(1)}, u32[]{:S(2)}, u32[]{:S(2)}) collective-permute-start(bf16[64,2688]{1,0:T(8,128)(2,1)S(1)} %pad_maximum_fusion.20), channel_id=1, source_target_pairs={{0,4},{1,5},{2,6},{3,7},{4,8},{5,9},{6,10},{7,11},{8,12},{9,13},{1... | collective-permute-start | bytes 1032200 | tf_op jit(solution)/shard_map/ppermute | solution.py:474
  738.0 12.0 %collective-permute-start.86 = (bf16[32,5248]{1,0:T(8,128)(2,1)S(1)}, bf16[32,5248]{1,0:T(8,128)(2,1)S(1)}, u32[]{:S(2)}, u32[]{:S(2)}) collective-permute-start(bf16[32,5248]{1,0:T(8,128)(2,1)S(1)} %get-tuple-element.221), channel_id=1, source_target_pairs={{0,48},{48,0},{16,32},{32,16},{1,49},{49,1},{17,33},{33,17},{2,50}... | collective-permute-start | bytes 1007624 | tf_op jit(solution)/shard_map/ppermute | solution.py:582
  752.1 24.1 %collective-permute-start.87 = (bf16[32,5248]{1,0:T(8,128)(2,1)S(1)}, bf16[32,5248]{1,0:T(8,128)(2,1)S(1)}, u32[]{:S(2)}, u32[]{:S(2)}) collective-permute-start(bf16[32,5248]{1,0:T(8,128)(2,1)S(1)} %get-tuple-element.219), channel_id=1, source_target_pairs={{0,16},{16,0},{32,48},{48,32},{1,17},{17,1},{33,49},{49,33},{2,18}... | collective-permute-start | bytes 1007624 | tf_op jit(solution)/shard_map/ppermute | solution.py:582
  755.7 14.3 %collective-permute-start.62 = (bf16[32,3200]{1,0:T(8,128)(2,1)S(1)}, bf16[32,3200]{1,0:T(8,128)(2,1)S(1)}, u32[]{:S(2)}, u32[]{:S(2)}) collective-permute-start(bf16[32,3200]{1,0:T(8,128)(2,1)S(1)} %get-tuple-element.281), channel_id=1, source_target_pairs={{0,16},{16,0},{32,48},{48,32},{1,17},{17,1},{33,49},{49,33},{2,18}... | collective-permute-start | bytes 614408 | tf_op jit(solution)/shard_map/ppermute | solution.py:582
  785.4 11.4 %collective-permute-start.90 = (bf16[32,5248]{1,0:T(8,128)(2,1)S(1)}, bf16[32,5248]{1,0:T(8,128)(2,1)S(1)}, u32[]{:S(2)}, u32[]{:S(2)}) collective-permute-start(bf16[32,5248]{1,0:T(8,128)(2,1)S(1)} %get-tuple-element.225), channel_id=1, source_target_pairs={{0,48},{48,0},{16,32},{32,16},{1,49},{49,1},{17,33},{33,17},{2,50}... | collective-permute-start | bytes 1007624 | tf_op jit(solution)/shard_map/ppermute | solution.py:582
  814.4 22.4 %all-to-all-start.1 = ((bf16[16,64,384]{2,1,0:T(8,128)(2,1)}), bf16[16,64,384]{2,1,0:T(8,128)(2,1)S(1)}, u32[]{:S(2)}, u32[]{:S(2)}) async-start(bf16[16,64,384]{2,1,0:T(8,128)(2,1)} %pad.83), calls=%async_computation.2 | async-start | bytes 1572864 | tf_op jit(solution)/shard_map/all_to_all | solution.py:917
  (183 other events, 2228.2 us)
Sparse Core Ops, SparseCore 0:
  20.7 91.3 all-gather.2
  114.9 125.6 all-gather.4
  429.7 91.1 reduce-scatter.6
  524.5 132.7 reduce-scatter.4

commit v3 on v2

--- a/solution.py
+++ b/solution.py
@@ -522,28 +522,29 @@
     )
 
 
-def torus_scatter(chunks, x_first):
+def scatter_parts(total, make):
+    quarter, half = total // SIDE, total // SIDE // 2
+    join = lambda one, two: make([(one, one + half), (two, two + half)])
+    return [
+        join(2 * quarter, quarter + half),
+        join(2 * quarter + half, 3 * quarter),
+        join(quarter, 3 * quarter + half),
+        make([(0, quarter)]),
+    ]
+
+
+def torus_scatter(first_parts, x_first):
     first, second = ("x", "z") if x_first else ("z", "x")
 
-    def parts(total, make):
-        quarter, half = total // SIDE, total // SIDE // 2
-        join = lambda one, two: make([(one, one + half), (two, two + half)])
-        return [
-            join(2 * quarter, quarter + half),
-            join(2 * quarter + half, 3 * quarter),
-            join(quarter, 3 * quarter + half),
-            make([(0, quarter)]),
-        ]
-
-    block = ring_scatter(parts(chunks.total, chunks.make), Ring(first))
+    block = ring_scatter(first_parts, Ring(first))
     make = lambda cuts: jnp.concatenate([block[i:j] for i, j in cuts], axis=0)
-    return ring_scatter(parts(block.shape[0], make), Ring(second))
+    return ring_scatter(scatter_parts(block.shape[0], make), Ring(second))
 
 
 class Chunks:
     def __init__(self, products):
         self.products = products
-        self.total = products[0][0].shape[1]
+        self.parts = scatter_parts(products[0][0].shape[1], self.make)
 
     def make(self, cuts):
         blocks = []
@@ -775,8 +776,10 @@
         layer_out = after_mix + pair_sum(part)
         return layer_out, (source, normed, pre_a, pre_b, inverse, mixed, after_mix, normed_ffn, gate_act, up_act, hidden)
 
-    def scattered(blocks):
-        full = jnp.concatenate([block.astype(BF16) for block in blocks], axis=1)
+    def side_by_side(blocks):
+        return jnp.concatenate([block.astype(BF16) for block in blocks], axis=1)
+
+    def scattered(full):
         return lax.psum_scatter(full, "fsdp", scatter_dimension=0, tiled=True)
 
     def backward_layer(grad_top, saved, in_full, ffn_full, params, by_ring):
@@ -797,22 +800,18 @@
         mix_low = mix_grad.astype(BF16)
         mixed_grad = dot(mix_low, ffn_w[:, out_first:down_first])
         if by_ring:
-            grad_ffn = (
-                torus_scatter(
-                    Chunks(
-                        [
-                            (flipped(normed_ffn), gate_grad, None),
-                            (flipped(mix_low), mixed, None),
-                            (flipped(down_grad), hidden[:, :split], None),
-                        ]
-                    ),
-                    True,
-                ),
-                torus_scatter(Chunks([(normed_ffn, up_grad, None), (down_grad, hidden[:, split:], None)]), False),
-            )
-            grad_ffn = jnp.concatenate(grad_ffn, axis=1)
+            parts_a = Chunks(
+                [
+                    (flipped(normed_ffn), gate_grad, None),
+                    (flipped(mix_low), mixed, None),
+                    (flipped(down_grad), hidden[:, :split], None),
+                ]
+            ).parts
+            parts_b = Chunks([(normed_ffn, up_grad, None), (down_grad, hidden[:, split:], None)]).parts
+            mixed_grad, parts_a, parts_b = lax.optimization_barrier((mixed_grad, parts_a, parts_b))
+            grad_ffn = jnp.concatenate([torus_scatter(parts_a, True), torus_scatter(parts_b, False)], axis=1)
         else:
-            grad_ffn = scattered(
+            full = side_by_side(
                 [
                     dot_tn(normed_ffn, gate_grad),
                     dot_tn(mix_low, mixed),
@@ -821,6 +820,8 @@
                     dot_tn(down_grad, hidden[:, split:]),
                 ]
             )
+            mixed_grad, full = lax.optimization_barrier((mixed_grad, full))
+            grad_ffn = scattered(full)
         grad_ffn = rep_sum(grad_ffn)
         pre_a_grad, pre_b_grad, gtq, gtk, gtv, ghead, ggain = mixer_backward(
             pre_a, pre_b, smalls, inverse, mixed_grad, length, heads, key_size, value_size
@@ -859,19 +860,22 @@
             turned = flipped(normed)
             grad_in = (
                 torus_scatter(
-                    Chunks([(turned, pre_a_grad[:, :main_a], None), (turned, pre_a_grad[:, main_a:], small)]), True
+                    Chunks([(turned, pre_a_grad[:, :main_a], None), (turned, pre_a_grad[:, main_a:], small)]).parts,
+                    True,
                 ),
-                torus_scatter(Chunks([(normed, pre_b_grad, None)]), False),
+                torus_scatter(Chunks([(normed, pre_b_grad, None)]).parts, False),
             )
             grad_in = jnp.concatenate(grad_in, axis=1)
         else:
-            grad_in = scattered(
+            full = side_by_side(
                 [
                     dot_tn(normed, pre_a_grad[:, :main_a]),
                     dot_tn(normed, pre_a_grad[:, main_a:]) + small.T.astype(F32),
                     dot_tn(normed, pre_b_grad),
                 ]
             )
+            source_grad, full = lax.optimization_barrier((source_grad, full))
+            grad_in = scattered(full)
         grad_in = rep_sum(grad_in)
         return source_grad, grad_in, grad_ffn
 

time: 858 us -> 834 us (0.972)
  waiting for transfers between devices: 319 us -> 299 us
  local copies, waits for them, and re-layouts: 132 us -> 113 us
    ppermute x64, waiting for transfers between devices: 258 us -> 250 us  [move(): return lax.ppermute(value, self.name, self.pairs(by))]
    unnamed x366 -> x336, local copies, waits for them, and re-layouts: 51.9 us -> 49 us
  transfers between devices with their start and end apart: 99 -> 99, of which waited for: 47 -> 40; matrix products, arithmetic and copies ran while one was open for 28% -> 28% of each run, Pallas kernels for 5% -> 7%
where the time goes in v3:
time: 834 us; the launch traced here: 823 us
  waiting for transfers between devices  299 us (36%)
  starting transfers between devices  129 us (15%)
  matrix products  127 us (15%)
  local copies, waits for them, and re-layouts  113 us (14%)
  Pallas kernels  73.2 us (9%)
  other arithmetic  65.1 us (8%)
  between operations  17.2 us (2%)
    ppermute x64, waiting for transfers between devices, move(): return lax.ppermute(value, self.name, self.pairs(by))  250 us
    ppermute x64, starting transfers between devices, move(): return lax.ppermute(value, self.name, self.pairs(by))  86 us
    unnamed x336, local copies, waits for them, and re-layouts  49 us
    dot_general x40, matrix products, dot_tn(): lax.dot_general(left, right, (((0,), (0,)), ((), ())), preferred_element_...  48.1 us
    pallas_call x2, Pallas kernels, mixer_forward(): pl.pallas_call(functools.partial(mixer_forward_kernel, heads, length), gr...  41.9 us
    dot_general x21, matrix products, dot(): return jnp.dot(left, right, preferred_element_type=F32)  41 us
    dot_general x19, matrix products, dot_nt(): lax.dot_general(left, right, (((1,), (1,)), ((), ())), preferred_element_...  34.5 us
    pallas_call x2, Pallas kernels, mixer_backward(): pl.pallas_call(functools.partial(mixer_backward_kernel, heads, length), g...  31.3 us
  transfers between devices with their start and end apart: 99, of which 40 were waited for; matrix products, arithmetic and copies ran while one was open for 28% of the time, Pallas kernels for 7%

profile of v3, /device:TPU:0, one launch (start us, length us, event | category | flops | bytes accessed | tf_op | source)
XLA Modules:
  0.0 822.6 jit_solution(6123187192487126839)
XLA Ops:
  22.9 8.0 all-to-all-start
  35.5 3.1 collective-permute-start.9
  39.4 2.7 collective-permute-start.1
  42.1 11.5 %collective-permute-done.10 = bf16[64,1536]{1,0:T(8,128)(2,1)S(1)} collective-permute-done((bf16[64,1536]{1,0:T(8,128)(2,1)S(1)}, bf16[64,1536]{1,0:T(8,128)(2,1)S(1)}, u32[]{:S(2)}, u32[]{:S(2)}) %collective-permute-start.10) | collective-permute-done | bytes 196640 | tf_op jit(solution)/shard_map/ppermute | solution.py:474
  53.8 3.3 collective-permute-start.12
  79.2 25.7 %collective-permute-done.14 = bf16[256,1536]{1,0:T(8,128)(2,1)} collective-permute-done((bf16[256,1536]{1,0:T(8,128)(2,1)}, bf16[256,1536]{1,0:T(8,128)(2,1)}, u32[]{:S(2)}, u32[]{:S(2)}) %collective-permute-start.14) | collective-permute-done | bytes 786464 | tf_op jit(solution)/shard_map/ppermute | solution.py:474
  107.2 3.1 collective-permute-start.16
  138.4 3.2 collective-permute-start.8
  141.8 3.3 collective-permute-start.31
  147.3 5.6 collective-permute-done.7
  176.9 20.9 %mixer_forward.2 = (bf16[256,1024]{1,0:T(8,128)(2,1)}, f32[4,2,128,128]{3,2,1,0:T(8,128)}) custom-call(f32[256,1664]{1,0:T(8,128)} %fusion.273.query_ref.value_ref.ab_ref, f32[256,1536]{1,0:T(8,128)} %fusion.274.key_ref.gate_ref, f32[256,1664]{1,0:T(8,128)} %fusion.273.query_ref.value_ref.ab_ref, f32[256,1536]{1,0:T(8,128)} %fusion.274.key_ref.gate_ref, ...), custom_call_target="tpu_custom_call" | custom-call | tf_op jit(solution)/shard_map/mixer_forward/pallas_call | solution.py:387
  197.8 26.3 %collective-permute-done.33 = bf16[256,2560]{1,0:T(8,128)(2,1)S(1)} collective-permute-done((bf16[256,2560]{1,0:T(8,128)(2,1)}, bf16[256,2560]{1,0:T(8,128)(2,1)S(1)}, u32[]{:S(2)}, u32[]{:S(2)}) %collective-permute-start.33) | collective-permute-done | bytes 1310752 | tf_op jit(solution)/shard_map/ppermute | solution.py:474
  224.3 3.3 collective-permute-start.35
  228.4 6.7 collective-permute-done.24
  235.2 3.3 collective-permute-start.26
  239.7 8.5 %collective-permute-done.34 = bf16[128,2560]{1,0:T(8,128)(2,1)S(1)} collective-permute-done((bf16[128,2560]{1,0:T(8,128)(2,1)S(1)}, bf16[128,2560]{1,0:T(8,128)(2,1)S(1)}, u32[]{:S(2)}, u32[]{:S(2)}) %collective-permute-start.34) | collective-permute-done | bytes 655392 | tf_op jit(solution)/shard_map/ppermute | solution.py:474
  252.4 2.6 collective-permute-done.27
  268.4 4.3 fusion.23.key_ref.gate_ref
  275.0 20.9 %mixer_forward.3 = (bf16[256,1024]{1,0:T(8,128)(2,1)}, f32[4,2,128,128]{3,2,1,0:T(8,128)}) custom-call(f32[256,1664]{1,0:T(8,128)} %fusion.19.query_ref.value_ref.ab_ref, f32[256,1536]{1,0:T(8,128)} %fusion.23.key_ref.gate_ref, f32[256,1664]{1,0:T(8,128)} %fusion.19.query_ref.value_ref.ab_ref, f32[256,1536]{1,0:T(8,128)} %fusion.23.key_ref.gate_ref, ...), custom_call_target="tpu_custom_call" | custom-call | tf_op jit(solution)/shard_map/mixer_forward/pallas_call | solution.py:387
  296.0 2.5 fusion.65
  300.5 2.8 convolution_bitcast_fusion
  309.9 3.9 fusion.13
  321.0 2.6 fusion.14
  325.9 3.3 fusion.63.grad_ref
  329.2 15.3 %mixer_backward.2 = (bf16[256,1664]{1,0:T(8,128)(2,1)}, bf16[256,1536]{1,0:T(8,128)(2,1)}, f32[8,512]{1,0:T(8,128)}, f32[8,512]{1,0:T(8,128)}, f32[8,1024]{1,0:T...) custom-call(f32[256,1664]{1,0:T(8,128)} %fusion.19.query_ref.value_ref.ab_ref, f32[256,1536]{1,0:T(8,128)} %fusion.23.key_ref.gate_ref, ...), custom_call_target="tpu_custom_call" | custom-call | tf_op jit(solution)/shard_map/mixer_backward/pallas_call | solution.py:411
  344.5 3.2 fusion.21
  347.7 4.1 fusion.83
  360.5 4.0 convolution_convert_fusion
  364.5 2.7 convolution_convert_fusion.1
  374.9 6.4 pad_maximum_fusion
  381.3 2.6 multiply_add_fusion.2
  389.8 2.5 fusion.56
  427.1 2.5 pad_maximum_fusion.9
  434.9 3.7 fusion.67.grad_ref
  446.0 16.0 %mixer_backward.3 = (bf16[256,1664]{1,0:T(8,128)(2,1)}, bf16[256,1536]{1,0:T(8,128)(2,1)}, f32[8,512]{1,0:T(8,128)}, f32[8,512]{1,0:T(8,128)}, f32[8,1024]{1,0:T...) custom-call(f32[256,1664]{1,0:T(8,128)} %fusion.273.query_ref.value_ref.ab_ref, f32[256,1536]{1,0:T(8,128)} %fusion.274.key_ref.gate_ref, ...), custom_call_target="tpu_custom_call" | custom-call | tf_op jit(solution)/shard_map/mixer_backward/pallas_call | solution.py:411
  487.8 14.1 %collective-permute-done.51 = bf16[256,1536]{1,0:T(8,128)(2,1)} collective-permute-done((bf16[256,1536]{1,0:T(8,128)(2,1)}, bf16[256,1536]{1,0:T(8,128)(2,1)}, u32[]{:S(2)}, u32[]{:S(2)}) %collective-permute-start.51) | collective-permute-done | bytes 786464 | tf_op jit(solution)/shard_map/ppermute | solution.py:474
  501.9 2.7 collective-permute-start.78
  507.6 2.6 multiply_reduce_fusion.1
  511.1 2.9 fusion
  519.6 3.8 collective-permute-start.54
  523.3 3.7 add_select_fusion
  527.6 43.9 %collective-permute-done.52 = bf16[128,1536]{1,0:T(8,128)(2,1)} collective-permute-done((bf16[128,1536]{1,0:T(8,128)(2,1)}, bf16[128,1536]{1,0:T(8,128)(2,1)}, u32[]{:S(2)}, u32[]{:S(2)}) %collective-permute-start.52) | collective-permute-done | bytes 393248 | tf_op jit(solution)/shard_map/ppermute | solution.py:474
  576.2 42.0 %collective-permute-done.57 = bf16[64,1536]{1,0:T(8,128)(2,1)S(1)} collective-permute-done((bf16[64,1536]{1,0:T(8,128)(2,1)S(1)}, bf16[64,1536]{1,0:T(8,128)(2,1)S(1)}, u32[]{:S(2)}, u32[]{:S(2)}) %collective-permute-start.57) | collective-permute-done | bytes 196640 | tf_op jit(solution)/shard_map/ppermute | solution.py:474
  624.3 19.6 %collective-permute-done.55 = bf16[64,1536]{1,0:T(8,128)(2,1)S(1)} collective-permute-done((bf16[64,1536]{1,0:T(8,128)(2,1)S(1)}, bf16[64,1536]{1,0:T(8,128)(2,1)S(1)}, u32[]{:S(2)}, u32[]{:S(2)}) %collective-permute-start.55) | collective-permute-done | bytes 196640 | tf_op jit(solution)/shard_map/ppermute | solution.py:474
  645.7 3.3 collective-permute-start.79
  650.8 4.0 collective-permute-done.56
  655.1 3.3 collective-permute-start.71
  663.5 11.1 %collective-permute-done.69 = bf16[128,2688]{1,0:T(8,128)(2,1)S(1)} collective-permute-done((bf16[128,2688]{1,0:T(8,128)(2,1)S(1)}, bf16[128,2688]{1,0:T(8,128)(2,1)S(1)}, u32[]{:S(2)}, u32[]{:S(2)}) %collective-permute-start.69) | collective-permute-done | bytes 688160 | tf_op jit(solution)/shard_map/ppermute | solution.py:474
  674.6 5.9 collective-permute-done.71
  686.1 2.6 collective-permute-start.83
  689.1 3.6 collective-permute-done.74
  695.1 3.2 collective-permute-done.75
  698.4 3.1 collective-permute-done.81
  702.0 3.2 collective-permute-start.49
  705.3 3.3 collective-permute-done.49
  708.6 3.8 collective-permute-start.50
  725.7 2.7 collective-permute-done.86
  732.5 2.7 collective-permute-start.60
  739.4 3.3 collective-permute-done.63
  748.7 3.0 collective-permute-done.66
  767.4 5.3 collective-permute-done.88
  778.8 5.4 collective-permute-done.91
  791.5 7.2 all-to-all-start.1
  800.6 12.8 %all-to-all-done.1 = bf16[16,64,384]{2,1,0:T(8,128)(2,1)S(1)} async-done(((bf16[16,64,384]{2,1,0:T(8,128)(2,1)}), bf16[16,64,384]{2,1,0:T(8,128)(2,1)S(1)}, u32[]{:S(2)}, u32[]{:S(2)}) %all-to-all-start.1) | async-done | bytes 786464 | tf_op jit(solution)/shard_map/all_to_all | solution.py:921
  (840 shorter events, 333.0 us)
Async XLA Ops:
  7.2 256.9 %all-gather.3.cloned.1.call-start = ((), (), s32[]{:S(2)}) async-start(), calls=%async_computation.4 | async-start | bytes 6963200 | tf_op jit(solution)/shard_map/all_gather | solution.py:890
  22.9 44.9 %all-to-all-start = ((bf16[16,64,384]{2,1,0:T(8,128)(2,1)}), bf16[16,64,384]{2,1,0:T(8,128)(2,1)S(1)}, u32[]{:S(2)}, u32[]{:S(2)}) async-start(bf16[16,64,384]{2,1,0:T(8,128)(2,1)} %bitcast.27), calls=%async_computation | async-start | bytes 1572864 | tf_op jit(solution)/shard_map/all_to_all | solution.py:676
  30.9 265.1 %all-gather.5.cloned.1.call-start = ((), (), s32[]{:S(2)}) async-start(), calls=%async_computation.5 | async-start | bytes 11419648 | tf_op jit(solution)/shard_map/all_gather | solution.py:891
  35.5 18.2 %collective-permute-start.9 = (bf16[64,1536]{1,0:T(8,128)(2,1)S(1)}, bf16[64,1536]{1,0:T(8,128)(2,1)S(1)}, u32[]{:S(2)}, u32[]{:S(2)}) collective-permute-start(bf16[64,1536]{1,0:T(8,128)(2,1)S(1)} %get-tuple-element.316), channel_id=1, source_target_pairs={{0,12},{1,13},{2,14},{3,15},{4,0},{5,1},{6,2},{7,3},{8,4},{9,5},{1... | collective-permute-start | bytes 589832 | tf_op jit(solution)/shard_map/ppermute | solution.py:474
  38.6 15.0 %collective-permute-start.10 = (bf16[64,1536]{1,0:T(8,128)(2,1)S(1)}, bf16[64,1536]{1,0:T(8,128)(2,1)S(1)}, u32[]{:S(2)}, u32[]{:S(2)}) collective-permute-start(bf16[64,1536]{1,0:T(8,128)(2,1)S(1)} %get-tuple-element.316), channel_id=1, source_target_pairs={{0,4},{1,5},{2,6},{3,7},{4,8},{5,9},{6,10},{7,11},{8,12},{9,13},{1... | collective-permute-start | bytes 589832 | tf_op jit(solution)/shard_map/ppermute | solution.py:474
  39.4 21.0 %collective-permute-start.1 = (bf16[64,1664]{1,0:T(8,128)(2,1)S(1)}, bf16[64,1664]{1,0:T(8,128)(2,1)S(1)}, u32[]{:S(2)}, u32[]{:S(2)}) collective-permute-start(bf16[64,1664]{1,0:T(8,128)(2,1)S(1)} %get-tuple-element.321), channel_id=1, source_target_pairs={{0,3},{1,0},{2,1},{3,2},{4,7},{5,4},{6,5},{7,6},{8,11},{9,8},{10,9... | collective-permute-start | bytes 638984 | tf_op jit(solution)/shard_map/ppermute | solution.py:474
  42.1 15.6 %collective-permute-start.2 = (bf16[64,1664]{1,0:T(8,128)(2,1)S(1)}, bf16[64,1664]{1,0:T(8,128)(2,1)S(1)}, u32[]{:S(2)}, u32[]{:S(2)}) collective-permute-start(bf16[64,1664]{1,0:T(8,128)(2,1)S(1)} %get-tuple-element.321), channel_id=1, source_target_pairs={{0,1},{1,2},{2,3},{3,0},{4,5},{5,6},{6,7},{7,4},{8,9},{9,10},{10,1... | collective-permute-start | bytes 638984 | tf_op jit(solution)/shard_map/ppermute | solution.py:474
  59.1 13.1 %collective-permute-start.3 = (bf16[32,1664]{1,0:T(8,128)(2,1)}, bf16[32,1664]{1,0:T(8,128)(2,1)}, u32[]{:S(2)}, u32[]{:S(2)}) collective-permute-start(bf16[32,1664]{1,0:T(8,128)(2,1)} %slice.1244), channel_id=1, source_target_pairs={{0,1},{1,2},{2,3},{3,0},{4,5},{5,6},{6,7},{7,4},{8,9},{9,10},{10,1... | collective-permute-start | bytes 319496 | tf_op jit(solution)/shard_map/ppermute | solution.py:474
  61.1 12.7 %collective-permute-start.4 = (bf16[32,1664]{1,0:T(8,128)(2,1)}, bf16[32,1664]{1,0:T(8,128)(2,1)}, u32[]{:S(2)}, u32[]{:S(2)}) collective-permute-start(bf16[32,1664]{1,0:T(8,128)(2,1)} %slice.1245), channel_id=1, source_target_pairs={{0,3},{1,0},{2,1},{3,2},{4,7},{5,4},{6,5},{7,6},{8,11},{9,8},{10,9... | collective-permute-start | bytes 319496 | tf_op jit(solution)/shard_map/ppermute | solution.py:474
  65.8 40.2 %collective-permute-start.13 = (bf16[256,1536]{1,0:T(8,128)(2,1)}, bf16[256,1536]{1,0:T(8,128)(2,1)}, u32[]{:S(2)}, u32[]{:S(2)}) collective-permute-start(bf16[256,1536]{1,0:T(8,128)(2,1)} %constant_dynamic-update-slice_fusion.14), channel_id=1, source_target_pairs={{0,3},{1,0},{2,1},{3,2},{4,7},{5,4},{6,5},{7,6},{8,11},{9,8},{10,9... | collective-permute-start | bytes 2359304 | tf_op jit(solution)/shard_map/ppermute | solution.py:474
  67.0 37.9 %collective-permute-start.14 = (bf16[256,1536]{1,0:T(8,128)(2,1)}, bf16[256,1536]{1,0:T(8,128)(2,1)}, u32[]{:S(2)}, u32[]{:S(2)}) collective-permute-start(bf16[256,1536]{1,0:T(8,128)(2,1)} %constant_dynamic-update-slice_fusion.14), channel_id=1, source_target_pairs={{0,1},{1,2},{2,3},{3,0},{4,5},{5,6},{6,7},{7,4},{8,9},{9,10},{10,1... | collective-permute-start | bytes 2359304 | tf_op jit(solution)/shard_map/ppermute | solution.py:474
  76.1 35.8 %collective-permute-start.5 = (bf16[256,1664]{1,0:T(8,128)(2,1)}, bf16[256,1664]{1,0:T(8,128)(2,1)}, u32[]{:S(2)}, u32[]{:S(2)}) collective-permute-start(bf16[256,1664]{1,0:T(8,128)(2,1)} %get-tuple-element.340), channel_id=1, source_target_pairs={{0,12},{1,13},{2,14},{3,15},{4,0},{5,1},{6,2},{7,3},{8,4},{9,5},{1... | collective-permute-start | bytes 2555912 | tf_op jit(solution)/shard_map/ppermute | solution.py:474
  76.1 40.6 %collective-permute-start.6 = (bf16[256,1664]{1,0:T(8,128)(2,1)}, bf16[256,1664]{1,0:T(8,128)(2,1)}, u32[]{:S(2)}, u32[]{:S(2)}) collective-permute-start(bf16[256,1664]{1,0:T(8,128)(2,1)} %get-tuple-element.340), channel_id=1, source_target_pairs={{0,4},{1,5},{2,6},{3,7},{4,8},{5,9},{6,10},{7,11},{8,12},{9,13},{1... | collective-permute-start | bytes 2555912 | tf_op jit(solution)/shard_map/ppermute | solution.py:474
  79.1 656.7 %reduce-scatter.7.cloned.1.call-start = ((), (), s32[]{:S(2)}) async-start(), calls=%async_computation.7 | async-start | bytes 6963200 | tf_op jit(solution)/shard_map/reduce_scatter | solution.py:783
  105.9 13.6 %collective-permute-start.15 = (bf16[128,1536]{1,0:T(8,128)(2,1)S(1)}, bf16[128,1536]{1,0:T(8,128)(2,1)S(1)}, u32[]{:S(2)}, u32[]{:S(2)}) collective-permute-start(bf16[128,1536]{1,0:T(8,128)(2,1)S(1)} %slice.1254), channel_id=1, source_target_pairs={{0,1},{1,2},{2,3},{3,0},{4,5},{5,6},{6,7},{7,4},{8,9},{9,10},{10,1... | collective-permute-start | bytes 1179656 | tf_op jit(solution)/shard_map/ppermute | solution.py:474
  107.2 24.2 %collective-permute-start.16 = (bf16[128,1536]{1,0:T(8,128)(2,1)S(1)}, bf16[128,1536]{1,0:T(8,128)(2,1)S(1)}, u32[]{:S(2)}, u32[]{:S(2)}) collective-permute-start(bf16[128,1536]{1,0:T(8,128)(2,1)S(1)} %slice.1261), channel_id=1, source_target_pairs={{0,3},{1,0},{2,1},{3,2},{4,7},{5,4},{6,5},{7,6},{8,11},{9,8},{10,9... | collective-permute-start | bytes 1179656 | tf_op jit(solution)/shard_map/ppermute | solution.py:474
  112.7 33.0 %collective-permute-start.19 = (bf16[64,2688]{1,0:T(8,128)(2,1)S(1)}, bf16[64,2688]{1,0:T(8,128)(2,1)S(1)}, u32[]{:S(2)}, u32[]{:S(2)}) collective-permute-start(bf16[64,2688]{1,0:T(8,128)(2,1)S(1)} %get-tuple-element.259), channel_id=1, source_target_pairs={{0,3},{1,0},{2,1},{3,2},{4,7},{5,4},{6,5},{7,6},{8,11},{9,8},{10,9... | collective-permute-start | bytes 1032200 | tf_op jit(solution)/shard_map/ppermute | solution.py:474
  113.2 28.6 %collective-permute-start.20 = (bf16[64,2688]{1,0:T(8,128)(2,1)S(1)}, bf16[64,2688]{1,0:T(8,128)(2,1)S(1)}, u32[]{:S(2)}, u32[]{:S(2)}) collective-permute-start(bf16[64,2688]{1,0:T(8,128)(2,1)S(1)} %get-tuple-element.259), channel_id=1, source_target_pairs={{0,1},{1,2},{2,3},{3,0},{4,5},{5,6},{6,7},{7,4},{8,9},{9,10},{10,1... | collective-permute-start | bytes 1032200 | tf_op jit(solution)/shard_map/ppermute | solution.py:474
  116.7 24.9 %collective-permute-start.28 = (bf16[64,2560]{1,0:T(8,128)(2,1)S(1)}, bf16[64,2560]{1,0:T(8,128)(2,1)S(1)}, u32[]{:S(2)}, u32[]{:S(2)}) collective-permute-start(bf16[64,2560]{1,0:T(8,128)(2,1)S(1)} %get-tuple-element.254), channel_id=1, source_target_pairs={{0,12},{1,13},{2,14},{3,15},{4,0},{5,1},{6,2},{7,3},{8,4},{9,5},{1... | collective-permute-start | bytes 983048 | tf_op jit(solution)/shard_map/ppermute | solution.py:474
  119.5 18.9 %collective-permute-start.29 = (bf16[64,2560]{1,0:T(8,128)(2,1)S(1)}, bf16[64,2560]{1,0:T(8,128)(2,1)S(1)}, u32[]{:S(2)}, u32[]{:S(2)}) collective-permute-start(bf16[64,2560]{1,0:T(8,128)(2,1)S(1)} %get-tuple-element.254), channel_id=1, source_target_pairs={{0,4},{1,5},{2,6},{3,7},{4,8},{5,9},{6,10},{7,11},{8,12},{9,13},{1... | collective-permute-start | bytes 983048 | tf_op jit(solution)/shard_map/ppermute | solution.py:474
  131.3 21.6 %collective-permute-start.7 = (bf16[128,1664]{1,0:T(8,128)(2,1)S(1)}, bf16[128,1664]{1,0:T(8,128)(2,1)S(1)}, u32[]{:S(2)}, u32[]{:S(2)}) collective-permute-start(bf16[128,1664]{1,0:T(8,128)(2,1)S(1)} %slice.1246), channel_id=1, source_target_pairs={{0,4},{1,5},{2,6},{3,7},{4,8},{5,9},{6,10},{7,11},{8,12},{9,13},{1... | collective-permute-start | bytes 1277960 | tf_op jit(solution)/shard_map/ppermute | solution.py:474
  138.4 16.8 %collective-permute-start.8 = (bf16[128,1664]{1,0:T(8,128)(2,1)S(1)}, bf16[128,1664]{1,0:T(8,128)(2,1)S(1)}, u32[]{:S(2)}, u32[]{:S(2)}) collective-permute-start(bf16[128,1664]{1,0:T(8,128)(2,1)S(1)} %slice.1247), channel_id=1, source_target_pairs={{0,12},{1,13},{2,14},{3,15},{4,0},{5,1},{6,2},{7,3},{8,4},{9,5},{1... | collective-permute-start | bytes 1277960 | tf_op jit(solution)/shard_map/ppermute | solution.py:474
  141.6 19.4 %collective-permute-start.30 = (bf16[32,2560]{1,0:T(8,128)(2,1)S(1)}, bf16[32,2560]{1,0:T(8,128)(2,1)S(1)}, u32[]{:S(2)}, u32[]{:S(2)}) collective-permute-start(bf16[32,2560]{1,0:T(8,128)(2,1)S(1)} %slice.1295), channel_id=1, source_target_pairs={{0,4},{1,5},{2,6},{3,7},{4,8},{5,9},{6,10},{7,11},{8,12},{9,13},{1... | collective-permute-start | bytes 491528 | tf_op jit(solution)/shard_map/ppermute | solution.py:474
  141.8 19.9 %collective-permute-start.31 = (bf16[32,2560]{1,0:T(8,128)(2,1)S(1)}, bf16[32,2560]{1,0:T(8,128)(2,1)S(1)}, u32[]{:S(2)}, u32[]{:S(2)}) collective-permute-start(bf16[32,2560]{1,0:T(8,128)(2,1)S(1)} %slice.1296), channel_id=1, source_target_pairs={{0,12},{1,13},{2,14},{3,15},{4,0},{5,1},{6,2},{7,3},{8,4},{9,5},{1... | collective-permute-start | bytes 491528 | tf_op jit(solution)/shard_map/ppermute | solution.py:474
  145.8 19.5 %collective-permute-start.21 = (bf16[32,2688]{1,0:T(8,128)(2,1)}, bf16[32,2688]{1,0:T(8,128)(2,1)}, u32[]{:S(2)}, u32[]{:S(2)}) collective-permute-start(bf16[32,2688]{1,0:T(8,128)(2,1)} %slice.1288), channel_id=1, source_target_pairs={{0,1},{1,2},{2,3},{3,0},{4,5},{5,6},{6,7},{7,4},{8,9},{9,10},{10,1... | collective-permute-start | bytes 516104 | tf_op jit(solution)/shard_map/ppermute | solution.py:474
  152.9 14.0 %collective-permute-start.22 = (bf16[32,2688]{1,0:T(8,128)(2,1)}, bf16[32,2688]{1,0:T(8,128)(2,1)}, u32[]{:S(2)}, u32[]{:S(2)}) collective-permute-start(bf16[32,2688]{1,0:T(8,128)(2,1)} %slice.1289), channel_id=1, source_target_pairs={{0,3},{1,0},{2,1},{3,2},{4,7},{5,4},{6,5},{7,6},{8,11},{9,8},{10,9... | collective-permute-start | bytes 516104 | tf_op jit(solution)/shard_map/ppermute | solution.py:474
  163.2 61.1 %collective-permute-start.32 = (bf16[256,2560]{1,0:T(8,128)(2,1)}, bf16[256,2560]{1,0:T(8,128)(2,1)S(1)}, u32[]{:S(2)}, u32[]{:S(2)}) collective-permute-start(bf16[256,2560]{1,0:T(8,128)(2,1)} %constant_dynamic-update-slice_fusion.44), channel_id=1, source_target_pairs={{0,3},{1,0},{2,1},{3,2},{4,7},{5,4},{6,5},{7,6},{8,11},{9,8},{10,9... | collective-permute-start | bytes 3932168 | tf_op jit(solution)/shard_map/ppermute | solution.py:474
  164.1 60.1 %collective-permute-start.33 = (bf16[256,2560]{1,0:T(8,128)(2,1)}, bf16[256,2560]{1,0:T(8,128)(2,1)S(1)}, u32[]{:S(2)}, u32[]{:S(2)}) collective-permute-start(bf16[256,2560]{1,0:T(8,128)(2,1)} %constant_dynamic-update-slice_fusion.44), channel_id=1, source_target_pairs={{0,1},{1,2},{2,3},{3,0},{4,5},{5,6},{6,7},{7,4},{8,9},{9,10},{10,1... | collective-permute-start | bytes 3932168 | tf_op jit(solution)/shard_map/ppermute | solution.py:474
  169.5 65.7 %collective-permute-start.23 = (bf16[256,2688]{1,0:T(8,128)(2,1)}, bf16[256,2688]{1,0:T(8,128)(2,1)S(1)}, u32[]{:S(2)}, u32[]{:S(2)}) collective-permute-start(bf16[256,2688]{1,0:T(8,128)(2,1)} %get-tuple-element.330), channel_id=1, source_target_pairs={{0,12},{1,13},{2,14},{3,15},{4,0},{5,1},{6,2},{7,3},{8,4},{9,5},{1... | collective-permute-start | bytes 4128776 | tf_op jit(solution)/shard_map/ppermute | solution.py:474
  171.9 63.1 %collective-permute-start.24 = (bf16[256,2688]{1,0:T(8,128)(2,1)}, bf16[256,2688]{1,0:T(8,128)(2,1)S(1)}, u32[]{:S(2)}, u32[]{:S(2)}) collective-permute-start(bf16[256,2688]{1,0:T(8,128)(2,1)} %get-tuple-element.330), channel_id=1, source_target_pairs={{0,4},{1,5},{2,6},{3,7},{4,8},{5,9},{6,10},{7,11},{8,12},{9,13},{1... | collective-permute-start | bytes 4128776 | tf_op jit(solution)/shard_map/ppermute | solution.py:474
  224.2 24.0 %collective-permute-start.34 = (bf16[128,2560]{1,0:T(8,128)(2,1)S(1)}, bf16[128,2560]{1,0:T(8,128)(2,1)S(1)}, u32[]{:S(2)}, u32[]{:S(2)}) collective-permute-start(bf16[128,2560]{1,0:T(8,128)(2,1)S(1)} %slice.1298), channel_id=1, source_target_pairs={{0,1},{1,2},{2,3},{3,0},{4,5},{5,6},{6,7},{7,4},{8,9},{9,10},{10,1... | collective-permute-start | bytes 1966088 | tf_op jit(solution)/shard_map/ppermute | solution.py:474
  224.3 24.2 %collective-permute-start.35 = (bf16[128,2560]{1,0:T(8,128)(2,1)S(1)}, bf16[128,2560]{1,0:T(8,128)(2,1)S(1)}, u32[]{:S(2)}, u32[]{:S(2)}) collective-permute-start(bf16[128,2560]{1,0:T(8,128)(2,1)S(1)} %slice.1305), channel_id=1, source_target_pairs={{0,3},{1,0},{2,1},{3,2},{4,7},{5,4},{6,5},{7,6},{8,11},{9,8},{10,9... | collective-permute-start | bytes 1966088 | tf_op jit(solution)/shard_map/ppermute | solution.py:474
  235.1 15.5 %collective-permute-start.25 = (bf16[128,2688]{1,0:T(8,128)(2,1)S(1)}, bf16[128,2688]{1,0:T(8,128)(2,1)S(1)}, u32[]{:S(2)}, u32[]{:S(2)}) collective-permute-start(bf16[128,2688]{1,0:T(8,128)(2,1)S(1)} %slice.1290), channel_id=1, source_target_pairs={{0,4},{1,5},{2,6},{3,7},{4,8},{5,9},{6,10},{7,11},{8,12},{9,13},{1... | collective-permute-start | bytes 2064392 | tf_op jit(solution)/shard_map/ppermute | solution.py:474
  235.2 15.7 %collective-permute-start.26 = (bf16[128,2688]{1,0:T(8,128)(2,1)S(1)}, bf16[128,2688]{1,0:T(8,128)(2,1)S(1)}, u32[]{:S(2)}, u32[]{:S(2)}) collective-permute-start(bf16[128,2688]{1,0:T(8,128)(2,1)S(1)} %slice.1291), channel_id=1, source_target_pairs={{0,12},{1,13},{2,14},{3,15},{4,0},{5,1},{6,2},{7,3},{8,4},{9,5},{1... | collective-permute-start | bytes 2064392 | tf_op jit(solution)/shard_map/ppermute | solution.py:474
  351.8 15.4 %collective-permute-start.39 = (f32[256,1024]{1,0:T(8,128)}, f32[256,1024]{1,0:T(8,128)}, u32[]{:S(2)}, u32[]{:S(2)}) collective-permute-start(f32[256,1024]{1,0:T(8,128)} %fusion.83), channel_id=1, source_target_pairs={{0,64},{64,0},{1,65},{65,1},{2,66},{66,2},{3,67},{67,3},{4,68},{68... | collective-permute-start | bytes 3145736 | tf_op jit(solution)/shard_map/ppermute | solution.py:444
  384.0 377.6 %reduce-scatter.5.cloned.1.call-start = ((), (), s32[]{:S(2)}) async-start(), calls=%async_computation.6 | async-start | bytes 11419648 | tf_op jit(solution)/shard_map/reduce_scatter | solution.py:783
  394.7 124.8 %collective-permute-start.42 = (f32[256,1024]{1,0:T(8,128)}, f32[256,1024]{1,0:T(8,128)}, u32[]{:S(2)}, u32[]{:S(2)}) collective-permute-start(f32[256,1024]{1,0:T(8,128)} %convolution_add_fusion), channel_id=1, source_target_pairs={{0,64},{64,0},{1,65},{65,1},{2,66},{66,2},{3,67},{67,3},{4,68},{68... | collective-permute-start | bytes 3145736 | tf_op jit(solution)/shard_map/ppermute | solution.py:444
  414.3 16.5 %collective-permute-start.40 = (f32[256,1024]{0,1:T(8,128)}, f32[256,1024]{0,1:T(8,128)}, u32[]{:S(2)}, u32[]{:S(2)}) collective-permute-start(f32[256,1024]{0,1:T(8,128)} %fusion.86), channel_id=1, source_target_pairs={{0,64},{64,0},{1,65},{65,1},{2,66},{66,2},{3,67},{67,3},{4,68},{68... | collective-permute-start | bytes 3145736 | tf_op jit(solution)/shard_map/ppermute | solution.py:444
  469.0 38.6 %collective-permute-start.41 = (f32[256,1024]{0,1:T(8,128)}, f32[256,1024]{0,1:T(8,128)}, u32[]{:S(2)}, u32[]{:S(2)}) collective-permute-start(f32[256,1024]{0,1:T(8,128)} %convolution_add_fusion.2), channel_id=1, source_target_pairs={{0,64},{64,0},{1,65},{65,1},{2,66},{66,2},{3,67},{67,3},{4,68},{68... | collective-permute-start | bytes 3145736 | tf_op jit(solution)/shard_map/ppermute | solution.py:444
  470.3 31.6 %collective-permute-start.51 = (bf16[256,1536]{1,0:T(8,128)(2,1)}, bf16[256,1536]{1,0:T(8,128)(2,1)}, u32[]{:S(2)}, u32[]{:S(2)}) collective-permute-start(bf16[256,1536]{1,0:T(8,128)(2,1)} %convolution_convert_fusion.6), channel_id=1, source_target_pairs={{0,4},{1,5},{2,6},{3,7},{4,8},{5,9},{6,10},{7,11},{8,12},{9,13},{1... | collective-permute-start | bytes 2359304 | tf_op jit(solution)/shard_map/ppermute | solution.py:474
  471.9 32.7 %collective-permute-start.53 = (bf16[256,1536]{1,0:T(8,128)(2,1)}, bf16[256,1536]{1,0:T(8,128)(2,1)}, u32[]{:S(2)}, u32[]{:S(2)}) collective-permute-start(bf16[256,1536]{1,0:T(8,128)(2,1)} %convolution_convert_fusion.5), channel_id=1, source_target_pairs={{0,12},{1,13},{2,14},{3,15},{4,0},{5,1},{6,2},{7,3},{8,4},{9,5},{1... | collective-permute-start | bytes 2359304 | tf_op jit(solution)/shard_map/ppermute | solution.py:474
  481.0 138.3 %collective-permute-start.76 = (bf16[256,2560]{1,0:T(8,128)(2,1)}, bf16[256,2560]{1,0:T(8,128)(2,1)}, u32[]{:S(2)}, u32[]{:S(2)}) collective-permute-start(bf16[256,2560]{1,0:T(8,128)(2,1)} %pad_maximum_fusion.7), channel_id=1, source_target_pairs={{0,4},{1,5},{2,6},{3,7},{4,8},{5,9},{6,10},{7,11},{8,12},{9,13},{1... | collective-permute-start | bytes 3932168 | tf_op jit(solution)/shard_map/ppermute | solution.py:474
  501.9 118.8 %collective-permute-start.78 = (bf16[256,2560]{1,0:T(8,128)(2,1)}, bf16[256,2560]{1,0:T(8,128)(2,1)}, u32[]{:S(2)}, u32[]{:S(2)}) collective-permute-start(bf16[256,2560]{1,0:T(8,128)(2,1)} %pad_maximum_fusion.8), channel_id=1, source_target_pairs={{0,12},{1,13},{2,14},{3,15},{4,0},{5,1},{6,2},{7,3},{8,4},{9,5},{1... | collective-permute-start | bytes 3932168 | tf_op jit(solution)/shard_map/ppermute | solution.py:474
  504.6 141.0 %collective-permute-start.68 = (bf16[256,2688]{1,0:T(8,128)(2,1)}, bf16[256,2688]{1,0:T(8,128)(2,1)}, u32[]{:S(2)}, u32[]{:S(2)}) collective-permute-start(bf16[256,2688]{1,0:T(8,128)(2,1)} %pad_maximum_fusion.3), channel_id=1, source_target_pairs={{0,1},{1,2},{2,3},{3,0},{4,5},{5,6},{6,7},{7,4},{8,9},{9,10},{10,1... | collective-permute-start | bytes 4128776 | tf_op jit(solution)/shard_map/ppermute | solution.py:474
  507.6 63.9 %collective-permute-start.52 = (bf16[128,1536]{1,0:T(8,128)(2,1)}, bf16[128,1536]{1,0:T(8,128)(2,1)}, u32[]{:S(2)}, u32[]{:S(2)}) collective-permute-start(bf16[128,1536]{1,0:T(8,128)(2,1)} %get-tuple-element.240), channel_id=1, source_target_pairs={{0,4},{1,5},{2,6},{3,7},{4,8},{5,9},{6,10},{7,11},{8,12},{9,13},{1... | collective-permute-start | bytes 1179656 | tf_op jit(solution)/shard_map/ppermute | solution.py:474
  519.6 54.2 %collective-permute-start.54 = (bf16[128,1536]{1,0:T(8,128)(2,1)S(1)}, bf16[128,1536]{1,0:T(8,128)(2,1)S(1)}, u32[]{:S(2)}, u32[]{:S(2)}) collective-permute-start(bf16[128,1536]{1,0:T(8,128)(2,1)S(1)} %copy-done.69), channel_id=1, source_target_pairs={{0,12},{1,13},{2,14},{3,15},{4,0},{5,1},{6,2},{7,3},{8,4},{9,5},{1... | collective-permute-start | bytes 1179656 | tf_op jit(solution)/shard_map/ppermute | solution.py:474
  571.4 77.5 %collective-permute-start.70 = (bf16[256,2688]{1,0:T(8,128)(2,1)S(1)}, bf16[256,2688]{1,0:T(8,128)(2,1)S(1)}, u32[]{:S(2)}, u32[]{:S(2)}) collective-permute-start(bf16[256,2688]{1,0:T(8,128)(2,1)S(1)} %copy-done.47), channel_id=1, source_target_pairs={{0,3},{1,0},{2,1},{3,2},{4,7},{5,4},{6,5},{7,6},{8,11},{9,8},{10,9... | collective-permute-start | bytes 4128776 | tf_op jit(solution)/shard_map/ppermute | solution.py:474
  575.4 42.8 %collective-permute-start.57 = (bf16[64,1536]{1,0:T(8,128)(2,1)S(1)}, bf16[64,1536]{1,0:T(8,128)(2,1)S(1)}, u32[]{:S(2)}, u32[]{:S(2)}) collective-permute-start(bf16[64,1536]{1,0:T(8,128)(2,1)S(1)} %concatenate.543), channel_id=1, source_target_pairs={{0,3},{1,0},{2,1},{3,2},{4,7},{5,4},{6,5},{7,6},{8,11},{9,8},{10,9... | collective-permute-start | bytes 589832 | tf_op jit(solution)/shard_map/ppermute | solution.py:474
  618.2 36.8 %collective-permute-start.43 = (bf16[256,1664]{1,0:T(8,128)(2,1)S(1)}, bf16[256,1664]{1,0:T(8,128)(2,1)S(1)}, u32[]{:S(2)}, u32[]{:S(2)}) collective-permute-start(bf16[256,1664]{1,0:T(8,128)(2,1)S(1)} %pad_maximum_fusion.11), channel_id=1, source_target_pairs={{0,1},{1,2},{2,3},{3,0},{4,5},{5,6},{6,7},{7,4},{8,9},{9,10},{10,1... | collective-permute-start | bytes 2555912 | tf_op jit(solution)/shard_map/ppermute | solution.py:474
  619.3 24.5 %collective-permute-start.55 = (bf16[64,1536]{1,0:T(8,128)(2,1)S(1)}, bf16[64,1536]{1,0:T(8,128)(2,1)S(1)}, u32[]{:S(2)}, u32[]{:S(2)}) collective-permute-start(bf16[64,1536]{1,0:T(8,128)(2,1)S(1)} %pad_maximum_fusion.23), channel_id=1, source_target_pairs={{0,1},{1,2},{2,3},{3,0},{4,5},{5,6},{6,7},{7,4},{8,9},{9,10},{10,1... | collective-permute-start | bytes 589832 | tf_op jit(solution)/shard_map/ppermute | solution.py:474
  620.7 24.9 %collective-permute-start.58 = (bf16[32,1536]{1,0:T(8,128)(2,1)S(1)}, bf16[32,1536]{1,0:T(8,128)(2,1)S(1)}, u32[]{:S(2)}, u32[]{:S(2)}) collective-permute-start(bf16[32,1536]{1,0:T(8,128)(2,1)S(1)} %add_convert_fusion.47), channel_id=1, source_target_pairs={{0,3},{1,0},{2,1},{3,2},{4,7},{5,4},{6,5},{7,6},{8,11},{9,8},{10,9... | collective-permute-start | bytes 294920 | tf_op jit(solution)/shard_map/ppermute | solution.py:474
  643.8 42.2 %collective-permute-start.45 = (bf16[256,1664]{1,0:T(8,128)(2,1)S(1)}, bf16[256,1664]{1,0:T(8,128)(2,1)S(1)}, u32[]{:S(2)}, u32[]{:S(2)}) collective-permute-start(bf16[256,1664]{1,0:T(8,128)(2,1)S(1)} %pad_maximum_fusion.12), channel_id=1, source_target_pairs={{0,3},{1,0},{2,1},{3,2},{4,7},{5,4},{6,5},{7,6},{8,11},{9,8},{10,9... | collective-permute-start | bytes 2555912 | tf_op jit(solution)/shard_map/ppermute | solution.py:474
  645.6 15.4 %collective-permute-start.77 = (bf16[128,2560]{1,0:T(8,128)(2,1)S(1)}, bf16[128,2560]{1,0:T(8,128)(2,1)S(1)}, u32[]{:S(2)}, u32[]{:S(2)}) collective-permute-start(bf16[128,2560]{1,0:T(8,128)(2,1)S(1)} %get-tuple-element.226), channel_id=1, source_target_pairs={{0,4},{1,5},{2,6},{3,7},{4,8},{5,9},{6,10},{7,11},{8,12},{9,13},{1... | collective-permute-start | bytes 1966088 | tf_op jit(solution)/shard_map/ppermute | solution.py:474
  645.7 15.9 %collective-permute-start.79 = (bf16[128,2560]{1,0:T(8,128)(2,1)S(1)}, bf16[128,2560]{1,0:T(8,128)(2,1)S(1)}, u32[]{:S(2)}, u32[]{:S(2)}) collective-permute-start(bf16[128,2560]{1,0:T(8,128)(2,1)S(1)} %get-tuple-element.227), channel_id=1, source_target_pairs={{0,12},{1,13},{2,14},{3,15},{4,0},{5,1},{6,2},{7,3},{8,4},{9,5},{1... | collective-permute-start | bytes 1966088 | tf_op jit(solution)/shard_map/ppermute | solution.py:474
  654.8 19.8 %collective-permute-start.69 = (bf16[128,2688]{1,0:T(8,128)(2,1)S(1)}, bf16[128,2688]{1,0:T(8,128)(2,1)S(1)}, u32[]{:S(2)}, u32[]{:S(2)}) collective-permute-start(bf16[128,2688]{1,0:T(8,128)(2,1)S(1)} %get-tuple-element.222), channel_id=1, source_target_pairs={{0,1},{1,2},{2,3},{3,0},{4,5},{5,6},{6,7},{7,4},{8,9},{9,10},{10,1... | collective-permute-start | bytes 2064392 | tf_op jit(solution)/shard_map/ppermute | solution.py:474
  655.1 25.4 %collective-permute-start.71 = (bf16[128,2688]{1,0:T(8,128)(2,1)S(1)}, bf16[128,2688]{1,0:T(8,128)(2,1)S(1)}, u32[]{:S(2)}, u32[]{:S(2)}) collective-permute-start(bf16[128,2688]{1,0:T(8,128)(2,1)S(1)} %get-tuple-element.223), channel_id=1, source_target_pairs={{0,3},{1,0},{2,1},{3,2},{4,7},{5,4},{6,5},{7,6},{8,11},{9,8},{10,9... | collective-permute-start | bytes 2064392 | tf_op jit(solution)/shard_map/ppermute | solution.py:474
  661.0 27.7 %collective-permute-start.44 = (bf16[128,1664]{1,0:T(8,128)(2,1)S(1)}, bf16[128,1664]{1,0:T(8,128)(2,1)S(1)}, u32[]{:S(2)}, u32[]{:S(2)}) collective-permute-start(bf16[128,1664]{1,0:T(8,128)(2,1)S(1)} %add_convert_fusion.12), channel_id=1, source_target_pairs={{0,1},{1,2},{2,3},{3,0},{4,5},{5,6},{6,7},{7,4},{8,9},{9,10},{10,1... | collective-permute-start | bytes 1277960 | tf_op jit(solution)/shard_map/ppermute | solution.py:474
  663.4 31.5 %collective-permute-start.80 = (bf16[64,2560]{1,0:T(8,128)(2,1)S(1)}, bf16[64,2560]{1,0:T(8,128)(2,1)S(1)}, u32[]{:S(2)}, u32[]{:S(2)}) collective-permute-start(bf16[64,2560]{1,0:T(8,128)(2,1)S(1)} %pad_maximum_fusion.21), channel_id=1, source_target_pairs={{0,1},{1,2},{2,3},{3,0},{4,5},{5,6},{6,7},{7,4},{8,9},{9,10},{10,1... | collective-permute-start | bytes 983048 | tf_op jit(solution)/shard_map/ppermute | solution.py:474
  682.2 12.9 %collective-permute-start.72 = (bf16[64,2688]{1,0:T(8,128)(2,1)S(1)}, bf16[64,2688]{1,0:T(8,128)(2,1)S(1)}, u32[]{:S(2)}, u32[]{:S(2)}) collective-permute-start(bf16[64,2688]{1,0:T(8,128)(2,1)S(1)} %pad_maximum_fusion.20), channel_id=1, source_target_pairs={{0,4},{1,5},{2,6},{3,7},{4,8},{5,9},{6,10},{7,11},{8,12},{9,13},{1... | collective-permute-start | bytes 1032200 | tf_op jit(solution)/shard_map/ppermute | solution.py:474
  689.0 12.7 %collective-permute-start.46 = (bf16[128,1664]{1,0:T(8,128)(2,1)S(1)}, bf16[128,1664]{1,0:T(8,128)(2,1)S(1)}, u32[]{:S(2)}, u32[]{:S(2)}) collective-permute-start(bf16[128,1664]{1,0:T(8,128)(2,1)S(1)} %get-tuple-element.237), channel_id=1, source_target_pairs={{0,3},{1,0},{2,1},{3,2},{4,7},{5,4},{6,5},{7,6},{8,11},{9,8},{10,9... | collective-permute-start | bytes 1277960 | tf_op jit(solution)/shard_map/ppermute | solution.py:474
  716.3 12.0 %collective-permute-start.86 = (bf16[32,5248]{1,0:T(8,128)(2,1)S(1)}, bf16[32,5248]{1,0:T(8,128)(2,1)S(1)}, u32[]{:S(2)}, u32[]{:S(2)}) collective-permute-start(bf16[32,5248]{1,0:T(8,128)(2,1)S(1)} %get-tuple-element.249), channel_id=1, source_target_pairs={{0,48},{48,0},{16,32},{32,16},{1,49},{49,1},{17,33},{33,17},{2,50}... | collective-permute-start | bytes 1007624 | tf_op jit(solution)/shard_map/ppermute | solution.py:583
  728.6 25.0 %collective-permute-start.85 = (bf16[32,5248]{1,0:T(8,128)(2,1)S(1)}, bf16[32,5248]{1,0:T(8,128)(2,1)S(1)}, u32[]{:S(2)}, u32[]{:S(2)}) collective-permute-start(bf16[32,5248]{1,0:T(8,128)(2,1)S(1)} %get-tuple-element.246), channel_id=1, source_target_pairs={{0,48},{48,0},{16,32},{32,16},{1,49},{49,1},{17,33},{33,17},{2,50}... | collective-permute-start | bytes 1007624 | tf_op jit(solution)/shard_map/ppermute | solution.py:583
  732.5 13.8 %collective-permute-start.60 = (bf16[32,3200]{1,0:T(8,128)(2,1)S(1)}, bf16[32,3200]{1,0:T(8,128)(2,1)S(1)}, u32[]{:S(2)}, u32[]{:S(2)}) collective-permute-start(bf16[32,3200]{1,0:T(8,128)(2,1)S(1)} %get-tuple-element.308), channel_id=1, source_target_pairs={{0,48},{48,0},{16,32},{32,16},{1,49},{49,1},{17,33},{33,17},{2,50}... | collective-permute-start | bytes 614408 | tf_op jit(solution)/shard_map/ppermute | solution.py:583
  791.5 21.8 %all-to-all-start.1 = ((bf16[16,64,384]{2,1,0:T(8,128)(2,1)}), bf16[16,64,384]{2,1,0:T(8,128)(2,1)S(1)}, u32[]{:S(2)}, u32[]{:S(2)}) async-start(bf16[16,64,384]{2,1,0:T(8,128)(2,1)} %pad.83), calls=%async_computation.2 | async-start | bytes 1572864 | tf_op jit(solution)/shard_map/all_to_all | solution.py:921
  (168 other events, 1650.5 us)
Sparse Core Ops, SparseCore 0:
  20.9 90.0 all-gather.2
  113.7 128.9 all-gather.4
  384.1 82.5 reduce-scatter.6
  470.4 131.0 reduce-scatter.4
